TPU v7x, 32 devices: a whole 2x2x4 slice. The times are simulated.
32 devices in a mesh: seq: 16 (over z, y, core), rows: 2 (over x).
Axes of the slice: x: 2, y: 2, z: 4, core: 2. Of those that a mesh axis runs over, the one named last changes fastest.
Arguments:
- inputs: bfloat16 [4, 2048, 1024], P('rows', 'seq'), may hold values from -6 to 6
- memory: bfloat16 [4, 512, 1024], P('rows', 'seq'), may hold values from -6 to 6
- out_grad: bfloat16 [4, 2048, 1024], P('rows', 'seq'), may hold values from -6 to 6
- token_docs: int32 [4, 2048], P('rows', 'seq'), may hold values from 0 to 3, as said below
- memory_docs: int32 [4, 512], P('rows', 'seq'), may hold values from 0 to 3, as said below
- self_project: bfloat16 [1024, 3072], P(('seq', 'rows')), may hold values from -0.1875 to 0.1875
- self_output: bfloat16 [1024, 1024], P(('seq', 'rows')), may hold values from -6 to 6
- cross_query: bfloat16 [1024, 1024], P(('seq', 'rows')), may hold values from -0.1875 to 0.1875
- cross_memory: bfloat16 [1024, 2048], P(('seq', 'rows')), may hold values from -0.1875 to 0.1875
- cross_output: bfloat16 [1024, 1024], P(('seq', 'rows')), may hold values from -6 to 6
- inner_weight: bfloat16 [1024, 4096], P(('seq', 'rows')), may hold values from -0.1875 to 0.1875
- outer_weight: bfloat16 [4096, 1024], P(('seq', 'rows')), may hold values from -0.09375 to 0.09375
- adapter_down: bfloat16 [1024, 512], P(('seq', 'rows')), may hold values from -0.1875 to 0.1875
- adapter_up: bfloat16 [512, 1024], P(('seq', 'rows')), may hold values from -0.25 to 0.25
- norm_gains: bfloat16 [3, 1024], P(None, ('seq', 'rows')), may hold values from 0.5 to 1.5
- prefixes: bfloat16 [4, 30, 1024], P(None, None, ('seq', 'rows')), may hold values from -6 to 6
Outputs:
- layer_out: bfloat16 [4, 2048, 1024], P('rows', 'seq')
- input_grad: float32 [4, 2048, 1024], P('rows', 'seq')
- memory_grad: float32 [4, 512, 1024], P('rows', 'seq')
- prefix_grad: float32 [4, 30, 1024], P(None, None, ('seq', 'rows'))
- down_grad: float32 [1024, 512], P(('seq', 'rows'))
- up_grad: float32 [512, 1024], P(('seq', 'rows'))
Inputs may be any that keep to these rules, and one draw needn't show every extreme that they name: `token_docs`: document numbers never fall along a row; decoder and memory tokens with equal numbers belong to one document; in each row one document runs from the first 128 tokens to the last 128. `memory_docs`: document numbers never fall along a row; in each row the document that spans the decoder row runs from the first 32 memory tokens to the last 32.
All inputs are finite; a program needn't handle non-finite values.
Results may differ from a plain program's by a relative error of at most 0.028.
Values may be sent and summed in bfloat16 or wider, within the bound.
A program may use at most 320 MiB of HBM per device.

v0:
```python
import math

import jax
import jax.numpy as jnp
from jax import lax
from jax.sharding import PartitionSpec as P

D = 1024
HEADS = 16
HEAD_DIM = 64


score_scale = 0.125
masked_score = -1000000000.0


def heads_of(matrix):
    return matrix.reshape(matrix.shape[0], HEADS, HEAD_DIM)


def dot_right(left, right):
    return lax.dot_general(
        left, right, (((1,), (1,)), ((), ())), preferred_element_type=jnp.float32
    )


def dot_left(left, right):
    return lax.dot_general(
        left, right, (((0,), (0,)), ((), ())), preferred_element_type=jnp.float32
    )


def norm_rows(resid, gain):
    middle = jnp.mean(resid, axis=-1, keepdims=True)
    centred = resid - middle
    spread = jnp.mean(centred * centred, axis=-1, keepdims=True)
    return centred * lax.rsqrt(spread + 1e-05) * gain


def norm_back(resid, gain, upstream):
    unused, pullback = jax.vjp(lambda values: norm_rows(values, gain), resid)
    return pullback(upstream)[0]


def gelu_back(pre_act, upstream):
    unused, pullback = jax.vjp(lambda values: jax.nn.gelu(values, approximate=False), pre_act)
    return pullback(upstream)[0]


def allowed_keys(query_docs, key_docs, query_pos, key_pos, causal):
    allowed = query_docs[:, None] == key_docs[None, :]
    if causal:
        allowed = allowed & (key_pos[None, :] <= query_pos[:, None])
    return allowed


def prefix_terms(queries, prefix_keys, prefix_values):
    scores = (
        jnp.einsum(
            "qhd,phd->hqp", queries, heads_of(prefix_keys), preferred_element_type=jnp.float32
        )
        * score_scale
    )
    weights = jnp.exp(scores)
    summed = jnp.einsum(
        "hqp,phd->qhd",
        weights.astype(jnp.bfloat16),
        heads_of(prefix_values),
        preferred_element_type=jnp.float32,
    )
    return (jnp.sum(weights, axis=-1), summed)


def fold_keys(running, arrived, queries, query_docs, key_docs, query_first, causal):
    key_count = arrived.shape[0]
    block_len = math.gcd(key_count, 512)
    query_count = queries.shape[0]
    query_pos = query_first + jnp.arange(query_count, dtype=jnp.int32)
    key_width = arrived.shape[1] // 2

    def fold_one_block(current, element):
        key_block, block_index = element
        key_first = block_index * block_len

        def compute(present):
            block_docs = lax.dynamic_slice_in_dim(key_docs, key_first, block_len, 0)
            allowed = allowed_keys(
                query_docs,
                block_docs,
                query_pos,
                key_first + jnp.arange(block_len, dtype=jnp.int32),
                causal,
            )
            scores = (
                jnp.einsum(
                    "qhd,khd->hqk",
                    queries,
                    heads_of(key_block[:, :key_width]),
                    preferred_element_type=jnp.float32,
                )
                * score_scale
            )
            weights = jnp.exp(jnp.where(allowed[None], scores, masked_score))
            summed = jnp.einsum(
                "hqk,khd->qhd",
                weights.astype(jnp.bfloat16),
                heads_of(key_block[:, key_width:]),
                preferred_element_type=jnp.float32,
            )
            return (present[0] + jnp.sum(weights, axis=-1), present[1] + summed)

        if causal:
            return (
                lax.cond(
                    key_first <= query_first + query_count - 1, compute, lambda held: held, current
                ),
                None,
            )
        return (compute(current), None)

    running, unused = lax.scan(
        fold_one_block,
        running,
        (
            arrived.reshape(key_count // block_len, block_len, arrived.shape[1]),
            jnp.arange(key_count // block_len, dtype=jnp.int32),
        ),
    )
    return running


def attend_back(
    queries,
    gathered,
    prefix_keys,
    prefix_values,
    grad_out,
    attended,
    totals,
    query_docs,
    key_docs,
    query_first,
    causal,
):
    query_count = queries.shape[0]
    key_count = gathered.shape[0]
    key_width = gathered.shape[1] // 2
    block_len = math.gcd(key_count, 512)
    query_pos = query_first + jnp.arange(query_count, dtype=jnp.int32)
    grad_heads = heads_of(grad_out)
    grad_summed = (grad_heads / totals.T[:, :, None]).astype(jnp.bfloat16)
    row_dot = jnp.sum(grad_heads * heads_of(attended), axis=-1).T / totals
    prefix_key_heads = heads_of(prefix_keys)
    prefix_value_heads = heads_of(prefix_values)
    prefix_weights = jnp.exp(
        jnp.einsum("qhd,phd->hqp", queries, prefix_key_heads, preferred_element_type=jnp.float32)
        * score_scale
    )
    prefix_dots = jnp.einsum(
        "qhd,phd->hqp", grad_summed, prefix_value_heads, preferred_element_type=jnp.float32
    )
    prefix_slopes = (prefix_weights * (prefix_dots - row_dot[:, :, None])).astype(jnp.bfloat16)
    query_grad = jnp.einsum(
        "hqp,phd->qhd", prefix_slopes, prefix_key_heads, preferred_element_type=jnp.float32
    )
    key_grad_prefix = (
        jnp.einsum("hqp,qhd->phd", prefix_slopes, queries, preferred_element_type=jnp.float32)
        * score_scale
    ).reshape(-1, D)
    value_grad_prefix = jnp.einsum(
        "hqp,qhd->phd",
        prefix_weights.astype(jnp.bfloat16),
        grad_summed,
        preferred_element_type=jnp.float32,
    ).reshape(-1, D)

    def attend_one_block(current, element):
        key_block, block_index = element
        key_first = block_index * block_len

        def compute(present):
            block_docs = lax.dynamic_slice_in_dim(key_docs, key_first, block_len, 0)
            allowed = allowed_keys(
                query_docs,
                block_docs,
                query_pos,
                key_first + jnp.arange(block_len, dtype=jnp.int32),
                causal,
            )
            key_heads = heads_of(key_block[:, :key_width])
            value_heads = heads_of(key_block[:, key_width:])
            scores = (
                jnp.einsum("qhd,khd->hqk", queries, key_heads, preferred_element_type=jnp.float32)
                * score_scale
            )
            weights = jnp.exp(jnp.where(allowed[None], scores, masked_score))
            dots = jnp.einsum(
                "qhd,khd->hqk", grad_summed, value_heads, preferred_element_type=jnp.float32
            )
            slopes = (weights * (dots - row_dot[:, :, None])).astype(jnp.bfloat16)
            present = present + jnp.einsum(
                "hqk,khd->qhd", slopes, key_heads, preferred_element_type=jnp.float32
            )
            key_grad = (
                jnp.einsum("hqk,qhd->khd", slopes, queries, preferred_element_type=jnp.float32)
                * score_scale
            )
            value_grad = jnp.einsum(
                "hqk,qhd->khd",
                weights.astype(jnp.bfloat16),
                grad_summed,
                preferred_element_type=jnp.float32,
            )
            return (
                present,
                jnp.concatenate(
                    [key_grad.reshape(block_len, D), value_grad.reshape(block_len, D)], axis=1
                ),
            )

        if causal:
            return lax.cond(
                key_first <= query_first + query_count - 1,
                compute,
                lambda held: (held, jnp.zeros((block_len, 2 * D), jnp.float32)),
                current,
            )
        return compute(current)

    query_grad, key_terms = lax.scan(
        attend_one_block,
        query_grad,
        (
            gathered.reshape(key_count // block_len, block_len, gathered.shape[1]),
            jnp.arange(key_count // block_len, dtype=jnp.int32),
        ),
    )
    query_low = (query_grad * score_scale).astype(jnp.bfloat16).reshape(query_count, D)
    key_terms = key_terms.reshape(key_count, 2 * D)
    return (query_low, key_terms, key_grad_prefix, value_grad_prefix, grad_summed, row_dot)


def fetch_all(
    self_project,
    self_output,
    cross_query,
    cross_memory,
    cross_output,
    inner_weight,
    outer_weight,
    adapter_down,
    adapter_up,
    norm_gains,
    prefixes,
):
    return (
        lax.all_gather(self_project, ("seq", "rows"), axis=0, tiled=True),
        lax.all_gather(self_output, ("seq", "rows"), axis=0, tiled=True),
        lax.all_gather(cross_query, ("seq", "rows"), axis=0, tiled=True),
        lax.all_gather(cross_memory, ("seq", "rows"), axis=0, tiled=True),
        lax.all_gather(cross_output, ("seq", "rows"), axis=0, tiled=True),
        lax.all_gather(inner_weight, ("seq", "rows"), axis=0, tiled=True),
        lax.all_gather(outer_weight, ("seq", "rows"), axis=0, tiled=True),
        lax.all_gather(adapter_down, ("seq", "rows"), axis=0, tiled=True),
        lax.all_gather(adapter_up, ("seq", "rows"), axis=0, tiled=True),
        lax.all_gather(norm_gains, ("seq", "rows"), axis=1, tiled=True),
        lax.all_gather(prefixes, ("seq", "rows"), axis=2, tiled=True),
    )


def fetch_again(
    self_project,
    self_output,
    cross_query,
    cross_memory,
    cross_output,
    inner_weight,
    outer_weight,
    adapter_down,
    adapter_up,
    norm_gains,
    prefixes,
):
    return (
        lax.all_gather(self_project, ("seq", "rows"), axis=0, tiled=True),
        lax.all_gather(self_output, ("seq", "rows"), axis=0, tiled=True),
        lax.all_gather(cross_query, ("seq", "rows"), axis=0, tiled=True),
        lax.all_gather(cross_memory, ("seq", "rows"), axis=0, tiled=True),
        lax.all_gather(cross_output, ("seq", "rows"), axis=0, tiled=True),
        lax.all_gather(inner_weight, ("seq", "rows"), axis=0, tiled=True),
        lax.all_gather(outer_weight, ("seq", "rows"), axis=0, tiled=True),
        lax.all_gather(adapter_down, ("seq", "rows"), axis=0, tiled=True),
        lax.all_gather(adapter_up, ("seq", "rows"), axis=0, tiled=True),
        lax.all_gather(norm_gains, ("seq", "rows"), axis=1, tiled=True),
        lax.all_gather(prefixes, ("seq", "rows"), axis=2, tiled=True),
    )


def forward_row(tokens, memory_rows, query_docs, token_docs, memory_docs, query_first, weights):
    (
        self_project,
        self_output,
        cross_query,
        cross_memory,
        cross_output,
        inner_weight,
        outer_weight,
        adapter_down,
        adapter_up,
        norm_gains,
        prefixes,
    ) = weights
    gains = norm_gains.astype(jnp.float32)
    projected = jnp.dot(tokens, self_project, preferred_element_type=jnp.float32).astype(
        jnp.bfloat16
    )
    queries = heads_of(projected[:, :D])
    local_pairs = projected[:, D:]
    start_self = prefix_terms(queries, prefixes[0], prefixes[1])
    totals, summed = fold_keys(
        start_self,
        lax.all_gather(local_pairs, "seq", axis=0, tiled=True),
        queries,
        query_docs,
        token_docs,
        query_first,
        True,
    )
    attended = (summed / totals.T[:, :, None]).reshape(-1, D)
    first_resid = tokens.astype(jnp.float32) + jnp.dot(
        attended.astype(jnp.bfloat16), self_output, preferred_element_type=jnp.float32
    )
    first_norm = norm_rows(first_resid, gains[0])
    first_low = first_norm.astype(jnp.bfloat16)
    cross_queries = heads_of(
        jnp.dot(first_low, cross_query, preferred_element_type=jnp.float32).astype(jnp.bfloat16)
    )
    memory_pairs = jnp.dot(memory_rows, cross_memory, preferred_element_type=jnp.float32).astype(
        jnp.bfloat16
    )
    start_cross = prefix_terms(cross_queries, prefixes[2], prefixes[3])
    cross_totals, cross_summed = fold_keys(
        start_cross,
        lax.all_gather(memory_pairs, "seq", axis=0, tiled=True),
        cross_queries,
        query_docs,
        memory_docs,
        query_first,
        False,
    )
    crossed = (cross_summed / cross_totals.T[:, :, None]).reshape(-1, D)
    second_resid = first_norm + jnp.dot(
        crossed.astype(jnp.bfloat16), cross_output, preferred_element_type=jnp.float32
    )
    second_norm = norm_rows(second_resid, gains[1])
    second_low = second_norm.astype(jnp.bfloat16)
    hidden_pre = jnp.dot(second_low, inner_weight, preferred_element_type=jnp.float32)
    hidden_act = jax.nn.gelu(hidden_pre, approximate=False).astype(jnp.bfloat16)
    adapter_pre = jnp.dot(second_low, adapter_down, preferred_element_type=jnp.float32)
    adapter_act = jax.nn.gelu(adapter_pre, approximate=False).astype(jnp.bfloat16)
    third_resid = (
        second_norm
        + jnp.dot(hidden_act, outer_weight, preferred_element_type=jnp.float32)
        + 4.0 * jnp.dot(adapter_act, adapter_up, preferred_element_type=jnp.float32)
    )
    layer_out = norm_rows(third_resid, gains[2]).astype(jnp.bfloat16)
    saved = (
        queries,
        local_pairs,
        totals,
        attended,
        first_resid,
        cross_queries,
        memory_pairs,
        cross_totals,
        crossed,
        second_resid,
        second_low,
        hidden_pre,
        adapter_pre,
        adapter_act,
        third_resid,
    )
    return (layer_out, saved)


def backward_row(cotangent, saved, weights, query_docs, token_docs, memory_docs, query_first):
    (
        self_project,
        self_output,
        cross_query,
        cross_memory,
        cross_output,
        inner_weight,
        outer_weight,
        adapter_down,
        adapter_up,
        norm_gains,
        prefixes,
    ) = weights
    (
        queries,
        local_pairs,
        totals,
        attended,
        first_resid,
        cross_queries,
        memory_pairs,
        cross_totals,
        crossed,
        second_resid,
        second_low,
        hidden_pre,
        adapter_pre,
        adapter_act,
        third_resid,
    ) = saved
    gains = norm_gains.astype(jnp.float32)
    third_grad = norm_back(third_resid, gains[2], cotangent.astype(jnp.float32))
    feed_low = third_grad.astype(jnp.bfloat16)
    adapter_low = (4.0 * third_grad).astype(jnp.bfloat16)
    hidden_grad = gelu_back(hidden_pre, dot_right(feed_low, outer_weight)).astype(jnp.bfloat16)
    up_grad = dot_left(adapter_act, adapter_low)
    adapter_grad = gelu_back(adapter_pre, dot_right(adapter_low, adapter_up)).astype(jnp.bfloat16)
    down_grad = dot_left(second_low, adapter_grad)
    second_grad = (
        third_grad + dot_right(hidden_grad, inner_weight) + dot_right(adapter_grad, adapter_down)
    )
    second_resid_grad = norm_back(second_resid, gains[1], second_grad)
    self_all, memory_all = (
        lax.all_gather(local_pairs, "seq", axis=0, tiled=True),
        lax.all_gather(memory_pairs, "seq", axis=0, tiled=True),
    )
    cross_out_grad = dot_right(second_resid_grad.astype(jnp.bfloat16), cross_output)
    (
        cross_query_low,
        memory_terms,
        cross_key_prefix,
        cross_value_prefix,
        cross_summed_grad,
        cross_dot,
    ) = attend_back(
        cross_queries,
        memory_all,
        prefixes[2],
        prefixes[3],
        cross_out_grad,
        crossed,
        cross_totals,
        query_docs,
        memory_docs,
        query_first,
        False,
    )
    first_grad = second_resid_grad + dot_right(cross_query_low, cross_query)
    first_resid_grad = norm_back(first_resid, gains[0], first_grad)
    self_out_grad = dot_right(first_resid_grad.astype(jnp.bfloat16), self_output)
    query_low, self_terms, self_key_prefix, self_value_prefix, self_summed_grad, self_dot = (
        attend_back(
            queries,
            self_all,
            prefixes[0],
            prefixes[1],
            self_out_grad,
            attended,
            totals,
            query_docs,
            token_docs,
            query_first,
            True,
        )
    )
    self_sums, memory_sums = (
        lax.psum_scatter(
            self_terms.astype(jnp.bfloat16), "seq", scatter_dimension=0, tiled=True
        ).astype(jnp.float32),
        lax.psum_scatter(
            memory_terms.astype(jnp.bfloat16), "seq", scatter_dimension=0, tiled=True
        ).astype(jnp.float32),
    )
    project_grad = jnp.concatenate([query_low, self_sums.astype(jnp.bfloat16)], axis=1)
    input_grad = first_resid_grad + dot_right(project_grad, self_project)
    memory_grad = dot_right(memory_sums.astype(jnp.bfloat16), cross_memory)
    prefix_grad = jnp.stack(
        [self_key_prefix, self_value_prefix, cross_key_prefix, cross_value_prefix]
    )
    return (input_grad, memory_grad, (down_grad, up_grad, prefix_grad))


def per_device(
    inputs,
    memory,
    out_grad,
    token_docs,
    memory_docs,
    self_project,
    self_output,
    cross_query,
    cross_memory,
    cross_output,
    inner_weight,
    outer_weight,
    adapter_down,
    adapter_up,
    norm_gains,
    prefixes,
):
    docs_full, memory_full = (
        lax.all_gather(token_docs, "seq", axis=1, tiled=True),
        lax.all_gather(memory_docs, "seq", axis=1, tiled=True),
    )
    query_first = lax.axis_index("seq") * inputs.shape[1]
    outputs = []
    input_grads = []
    memory_grads = []
    adjusted_grads = None
    for row_index in range(inputs.shape[0]):
        weights = fetch_all(
            self_project,
            self_output,
            cross_query,
            cross_memory,
            cross_output,
            inner_weight,
            outer_weight,
            adapter_down,
            adapter_up,
            norm_gains,
            prefixes,
        )
        layer_out, saved = forward_row(
            inputs[row_index],
            memory[row_index],
            token_docs[row_index],
            docs_full[row_index],
            memory_full[row_index],
            query_first,
            weights,
        )
        weights_back = fetch_again(
            self_project,
            self_output,
            cross_query,
            cross_memory,
            cross_output,
            inner_weight,
            outer_weight,
            adapter_down,
            adapter_up,
            norm_gains,
            prefixes,
        )
        input_grad, memory_grad, row_grads = backward_row(
            out_grad[row_index],
            saved,
            weights_back,
            token_docs[row_index],
            docs_full[row_index],
            memory_full[row_index],
            query_first,
        )
        shares = (
            lax.psum_scatter(row_grads[0], ("seq", "rows"), scatter_dimension=0, tiled=True),
            lax.psum_scatter(row_grads[1], ("seq", "rows"), scatter_dimension=0, tiled=True),
            lax.psum_scatter(row_grads[2], ("seq", "rows"), scatter_dimension=2, tiled=True),
        )
        if adjusted_grads is None:
            adjusted_grads = shares
        else:
            adjusted_grads = tuple(
                (former + latter for former, latter in zip(adjusted_grads, shares))
            )
        outputs.append(layer_out)
        input_grads.append(input_grad)
        memory_grads.append(memory_grad)
    return (
        jnp.stack(outputs),
        jnp.stack(input_grads),
        jnp.stack(memory_grads),
        adjusted_grads[2],
        adjusted_grads[0],
        adjusted_grads[1],
    )


def solution(mesh):
    placed = (
        P("rows", "seq", None),
        P("rows", "seq", None),
        P("rows", "seq", None),
        P("rows", "seq"),
        P("rows", "seq"),
        P(("seq", "rows"), None),
        P(("seq", "rows"), None),
        P(("seq", "rows"), None),
        P(("seq", "rows"), None),
        P(("seq", "rows"), None),
        P(("seq", "rows"), None),
        P(("seq", "rows"), None),
        P(("seq", "rows"), None),
        P(("seq", "rows"), None),
        P(None, ("seq", "rows")),
        P(None, None, ("seq", "rows")),
    )
    return jax.shard_map(
        per_device,
        mesh=mesh,
        in_specs=placed,
        out_specs=(
            P("rows", "seq", None),
            P("rows", "seq", None),
            P("rows", "seq", None),
            P(None, None, ("seq", "rows")),
            P(("seq", "rows"), None),
            P(("seq", "rows"), None),
        ),
        check_vma=False,
    )
```

profile of v0, /device:TPU:28, one launch (start us, length us, event | category | flops | bytes accessed | tf_op | source)
XLA Modules:
  0.0 1667.9 jit_solution(11535043683178350788)
XLA Ops:
  8.7 63.9 %all-gather.24.cloned.1.call-done = bf16[1024,2048]{1,0:T(8,128)(2,1)} async-done(((bf16[32,2048]{1,0:T(8,128)(2,1)}), bf16[1024,2048]{1,0:T(8,128)(2,1)}) %all-gather.24.cloned.1.call-update) | async-done | bytes 4194320 | tf_op jit(solution)/shard_map/all_gather | solution.py:260
  80.2 63.3 %all-gather.16.cloned.1.call-done = bf16[1024,3072]{1,0:T(8,128)(2,1)} async-done(((bf16[32,3072]{1,0:T(8,128)(2,1)}), bf16[1024,3072]{1,0:T(8,128)(2,1)}) %all-gather.16.cloned.1.call-update) | async-done | bytes 6291472 | tf_op jit(solution)/shard_map/all_gather | solution.py:257
  159.9 16.5 all_gather.36
  176.6 69.2 %all_gather.35 = bf16[4,30,1024]{1,0,2:T(4,128)(2,1)S(1)} all-gather(bf16[4,30,32]{1,0,2:T(4,128)(2,1)S(1)} %copy.190), channel_id=1, replica_groups=mesh['seq'=16,'rows'=2] {'seq','rows'}, dimensions={2}, use_global_device_ids=true | all-gather | bytes 253440 | tf_op jit(solution)/shard_map/all_gather | solution.py:267
  248.9 65.0 %all-gather = bf16[32,32,3]{1,2,0:T(4,128)(2,1)S(1)} all-gather(bf16[1,32,3]{1,2,0:T(4,128)(2,1)S(1)} %bitcast.504), channel_id=1, replica_groups=mesh['seq'=16,'rows'=2] {'seq','rows'}, dimensions={0}, use_global_device_ids=true | all-gather | bytes 6336 | tf_op jit(solution)/shard_map/all_gather | solution.py:266
  315.1 24.5 %all-gather.1 = s32[16,32,2]{1,2,0:T(2,128)S(1)} all-gather(s32[1,32,2]{1,2,0:T(2,128)S(1)} %bitcast.505), channel_id=1, replica_groups=mesh['seq'=16,'rows'=2] {'seq'}, dimensions={0}, use_global_device_ids=true | all-gather | bytes 4352 | tf_op jit(solution)/shard_map/all_gather | solution.py:510
  352.0 11.5 copy.195
  363.5 23.4 %while.86 = (s32[]{:T(128)}, f32[16,128]{1,0:T(8,128)S(1)}, f32[128,16,64]{0,2,1:T(8,128)S(1)}, s32[4]{0:T(128)S(1)}, s32[]{:T(128)}, /*index=5*/s32[1,128]{1,0:...) while((s32[]{:T(128)}, f32[16,128]{1,0:T(8,128)S(1)}, ...), condition=%wide.region_5.6_spmd.clone, body=%wide.region_1.5_spmd.clone.sunk | while | flops 275055232 | bytes 20427596 | solution.py:121
  364.7 4.6 conditional.12
  370.6 4.6 conditional.12
  376.5 4.6 conditional.12
  382.3 4.6 conditional.12
  389.7 32.9 %all-gather.22.cloned.1.call-done = bf16[1024,1024]{1,0:T(8,128)(2,1)} async-done(((bf16[32,1024]{1,0:T(8,128)(2,1)}), bf16[1024,1024]{1,0:T(8,128)(2,1)}) %all-gather.22.cloned.1.call-update) | async-done | bytes 2097168 | tf_op jit(solution)/shard_map/all_gather | solution.py:259
  431.6 49.4 %all-gather.28.cloned.1.call-done = bf16[1024,1024]{1,0:T(8,128)(2,1)} async-done(((bf16[32,1024]{1,0:T(8,128)(2,1)}), bf16[1024,1024]{1,0:T(8,128)(2,1)}) %all-gather.28.cloned.1.call-update) | async-done | bytes 2097168 | tf_op jit(solution)/shard_map/all_gather | solution.py:261
  483.9 71.5 %all-gather.38.cloned.1.call-done = bf16[2048,2048]{1,0:T(8,128)(2,1)} async-done(((bf16[128,2048]{1,0:T(8,128)(2,1)}), bf16[2048,2048]{1,0:T(8,128)(2,1)}) %all-gather.38.cloned.1.call-update) | async-done | bytes 8388624 | tf_op jit(solution)/shard_map/all_gather | solution.py:322
  555.5 11.4 copy.208
  566.9 25.9 %while.87 = (s32[]{:T(128)}, f32[16,128]{1,0:T(8,128)S(1)}, f32[128,16,64]{0,2,1:T(8,128)S(1)}, s32[4]{0:T(128)S(1)}, s32[]{:T(128)}, /*index=5*/s32[1,128]{1,0:...) while((s32[]{:T(128)}, f32[16,128]{1,0:T(8,128)S(1)}, ...), condition=%wide.region_19.20_spmd.clone, body=%wide.region_15.19_spmd.clone.sunk | while | flops 275055232 | bytes 20427596 | solution.py:121
  568.0 5.3 conditional.13
  574.4 5.3 conditional.13
  580.9 5.3 conditional.13
  587.3 5.3 conditional.13
  604.4 30.8 %all-gather.30.cloned.1.call-done = bf16[1024,4096]{1,0:T(8,128)(2,1)} async-done(((bf16[32,4096]{1,0:T(8,128)(2,1)}), bf16[1024,4096]{1,0:T(8,128)(2,1)}) %all-gather.30.cloned.1.call-update) | async-done | bytes 8388624 | tf_op jit(solution)/shard_map/all_gather | solution.py:262
  635.2 6.0 fusion.273
  641.2 49.6 %all-gather.34.cloned.1.call-done = bf16[1024,512]{1,0:T(8,128)(2,1)} async-done(((bf16[32,512]{1,0:T(8,128)(2,1)}), bf16[1024,512]{1,0:T(8,128)(2,1)}) %all-gather.34.cloned.1.call-update) | async-done | bytes 1048592 | tf_op jit(solution)/shard_map/all_gather | solution.py:264
  693.6 75.9 %all-gather.32.cloned.1.call-done = bf16[4096,1024]{1,0:T(8,128)(2,1)} async-done(((bf16[128,1024]{1,0:T(8,128)(2,1)}), bf16[4096,1024]{1,0:T(8,128)(2,1)}) %all-gather.32.cloned.1.call-update) | async-done | bytes 8388624 | tf_op jit(solution)/shard_map/all_gather | solution.py:263
  769.5 10.2 convolution_add_fusion.13
  779.7 45.5 %all-gather.36.cloned.1.call-done = bf16[512,1024]{1,0:T(8,128)(2,1)} async-done(((bf16[16,1024]{1,0:T(8,128)(2,1)}), bf16[512,1024]{1,0:T(8,128)(2,1)}) %all-gather.36.cloned.1.call-update) | async-done | bytes 1048592 | tf_op jit(solution)/shard_map/all_gather | solution.py:265
  827.3 4.8 fusion.274
  833.8 5.4 convolution_add_fusion.12
  843.2 17.0 %convolution_add_fusion.11 = f32[128,1024]{1,0:T(8,128)} fusion(bf16[1024,4096]{1,0:T(8,128)(2,1)} %all-gather.30.cloned.1.call-done, f32[128,4096]{1,0:T(8,128)} %fusion.273, f32[128,1024]{1,0:T(8,128)S(1)} %get-tuple-element.1271, bf16[4096,1024]{1,0:T(8,128)(2,1)} %all-gather.32.cloned.1.call-done, f32[128]{0:T(128)} %negate_multiply_fusion.9), kind=kOutput, calls=%fused_computation.167 | convolution fusion | flops 2185756672 | bytes 19923456 | tf_op jit(solution)/shard_map/dot_general | solution.py:22
  869.2 14.8 convolution_add_fusion.10
  937.0 83.3 %while.89 = (s32[]{:T(128)}, f32[128,16,64]{0,2,1:T(8,128)}, bf16[4,512,2048]{2,1,0:T(8,128)(2,1)}, s32[4]{0:T(128)S(1)}, s32[]{:T(128)}, /*index=5*/s32[1,128]{...) while((s32[]{:T(128)}, f32[128,16,64]{0,2,1:T(8,128)}, ...), condition=%wide.region_52.53_spmd.clone, body=%wide.region_49.52_spmd.clone.sunk | while | flops 685048448 | bytes 76764600 | solution.py:230
  938.2 13.8 conditional.15
  959.0 13.8 conditional.15
  979.8 13.8 conditional.15
  1000.6 13.8 conditional.15
  1025.8 84.9 %while.88 = (s32[]{:T(128)}, f32[128,16,64]{0,2,1:T(8,128)}, bf16[4,512,2048]{2,1,0:T(8,128)(2,1)}, s32[4]{0:T(128)S(1)}, s32[]{:T(128)}, /*index=5*/s32[1,128]{...) while((s32[]{:T(128)}, f32[128,16,64]{0,2,1:T(8,128)}, ...), condition=%wide.region_39.40_spmd.clone, body=%wide.region_36.39_spmd.clone.sunk | while | flops 685048448 | bytes 73618856 | solution.py:230
  1027.3 14.0 conditional.14
  1048.3 14.1 conditional.14
  1069.5 14.3 conditional.14
  1090.8 14.1 conditional.14
  1126.1 46.1 %reduce-scatter.22.cloned.1.call-done = bf16[32,2048]{1,0:T(8,128)(2,1)} async-done(((bf16[512,2048]{1,0:T(8,128)(2,1)}), bf16[32,2048]{1,0:T(8,128)(2,1)}) %reduce-scatter.22.cloned.1.call-update) | async-done | bytes 131088
  1176.5 104.5 %reduce-scatter.16.cloned.1.call-done = bf16[128,2048]{1,0:T(8,128)(2,1)} async-done(((bf16[2048,2048]{1,0:T(8,128)(2,1)}), bf16[128,2048]{1,0:T(8,128)(2,1)}) %reduce-scatter.16.cloned.1.call-update) | async-done | bytes 524304 | tf_op jit(solution)/shard_map/reduce_scatter | solution.py:474
  1281.0 5.2 fusion.92
  1286.2 103.7 %reduce-scatter.14.cloned.1.call-done = bf16[128,2048]{1,0:T(8,128)(2,1)} async-done(((bf16[2048,2048]{1,0:T(8,128)(2,1)}), bf16[128,2048]{1,0:T(8,128)(2,1)}) %reduce-scatter.14.cloned.1.call-update) | async-done | bytes 524304 | tf_op jit(solution)/shard_map/reduce_scatter | solution.py:474
  1389.9 5.2 fusion.93
  1396.1 128.1 %reduce-scatter.18.cloned.1.call-done = f32[32,512]{1,0:T(8,128)} async-done(((f32[1024,512]{1,0:T(8,128)}), f32[32,512]{1,0:T(8,128)}) %reduce-scatter.18.cloned.1.call-update) | async-done | bytes 65552 | tf_op jit(solution)/shard_map/reduce_scatter | solution.py:563
  1524.3 136.3 %reduce-scatter.20.cloned.1.call-done = f32[16,1024]{1,0:T(8,128)} async-done(((f32[512,1024]{1,0:T(8,128)}), f32[16,1024]{1,0:T(8,128)}) %reduce-scatter.20.cloned.1.call-update) | async-done | bytes 65552 | tf_op jit(solution)/shard_map/reduce_scatter | solution.py:564
  (797 shorter events, 370.5 us)
Async XLA Ops:
  7.2 65.4 %all-gather.24.cloned.1.call-start = ((), (), s32[]{:S(2)}) async-start(), calls=%async_computation.11 | async-start | bytes 4325376 | tf_op jit(solution)/shard_map/all_gather | solution.py:260
  7.9 135.6 %all-gather.16.cloned.1.call-start = ((), (), s32[]{:S(2)}) async-start(), calls=%async_computation.7 | async-start | bytes 6488064 | tf_op jit(solution)/shard_map/all_gather | solution.py:257
  8.6 67.7 %copy-start.100 = (bf16[2,32,1024]{2,1,0:T(8,128)(2,1)S(1)}, bf16[2,32,1024]{2,1,0:T(8,128)(2,1)}, u32[]{:S(2)}) copy-start(bf16[2,32,1024]{2,1,0:T(8,128)(2,1)} %param.33) | copy-start | bytes 393220
  8.7 333.0 %all-gather.26.cloned.1.call-start = ((), (), s32[]{:S(2)}) async-start(), calls=%async_computation.12 | async-start | bytes 2228224 | tf_op jit(solution)/shard_map/all_gather | solution.py:344
  76.3 67.2 %copy-start.58 = (bf16[2,128,1024]{2,1,0:T(8,128)(2,1)S(1)}, bf16[2,128,1024]{2,1,0:T(8,128)(2,1)}, u32[]{:S(2)}) copy-start(bf16[2,128,1024]{2,1,0:T(8,128)(2,1)} %param.32) | copy-start | bytes 1572868
  76.3 269.7 %all-gather.40.cloned.1.call-start = ((), (), s32[]{:S(2)}) async-start(), calls=%async_computation.19 | async-start | bytes 2228224 | tf_op jit(solution)/shard_map/all_gather | solution.py:344
  80.1 271.8 %all-gather.18.cloned.1.call-start = ((), (), s32[]{:S(2)}) async-start(), calls=%async_computation.8 | async-start | bytes 8912896 | tf_op jit(solution)/shard_map/all_gather | solution.py:322
  149.0 238.0 %all-gather.20.cloned.1.call-start = ((), (), s32[]{:S(2)}) async-start(), calls=%async_computation.9 | async-start | bytes 2162688 | tf_op jit(solution)/shard_map/all_gather | solution.py:258
  149.6 273.0 %all-gather.22.cloned.1.call-start = ((), (), s32[]{:S(2)}) async-start(), calls=%async_computation.10 | async-start | bytes 2162688 | tf_op jit(solution)/shard_map/all_gather | solution.py:259
  150.4 330.6 %all-gather.28.cloned.1.call-start = ((), (), s32[]{:S(2)}) async-start(), calls=%async_computation.13 | async-start | bytes 2162688 | tf_op jit(solution)/shard_map/all_gather | solution.py:261
  151.1 404.4 %all-gather.38.cloned.1.call-start = ((), (), s32[]{:S(2)}) async-start(), calls=%async_computation.18 | async-start | bytes 8912896 | tf_op jit(solution)/shard_map/all_gather | solution.py:322
  155.8 20.6 %copy-start.109 = (bf16[4,30,32]{2,0,1:T(4,128)(2,1)S(1)}, bf16[4,30,32]{2,0,1:T(4,128)(2,1)}, u32[]{:S(2)}) copy-start(bf16[4,30,32]{2,0,1:T(4,128)(2,1)} %param.47) | copy-start | bytes 23044
  156.7 478.5 %all-gather.30.cloned.1.call-start = ((), (), s32[]{:S(2)}) async-start(), calls=%async_computation.14 | async-start | bytes 8650752 | tf_op jit(solution)/shard_map/all_gather | solution.py:262
  157.3 533.5 %all-gather.34.cloned.1.call-start = ((), (), s32[]{:S(2)}) async-start(), calls=%async_computation.16 | async-start | bytes 1081344 | tf_op jit(solution)/shard_map/all_gather | solution.py:264
  158.0 611.5 %all-gather.32.cloned.1.call-start = ((), (), s32[]{:S(2)}) async-start(), calls=%async_computation.15 | async-start | bytes 8650752 | tf_op jit(solution)/shard_map/all_gather | solution.py:263
  158.6 666.5 %all-gather.36.cloned.1.call-start = ((), (), s32[]{:S(2)}) async-start(), calls=%async_computation.17 | async-start | bytes 1081344 | tf_op jit(solution)/shard_map/all_gather | solution.py:265
  159.3 961.4 %reduce-scatter.26.cloned.1.call-start = ((), (), s32[]{:S(2)}) async-start(), calls=%async_computation.26 | async-start | bytes 540672
  247.3 67.7 %copy-start.142 = (s32[2,32]{1,0:T(2,128)S(1)}, s32[2,32]{1,0:T(2,128)}, u32[]{:S(2)}) copy-start(s32[2,32]{1,0:T(2,128)} %param.36) | copy-start | bytes 772
  247.8 103.2 %copy-start.61 = (bf16[30,16,64]{2,1,0:T(8,128)(2,1)}, bf16[30,16,64]{2,1,0:T(8,128)(2,1)S(1)}, u32[]{:S(2)}) copy-start(bf16[30,16,64]{2,1,0:T(8,128)(2,1)S(1)} %reshape_squeeze.8) | copy-start | bytes 184324
  248.3 103.4 %copy-start.59 = (bf16[30,16,64]{2,1,0:T(8,128)(2,1)}, bf16[30,16,64]{2,1,0:T(8,128)(2,1)S(1)}, u32[]{:S(2)}) copy-start(bf16[30,16,64]{2,1,0:T(8,128)(2,1)S(1)} %reshape_squeeze.9) | copy-start | bytes 184324
  315.0 109.8 %copy-start.63 = (bf16[30,16,64]{2,1,0:T(8,128)(2,1)}, bf16[30,16,64]{2,1,0:T(8,128)(2,1)S(1)}, u32[]{:S(2)}) copy-start(bf16[30,16,64]{2,1,0:T(8,128)(2,1)S(1)} %reshape_squeeze.10) | copy-start | bytes 184324
  351.2 12.3 copy-start.43
  352.0 11.5 copy-start.104
  389.3 91.6 %copy-start.22 = (f32[128,1024]{1,0:T(8,128)}, f32[128,1024]{1,0:T(8,128)S(1)}, u32[]{:S(2)}) copy-start(f32[128,1024]{1,0:T(8,128)S(1)} %get-tuple-element.1331) | copy-start | bytes 1572868
  389.4 91.6 %copy-start.110 = (f32[128]{0:T(128)}, f32[128]{0:T(128)S(1)}, u32[]{:S(2)}) copy-start(f32[128]{0:T(128)S(1)} %broadcast_multiply_fusion.5) | copy-start | bytes 1540
  389.6 35.5 %copy-start.144 = (f32[128]{0:T(128)}, f32[128]{0:T(128)S(1)}, u32[]{:S(2)}) copy-start(f32[128]{0:T(128)S(1)} %multiply_reduce_fusion.13) | copy-start | bytes 1540
  389.6 35.5 %copy-start.86 = (pred[128,512]{1,0:T(8,128)(4,1)S(1)}, pred[128,512]{1,0:T(8,128)(4,1)}, u32[]{:S(2)}) copy-start(pred[128,512]{1,0:T(8,128)(4,1)} %broadcast_compare_fusion.1) | copy-start | bytes 196612
  389.6 91.3 %copy-start.121 = (f32[128]{0:T(128)}, f32[128]{0:T(128)S(1)}, u32[]{:S(2)}) copy-start(f32[128]{0:T(128)S(1)} %fusion.210) | copy-start | bytes 1540
  483.2 83.6 %copy-start.115 = (f32[128]{0:T(128)}, f32[128]{0:T(128)S(1)}, u32[]{:S(2)}) copy-start(f32[128]{0:T(128)S(1)} %broadcast_multiply_fusion.4) | copy-start | bytes 1540
  483.4 83.4 %copy-start.146 = (f32[128]{0:T(128)}, f32[128]{0:T(128)S(1)}, u32[]{:S(2)}) copy-start(f32[128]{0:T(128)S(1)} %multiply_reduce_fusion.12) | copy-start | bytes 1540
  555.5 11.4 copy-start.106
  604.4 86.4 %copy-start.68 = (bf16[128,1024]{1,0:T(8,128)(2,1)}, bf16[128,1024]{1,0:T(8,128)(2,1)S(1)}, u32[]{:S(2)}) copy-start(bf16[128,1024]{1,0:T(8,128)(2,1)S(1)} %get-tuple-element.1316) | copy-start | bytes 786436
  604.4 227.7 %copy-start.66 = (bf16[128,1024]{1,0:T(8,128)(2,1)}, bf16[128,1024]{1,0:T(8,128)(2,1)S(1)}, u32[]{:S(2)}) copy-start(bf16[128,1024]{1,0:T(8,128)(2,1)S(1)} %get-tuple-element.1317) | copy-start | bytes 786436
  693.6 131.5 %copy-start.94 = (bf16[128,512]{1,0:T(8,128)(2,1)S(1)}, bf16[128,512]{1,0:T(8,128)(2,1)}, u32[]{:S(2)}) copy-start(bf16[128,512]{1,0:T(8,128)(2,1)} %get-tuple-element.1278) | copy-start | bytes 393220
  825.1 8.6 slice-start.2
  827.3 6.4 slice-start.3
  842.6 17.6 %copy-start.35 = (f32[128,1024]{1,0:T(8,128)}, f32[128,1024]{1,0:T(8,128)S(1)}, u32[]{:S(2)}) copy-start(f32[128,1024]{1,0:T(8,128)S(1)} %get-tuple-element.1271) | copy-start | bytes 1572868
  869.2 14.9 copy-start.128
  914.1 208.2 %reduce-scatter.24.cloned.1.call-start = ((), (), s32[]{:S(2)}) async-start(), calls=%async_computation.25 | async-start | bytes 2228224
  921.6 250.6 %reduce-scatter.22.cloned.1.call-start = ((), (), s32[]{:S(2)}) async-start(), calls=%async_computation.24 | async-start | bytes 2228224
  930.5 350.5 %reduce-scatter.16.cloned.1.call-start = ((), (), s32[]{:S(2)}) async-start(), calls=%async_computation.21 | async-start | bytes 8912896 | tf_op jit(solution)/shard_map/reduce_scatter | solution.py:474
  1020.3 369.7 %reduce-scatter.14.cloned.1.call-start = ((), (), s32[]{:S(2)}) async-start(), calls=%async_computation.20 | async-start | bytes 8912896 | tf_op jit(solution)/shard_map/reduce_scatter | solution.py:474
  1110.7 413.6 %reduce-scatter.18.cloned.1.call-start = ((), (), s32[]{:S(2)}) async-start(), calls=%async_computation.22 | async-start | bytes 2162688 | tf_op jit(solution)/shard_map/reduce_scatter | solution.py:563
  1114.0 546.6 %reduce-scatter.20.cloned.1.call-start = ((), (), s32[]{:S(2)}) async-start(), calls=%async_computation.23 | async-start | bytes 2162688 | tf_op jit(solution)/shard_map/reduce_scatter | solution.py:564
  1126.0 155.0 %copy-start.40 = (f32[128,1024]{1,0:T(8,128)S(1)}, f32[128,1024]{1,0:T(8,128)}, u32[]{:S(2)}) copy-start(f32[128,1024]{1,0:T(8,128)} %copy-done.39) | copy-start | bytes 1572868
  1126.1 154.9 %copy-start.136 = (f32[128]{0:T(128)S(1)}, f32[128]{0:T(128)}, u32[]{:S(2)}) copy-start(f32[128]{0:T(128)} %copy-done.135) | copy-start | bytes 1540
  1176.5 213.4 %copy-start.38 = (f32[128,1024]{1,0:T(8,128)S(1)}, f32[128,1024]{1,0:T(8,128)}, u32[]{:S(2)}) copy-start(f32[128,1024]{1,0:T(8,128)} %copy-done.37) | copy-start | bytes 1572868
  1176.5 213.4 %copy-start.138 = (f32[128]{0:T(128)S(1)}, f32[128]{0:T(128)}, u32[]{:S(2)}) copy-start(f32[128]{0:T(128)} %copy-done.137) | copy-start | bytes 1540
  (149 other events, 300.8 us)
Sparse Core Ops, SparseCore 0:
  11.0 61.5 all-gather.23
  75.5 67.9 all-gather.15
  146.2 39.2 all-gather.25
  187.6 41.0 all-gather.39
  231.2 73.8 all-gather.17
  308.0 56.1 all-gather.19
  367.2 55.3 all-gather.21
  425.6 55.3 all-gather.27
  483.1 72.2 all-gather.37
  558.3 76.8 all-gather.29
  638.1 52.6 all-gather.33
  693.6 75.8 all-gather.31
  772.4 52.6 all-gather.35
  914.2 126.8 reduce-scatter.25
  1045.2 62.7 reduce-scatter.23
  1111.5 60.5 reduce-scatter.21
  1176.6 104.3 reduce-scatter.15
  1285.5 104.4 reduce-scatter.13
  1392.8 131.3 reduce-scatter.17
  1526.9 133.5 reduce-scatter.19
where the time goes:
time: 1680 us; the launch traced here: 1670 us
  waiting for transfers between devices  1010 us (60%)
  matrix products  255 us (15%)
  local copies, waits for them, and re-layouts  183 us (11%)
  blocking collectives  175 us (10%)
  other arithmetic  17 us (1%)
  between operations  17 us (1%)
    reduce_scatter x2, waiting for transfers between devices, backward_row(): lax.psum_scatter(self_terms.astype(jnp.bfloat16), 'seq', scatter_dimensio...  208 us
    reduce_scatter x1, waiting for transfers between devices, per_device(): lax.psum_scatter(row_grads[1], ('seq', 'rows'), scatter_dimension=0, tile...  136 us
    reduce_scatter x1, waiting for transfers between devices, per_device(): lax.psum_scatter(row_grads[0], ('seq', 'rows'), scatter_dimension=0, tile...  128 us
    all_gather x1, waiting for transfers between devices, fetch_all(): lax.all_gather(outer_weight, ('seq', 'rows'), axis=0, tiled=True)  75.9 us
    all_gather x2, waiting for transfers between devices, forward_row(): lax.all_gather(local_pairs, 'seq', axis=0, tiled=True)  71.6 us
    all_gather x1, blocking collectives, fetch_all(): lax.all_gather(prefixes, ('seq', 'rows'), axis=2, tiled=True)  69.2 us
    all_gather x1, blocking collectives, fetch_all(): lax.all_gather(norm_gains, ('seq', 'rows'), axis=1, tiled=True)  65 us
    all_gather x1, waiting for transfers between devices, fetch_all(): lax.all_gather(cross_memory, ('seq', 'rows'), axis=0, tiled=True)  63.9 us
  transfers between devices with their start and end apart: 20, of which 14 were waited for; matrix products, arithmetic and copies ran while one was open for 20% of the time, Pallas kernels for 0%

commit v1 on v0

--- a/solution.py
+++ b/solution.py
@@ -3,11 +3,17 @@
 import jax
 import jax.numpy as jnp
 from jax import lax
+from jax.experimental import pallas as pl
+from jax.experimental.pallas import tpu as pltpu
 from jax.sharding import PartitionSpec as P
 
 D = 1024
 HEADS = 16
 HEAD_DIM = 64
+ADAPTER = 512
+PREFIX = 30
+S_DEV = 128
+M_DEV = 32
 
 
 score_scale = 0.125
@@ -583,6 +589,820 @@
     )
 
 
+MESH_ID = pl.DeviceIdType.MESH
+F32 = jnp.float32
+BF16 = jnp.bfloat16
+VMEM_BYTES = 60 * 1024 * 1024
+PAIRS = HEADS // 2
+LANES = 2 * HEAD_DIM
+Q_AT, K_AT, V_AT, SELF_OUT_AT, CROSS_Q_AT, MEM_K_AT, MEM_V_AT, CROSS_OUT_AT, SMALL_AT = range(0, 288, 32)
+SMALL_ROWS = 16
+FIRST_ROWS = SMALL_AT + SMALL_ROWS
+FEED_ROWS = 288
+
+
+def whole(space=pltpu.VMEM):
+    return pl.BlockSpec(memory_space=space)
+
+
+def params(collective_id=None):
+    if collective_id is None:
+        return pltpu.CompilerParams(vmem_limit_bytes=VMEM_BYTES)
+    return pltpu.CompilerParams(
+        vmem_limit_bytes=VMEM_BYTES, collective_id=collective_id, has_side_effects=True
+    )
+
+
+def remote(src, dst, send_sem, recv_sem, device):
+    return pltpu.make_async_remote_copy(
+        src_ref=src, dst_ref=dst, send_sem=send_sem, recv_sem=recv_sem,
+        device_id=device, device_id_type=MESH_ID,
+    )
+
+
+def greet(peers):
+    barrier = pltpu.get_barrier_semaphore()
+    for peer in peers:
+        pl.semaphore_signal(barrier, inc=1, device_id=peer, device_id_type=MESH_ID)
+    pl.semaphore_wait(barrier, len(peers))
+
+
+def dot_nn(left, right):
+    return lax.dot_general(left, right, (((1,), (0,)), ((), ())), preferred_element_type=F32)
+
+
+def gather_kernel(
+    project, self_out, cross_q, cross_mem, cross_out, small, memory,
+    full, memory_full, local_sem, *sems,
+):
+    seq, x = lax.axis_index("seq"), lax.axis_index("rows")
+    z, y, core = seq // 4, (seq // 2) % 2, seq % 2
+
+    def device(z, y, core, x):
+        return ((z * 2 + y) * 2 + core, x)
+
+    along_z = [device((z + step) % 4, y, core, x) for step in (1, 2, 3)]
+    along_x, along_y = device(z, y, core, 1 - x), device(z, 1 - y, core, x)
+    other_core = device(z, y, 1 - core, x)
+    greet(along_z + [along_x, along_y, other_core])
+    send0, recv0, send1, recv1, send2, recv2, send3, recv3 = sems
+
+    pieces = [
+        (project.at[:, pl.ds(0, 1024)], Q_AT, 32),
+        (project.at[:, pl.ds(1024, 1024)], K_AT, 32),
+        (project.at[:, pl.ds(2048, 1024)], V_AT, 32),
+        (small, SMALL_AT, SMALL_ROWS),
+        (self_out, SELF_OUT_AT, 32),
+        (cross_q, CROSS_Q_AT, 32),
+        (cross_mem.at[:, pl.ds(0, 1024)], MEM_K_AT, 32),
+        (cross_mem.at[:, pl.ds(1024, 1024)], MEM_V_AT, 32),
+        (cross_out, CROSS_OUT_AT, 32),
+    ]
+    stages = []
+    for k, (source, first, count) in enumerate(pieces):
+        rows = pl.ds(first, count)
+        mine = full.at[z, y, core, x, rows]
+        near, far = pl.ds(0, 2), pl.ds(2, 2)
+        near1, far1 = full.at[near, y, core, x, rows], full.at[far, y, core, x, rows]
+        near2, far2 = full.at[near, y, core, :, rows], full.at[far, :, core, x, rows]
+        half = full.at[:, :, core, :, rows]
+        stages.append((
+            pltpu.make_async_copy(source, mine, local_sem.at[k]),
+            [remote(source, mine, send0.at[k, d], recv0.at[k, d], along_z[d]) for d in range(3)],
+            [remote(near1, near1, send1.at[k, 0], recv1.at[k, 0], along_x),
+             remote(far1, far1, send1.at[k, 1], recv1.at[k, 1], along_y)],
+            [remote(near2, near2, send2.at[k, 0], recv2.at[k, 0], along_y),
+             remote(far2, far2, send2.at[k, 1], recv2.at[k, 1], along_x)],
+            [remote(half, half, send3.at[k, 0], recv3.at[k, 0], other_core)],
+        ))
+    k = len(pieces)
+    mine = memory_full.at[z, y, core]
+    column = memory_full.at[:, y, core]
+    half = memory_full.at[:, :, core]
+    stages.append((
+        pltpu.make_async_copy(memory, mine, local_sem.at[k]),
+        [remote(memory, mine, send0.at[k, d], recv0.at[k, d], along_z[d]) for d in range(3)],
+        [remote(column, column, send1.at[k, 1], recv1.at[k, 1], along_y)],
+        [],
+        [remote(half, half, send3.at[k, 0], recv3.at[k, 0], other_core)],
+    ))
+    order = list(range(4)) + [k] + list(range(4, k))
+    stages = [stages[at] for at in order]
+    for local, *_ in stages:
+        local.start()
+    total = len(stages)
+    for tick in range(total + 4):
+        for level in range(5):
+            k = tick - level
+            if not 0 <= k < total:
+                continue
+            if level == 1:
+                stages[k][0].wait()
+            if level > 0:
+                for copy in stages[k][level]:
+                    copy.wait_recv()
+            if level < 4:
+                for copy in stages[k][level + 1]:
+                    copy.start()
+    for _, *levels in stages:
+        for level in levels:
+            for copy in level:
+                copy.wait_send()
+
+
+def gather_first(project, self_out, cross_q, cross_mem, cross_out, small, memory):
+    count = 10
+    sems = []
+    for width in (3, 2, 2, 1):
+        sems += [pltpu.SemaphoreType.DMA((count, width))] * 2
+    full, memory_full = pl.pallas_call(
+        gather_kernel,
+        out_shape=(
+            jax.ShapeDtypeStruct((4, 2, 2, 2, FIRST_ROWS, D), BF16),
+            jax.ShapeDtypeStruct((4, 2, 2) + memory.shape, BF16),
+        ),
+        in_specs=[whole(pl.ANY)] * 7,
+        out_specs=(whole(pl.ANY), whole(pl.ANY)),
+        scratch_shapes=[pltpu.SemaphoreType.DMA((count,))] + sems,
+        compiler_params=params(0),
+        name="gather_first",
+    )(project, self_out, cross_q, cross_mem, cross_out, small, memory)
+    return full.reshape(32, FIRST_ROWS, D), memory_full.reshape((16,) + memory.shape)
+
+
+def project_kernel(tokens, full, arrived, weights, staged, weight_sem, local_sem, send_sem, recv_sem):
+    seq, x = lax.axis_index("seq"), lax.axis_index("rows")
+    fetches = [
+        pltpu.make_async_copy(full.at[:, pl.ds(32 * part, 32)], weights.at[part], weight_sem.at[part])
+        for part in range(3)
+    ]
+    for fetch in fetches:
+        fetch.start()
+    greet([((seq + step) % 16, x) for step in range(1, 16)])
+    rows = tokens[...].reshape(2 * S_DEV, D)
+    for part in range(3):
+        fetches[part].wait()
+        result = dot_nn(rows, weights[part].reshape(D, D)).astype(BF16)
+        for row in range(2):
+            for pair in range(PAIRS):
+                staged[pair, row, part] = result[
+                    row * S_DEV:(row + 1) * S_DEV, pair * LANES:(pair + 1) * LANES
+                ]
+    copies = []
+    for step in range(1, 16):
+        to = (seq + step) % 16
+        copies.append(remote(
+            staged.at[to // 2, to % 2], arrived.at[seq], send_sem.at[step], recv_sem.at[step], (to, x)
+        ))
+    own = pltpu.make_async_copy(staged.at[seq // 2, seq % 2], arrived.at[seq], local_sem)
+    own.start()
+    for copy in copies:
+        copy.start()
+    own.wait()
+    for copy in copies:
+        copy.wait()
+
+
+def project_exchange(tokens, full):
+    return pl.pallas_call(
+        project_kernel,
+        out_shape=jax.ShapeDtypeStruct((16, 3, S_DEV, LANES), BF16),
+        in_specs=[whole(), whole(pl.ANY)],
+        out_specs=whole(pl.ANY),
+        scratch_shapes=[
+            pltpu.VMEM((3, 32, 32, D), BF16),
+            pltpu.VMEM((PAIRS, 2, 3, S_DEV, LANES), BF16),
+            pltpu.SemaphoreType.DMA((3,)),
+            pltpu.SemaphoreType.DMA,
+            pltpu.SemaphoreType.DMA((16,)),
+            pltpu.SemaphoreType.DMA((16,)),
+        ],
+        compiler_params=params(1),
+        name="project_exchange",
+    )(tokens, full)
+
+
+def head_masks():
+    lane = lax.broadcasted_iota(jnp.int32, (1, LANES), 1)
+    first = (lane < HEAD_DIM).astype(F32).astype(BF16)
+    return first, (1.0 - first.astype(F32)).astype(BF16)
+
+
+def stack_heads(block):
+    first, second = head_masks()
+    return jnp.concatenate([block * first, block * second], axis=0)
+
+
+def merge_heads(stacked):
+    half = stacked.shape[0] // 2
+    lane = lax.broadcasted_iota(jnp.int32, (half, LANES), 1)
+    return jnp.where(lane < HEAD_DIM, stacked[:half], stacked[half:])
+
+
+def rows_in_lanes(values):
+    lane = lax.broadcasted_iota(jnp.int32, (8, LANES), 1)
+    row = lax.broadcasted_iota(jnp.int32, (8, LANES), 0)
+    picks = (lane // HEAD_DIM == row).astype(F32)
+    return lax.dot_general(
+        picks, values, (((1,), (1,)), ((), ())),
+        precision=lax.Precision.HIGHEST, preferred_element_type=F32,
+    )
+
+
+def self_forward_kernel(
+    arrived, docs_row, docs_column, prefix_keys, prefix_values,
+    gathered, attended, inverse, staged, sums, parts, local_sem, send_sem, recv_sem,
+):
+    seq, x = lax.axis_index("seq"), lax.axis_index("rows")
+    block = 2 * S_DEV
+    greet([((seq + step) % 16, x) for step in range(1, 16)])
+    pair, row = seq // 2, seq % 2
+    columns = pl.ds(pl.multiple_of(pair * LANES, LANES), LANES)
+    mine = gathered.at[row, :, columns]
+    away = (
+        lax.broadcasted_iota(jnp.int32, (block, block), 1)
+        - lax.broadcasted_iota(jnp.int32, (block, block), 0)
+    )
+    prefix_lane = lax.broadcasted_iota(jnp.int32, (2 * block, 32), 1)
+
+    def one_block(step, carry):
+        at = (step + seq // 2) % 8
+        queries = stack_heads(arrived[pl.ds(2 * at, 2), 0].reshape(block, LANES))
+        query_docs = docs_column[pl.ds(at * block, block)]
+        scores = dot_right(queries, prefix_keys[...]) * score_scale
+        weights = jnp.where(prefix_lane < PREFIX, jnp.exp(scores), 0.0)
+        sums[...] = jnp.concatenate([weights, jnp.zeros((2 * block, LANES - 32), F32)], axis=1)
+        parts[...] = dot_nn(weights.astype(BF16), prefix_values[...])
+
+        def one_tile(key_at, carry):
+            keys = arrived[pl.ds(2 * key_at, 2), 1].reshape(block, LANES)
+            values = arrived[pl.ds(2 * key_at, 2), 2].reshape(block, LANES)
+            key_docs = docs_row[:, pl.ds(pl.multiple_of(key_at * block, block), block)]
+            same = jnp.concatenate([query_docs, query_docs], axis=1) == key_docs
+            allowed = same & (away <= (at - key_at) * block)
+            scores = dot_right(queries, keys) * score_scale
+            weights = jnp.where(allowed[None], jnp.exp(scores).reshape(2, block, block), 0.0)
+            weights = weights.reshape(2 * block, block)
+            sums[...] += weights[:, :LANES] + weights[:, LANES:]
+            parts[...] += dot_nn(weights.astype(BF16), values)
+            return carry
+
+        lax.fori_loop(0, at + 1, one_tile, 0)
+        totals = 1.0 / jnp.sum(sums[...], axis=1, keepdims=True)
+        result = merge_heads(parts[...] * totals)
+        here = pl.ds(at * block, block)
+        attended[here] = result
+        inverse[here] = merge_heads(jnp.broadcast_to(totals, (2 * block, LANES)))
+        staged[pl.ds(2 * at, 2)] = result.astype(BF16).reshape(2, S_DEV, LANES)
+        for half in range(2):
+            to = 2 * at + half
+
+            @pl.when(to != seq)
+            def _():
+                remote(staged.at[to], mine, send_sem.at[to], recv_sem.at[seq], (to, x)).start()
+
+            @pl.when(to == seq)
+            def _():
+                pltpu.make_async_copy(staged.at[to], mine, local_sem).start()
+
+        return carry
+
+    lax.fori_loop(0, 8, one_block, 0)
+    pltpu.make_async_copy(staged.at[seq], mine, local_sem).wait()
+    for step in range(1, 16):
+        other = (seq + step) % 16
+        remote(staged.at[other], mine, send_sem.at[other], recv_sem.at[other], (other, x)).wait()
+
+
+def self_forward(arrived, docs_row, docs_column, prefix_keys, prefix_values):
+    length = 16 * S_DEV
+    return pl.pallas_call(
+        self_forward_kernel,
+        out_shape=(
+            jax.ShapeDtypeStruct((2, S_DEV, D), BF16),
+            jax.ShapeDtypeStruct((length, LANES), F32),
+            jax.ShapeDtypeStruct((length, LANES), F32),
+        ),
+        in_specs=[whole()] * 5,
+        out_specs=(whole(), whole(), whole()),
+        scratch_shapes=[
+            pltpu.VMEM((16, S_DEV, LANES), BF16),
+            pltpu.VMEM((4 * S_DEV, LANES), F32),
+            pltpu.VMEM((4 * S_DEV, LANES), F32),
+            pltpu.SemaphoreType.DMA,
+            pltpu.SemaphoreType.DMA((16,)),
+            pltpu.SemaphoreType.DMA((16,)),
+        ],
+        compiler_params=params(2),
+        name="self_forward",
+    )(arrived, docs_row, docs_column, prefix_keys, prefix_values)
+
+
+def self_backward_kernel(
+    arrived, grad_out, attended, inverse, docs_row, docs_column, prefix_keys, prefix_values,
+    gathered, prefix_grads,
+    grads, grad_low, delta, query_grads, key_grads, value_grads, staged,
+    local_sem, in_send, in_recv, out_send, out_recv, query_send, query_recv,
+):
+    seq, x = lax.axis_index("seq"), lax.axis_index("rows")
+    block = 2 * S_DEV
+    pair, row = seq // 2, seq % 2
+    greet([((seq + step) % 16, x) for step in range(1, 16)])
+
+    def heads_for(to):
+        return grad_out.at[to % 2, :, pl.ds(pl.multiple_of((to // 2) * LANES, LANES), LANES)]
+
+    own = pltpu.make_async_copy(heads_for(seq), grads.at[seq], local_sem.at[0])
+    own.start()
+    arrivals = []
+    for step in range(1, 16):
+        to = (seq + step) % 16
+        arrivals.append(remote(heads_for(to), grads.at[seq], in_send.at[step], in_recv.at[step], (to, x)))
+        arrivals[-1].start()
+    own.wait()
+    for copy in arrivals:
+        copy.wait()
+
+    pad_row = lax.broadcasted_iota(jnp.int32, (64, block), 0) % 32
+    prefix_key_stack = stack_heads(prefix_keys[...])
+    prefix_value_stack = stack_heads(prefix_values[...])
+
+    def head_rows(at, count):
+        there = delta[:, pl.ds(pl.multiple_of(at * block, block), block)]
+        return jnp.concatenate(
+            [jnp.broadcast_to(there[0:1], (count, block)), jnp.broadcast_to(there[1:2], (count, block))],
+            axis=0,
+        )
+
+    prefix_grads[...] = jnp.zeros(prefix_grads.shape, F32)
+
+    def prepare(at, carry):
+        here = pl.ds(at * block, block)
+        grad = grads[pl.ds(2 * at, 2)].reshape(block, LANES).astype(F32) * inverse[here]
+        low = grad.astype(BF16)
+        grad_low[here] = low
+        delta[:, pl.ds(pl.multiple_of(at * block, block), block)] = rows_in_lanes(grad * attended[here])
+        queries = arrived[pl.ds(2 * at, 2), 0].reshape(block, LANES)
+        weights = jnp.exp(dot_right(prefix_key_stack, queries) * score_scale)
+        weights = jnp.where(pad_row < PREFIX, weights, 0.0)
+        slopes = (weights * (dot_right(prefix_value_stack, low) - head_rows(at, 32))).astype(BF16)
+        prefix_grads[0] += merge_heads(dot_nn(slopes, queries)) * score_scale
+        prefix_grads[1] += merge_heads(dot_nn(weights.astype(BF16), low))
+        query_grads[here] = dot_left(slopes, prefix_key_stack)
+        return carry
+
+    lax.fori_loop(0, 8, prepare, 0)
+    away = (
+        lax.broadcasted_iota(jnp.int32, (block, block), 0)
+        - lax.broadcasted_iota(jnp.int32, (block, block), 1)
+    )
+
+    def send_block(part, count, at, send, recv):
+        for half in range(2):
+            to = 2 * at + half
+            source = staged.at[to, pl.ds(part, count)]
+            mine = gathered.at[pair, row, pl.ds(part, count)]
+
+            @pl.when(to != seq)
+            def _():
+                remote(source, mine, send.at[to], recv.at[seq], (to, x)).start()
+
+            @pl.when(to == seq)
+            def _():
+                pltpu.make_async_copy(source, mine, local_sem.at[1 + part]).start()
+
+    def one_block(step, carry):
+        key_at = (step + seq // 2) % 8
+        keys = stack_heads(arrived[pl.ds(2 * key_at, 2), 1].reshape(block, LANES))
+        values = stack_heads(arrived[pl.ds(2 * key_at, 2), 2].reshape(block, LANES))
+        key_docs = docs_column[pl.ds(key_at * block, block)]
+        key_docs = jnp.concatenate([key_docs, key_docs], axis=1)
+        key_grads[...] = jnp.zeros(key_grads.shape, F32)
+        value_grads[...] = jnp.zeros(value_grads.shape, F32)
+
+        def one_tile(at, carry):
+            here = pl.ds(at * block, block)
+            queries = arrived[pl.ds(2 * at, 2), 0].reshape(block, LANES)
+            low = grad_low[here]
+            query_docs = docs_row[:, pl.ds(pl.multiple_of(at * block, block), block)]
+            allowed = (key_docs == query_docs) & (away <= (at - key_at) * block)
+            weights = jnp.exp(dot_right(keys, queries) * score_scale).reshape(2, block, block)
+            weights = jnp.where(allowed[None], weights, 0.0).reshape(2 * block, block)
+            slopes = (weights * (dot_right(values, low) - head_rows(at, block))).astype(BF16)
+            key_grads[...] += dot_nn(slopes, queries)
+            value_grads[...] += dot_nn(weights.astype(BF16), low)
+            query_grads[here] += dot_left(slopes, keys)
+            return carry
+
+        lax.fori_loop(key_at, 8, one_tile, 0)
+        there = pl.ds(2 * key_at, 2)
+        staged[there, 1] = (merge_heads(key_grads[...]) * score_scale).astype(BF16).reshape(2, S_DEV, LANES)
+        staged[there, 2] = merge_heads(value_grads[...]).astype(BF16).reshape(2, S_DEV, LANES)
+        send_block(1, 2, key_at, out_send, out_recv)
+        return carry
+
+    lax.fori_loop(0, 8, one_block, 0)
+
+    def last_block(step, carry):
+        at = (step + seq // 2) % 8
+        result = (query_grads[pl.ds(at * block, block)] * score_scale).astype(BF16)
+        staged[pl.ds(2 * at, 2), 0] = result.reshape(2, S_DEV, LANES)
+        send_block(0, 1, at, query_send, query_recv)
+        return carry
+
+    lax.fori_loop(0, 8, last_block, 0)
+    pltpu.make_async_copy(staged.at[seq, pl.ds(1, 2)], gathered.at[pair, row, pl.ds(1, 2)], local_sem.at[2]).wait()
+    pltpu.make_async_copy(staged.at[seq, pl.ds(0, 1)], gathered.at[pair, row, pl.ds(0, 1)], local_sem.at[1]).wait()
+    for step in range(1, 16):
+        other = (seq + step) % 16
+        mine = gathered.at[other // 2, other % 2]
+        remote(
+            staged.at[other, pl.ds(1, 2)], mine.at[pl.ds(1, 2)], out_send.at[other], out_recv.at[other], (other, x)
+        ).wait()
+        remote(
+            staged.at[other, pl.ds(0, 1)], mine.at[pl.ds(0, 1)], query_send.at[other], query_recv.at[other], (other, x)
+        ).wait()
+
+
+def self_backward(arrived, grad_out, attended, inverse, docs_row, docs_column, prefix_keys, prefix_values):
+    length = 16 * S_DEV
+    dma = pltpu.SemaphoreType.DMA
+    return pl.pallas_call(
+        self_backward_kernel,
+        out_shape=(
+            jax.ShapeDtypeStruct((PAIRS, 2, 3, S_DEV, LANES), BF16),
+            jax.ShapeDtypeStruct((2, 32, LANES), F32),
+        ),
+        in_specs=[whole()] * 8,
+        out_specs=(whole(), whole()),
+        scratch_shapes=[
+            pltpu.VMEM((16, S_DEV, LANES), BF16),
+            pltpu.VMEM((length, LANES), BF16),
+            pltpu.VMEM((8, length), F32),
+            pltpu.VMEM((length, LANES), F32),
+            pltpu.VMEM((4 * S_DEV, LANES), F32),
+            pltpu.VMEM((4 * S_DEV, LANES), F32),
+            pltpu.VMEM((16, 3, S_DEV, LANES), BF16),
+            dma((3,)), dma((16,)), dma((16,)), dma((16,)), dma((16,)), dma((16,)), dma((16,)),
+        ],
+        compiler_params=params(3),
+        name="self_backward",
+    )(arrived, grad_out, attended, inverse, docs_row, docs_column, prefix_keys, prefix_values)
+
+
+def cross_forward_kernel(
+    queries, keys, values, query_docs, key_docs, prefix_keys, prefix_values, crossed, inverse
+):
+    stacked = stack_heads(queries[0])
+    count = 2 * S_DEV
+    prefix_lane = lax.broadcasted_iota(jnp.int32, (count, 32), 1)
+    scores = dot_right(stacked, prefix_keys[...]) * score_scale
+    prefix_weights = jnp.where(prefix_lane < PREFIX, jnp.exp(scores), 0.0)
+    memory_len = keys.shape[0] * keys.shape[2]
+    scores = dot_right(stacked, keys[...].reshape(memory_len, LANES)) * score_scale
+    allowed = query_docs[0] == key_docs[0]
+    weights = jnp.where(allowed[None], jnp.exp(scores).reshape(2, S_DEV, memory_len), 0.0)
+    weights = weights.reshape(count, memory_len)
+    totals = jnp.sum(weights, axis=1, keepdims=True) + jnp.sum(prefix_weights, axis=1, keepdims=True)
+    totals = 1.0 / totals
+    summed = dot_nn(weights.astype(BF16), values[...].reshape(memory_len, LANES))
+    summed += dot_nn(prefix_weights.astype(BF16), prefix_values[...])
+    crossed[0] = merge_heads(summed * totals)
+    inverse[0] = merge_heads(jnp.broadcast_to(totals, (count, LANES)))
+
+
+def cross_forward(queries, memory_pairs, query_docs, key_docs, prefix_keys, prefix_values):
+    memory_len = 16 * M_DEV
+    head_block = pl.BlockSpec((1, S_DEV, LANES), lambda row, pair: (row, 0, pair))
+    keys = pl.BlockSpec((16, 1, M_DEV, LANES), lambda row, pair: (0, row, 0, pair))
+    values = pl.BlockSpec((16, 1, M_DEV, LANES), lambda row, pair: (0, row, 0, PAIRS + pair))
+    prefix = pl.BlockSpec((32, LANES), lambda row, pair: (0, pair))
+    return pl.pallas_call(
+        cross_forward_kernel,
+        grid=(2, PAIRS),
+        out_shape=(jax.ShapeDtypeStruct((2, S_DEV, D), F32),) * 2,
+        in_specs=[
+            head_block, keys, values,
+            pl.BlockSpec((1, S_DEV, memory_len), lambda row, pair: (row, 0, 0)),
+            pl.BlockSpec((1, 1, memory_len), lambda row, pair: (row, 0, 0)),
+            prefix, prefix,
+        ],
+        out_specs=(head_block, head_block),
+        compiler_params=params(),
+        name="cross_forward",
+    )(queries, memory_pairs, memory_pairs, query_docs, key_docs, prefix_keys, prefix_values)
+
+
+def cross_backward_kernel(
+    queries, keys, values, query_docs, key_docs, prefix_keys, prefix_values, grad_out, crossed, inverse,
+    query_grad, key_grad, value_grad, prefix_grads,
+):
+    row = pl.program_id(1)
+    memory_len = keys.shape[0] * keys.shape[2]
+    heads = queries[0]
+    grad = grad_out[0] * inverse[0]
+    low = grad.astype(BF16)
+    delta = rows_in_lanes(grad * crossed[0])
+
+    def head_rows(count):
+        return jnp.concatenate(
+            [jnp.broadcast_to(delta[0:1], (count, S_DEV)), jnp.broadcast_to(delta[1:2], (count, S_DEV))],
+            axis=0,
+        )
+
+    pad_row = lax.broadcasted_iota(jnp.int32, (64, S_DEV), 0) % 32
+    prefix_key_stack = stack_heads(prefix_keys[...])
+    weights = jnp.exp(dot_right(prefix_key_stack, heads) * score_scale)
+    weights = jnp.where(pad_row < PREFIX, weights, 0.0)
+    slopes = (weights * (dot_right(stack_heads(prefix_values[...]), low) - head_rows(32))).astype(BF16)
+    from_prefix = dot_left(slopes, prefix_key_stack)
+    prefix_key_grad = merge_heads(dot_nn(slopes, heads)) * score_scale
+    prefix_value_grad = merge_heads(dot_nn(weights.astype(BF16), low))
+
+    @pl.when(row == 0)
+    def _():
+        prefix_grads[0] = prefix_key_grad
+        prefix_grads[1] = prefix_value_grad
+
+    @pl.when(row > 0)
+    def _():
+        prefix_grads[0] += prefix_key_grad
+        prefix_grads[1] += prefix_value_grad
+
+    key_stack = stack_heads(keys[...].reshape(memory_len, LANES))
+    value_stack = stack_heads(values[...].reshape(memory_len, LANES))
+    allowed = key_docs[0] == query_docs[0]
+    weights = jnp.exp(dot_right(key_stack, heads) * score_scale).reshape(2, memory_len, S_DEV)
+    weights = jnp.where(allowed[None], weights, 0.0).reshape(2 * memory_len, S_DEV)
+    slopes = (weights * (dot_right(value_stack, low) - head_rows(memory_len))).astype(BF16)
+    key_grad[...] = (merge_heads(dot_nn(slopes, heads)) * score_scale).astype(BF16).reshape(key_grad.shape)
+    value_grad[...] = merge_heads(dot_nn(weights.astype(BF16), low)).astype(BF16).reshape(value_grad.shape)
+    query_grad[0] = ((from_prefix + dot_left(slopes, key_stack)) * score_scale).astype(BF16)
+
+
+def cross_backward(queries, memory_pairs, query_docs, key_docs, prefix_keys, prefix_values, grad_out, crossed, inverse):
+    memory_len = 16 * M_DEV
+    head_block = pl.BlockSpec((1, S_DEV, LANES), lambda pair, row: (row, 0, pair))
+    keys = pl.BlockSpec((16, 1, M_DEV, LANES), lambda pair, row: (0, row, 0, pair))
+    values = pl.BlockSpec((16, 1, M_DEV, LANES), lambda pair, row: (0, row, 0, PAIRS + pair))
+    prefix = pl.BlockSpec((32, LANES), lambda pair, row: (0, pair))
+    terms = jax.ShapeDtypeStruct((16, 2, M_DEV, D), BF16)
+    return pl.pallas_call(
+        cross_backward_kernel,
+        grid=(PAIRS, 2),
+        out_shape=(
+            jax.ShapeDtypeStruct((2, S_DEV, D), BF16), terms, terms,
+            jax.ShapeDtypeStruct((2, 32, D), F32),
+        ),
+        in_specs=[
+            head_block, keys, values,
+            pl.BlockSpec((1, 1, S_DEV), lambda pair, row: (row, 0, 0)),
+            pl.BlockSpec((1, memory_len, LANES), lambda pair, row: (row, 0, 0)),
+            prefix, prefix, head_block, head_block, head_block,
+        ],
+        out_specs=(
+            head_block, keys, keys, pl.BlockSpec((2, 32, LANES), lambda pair, row: (0, 0, pair)),
+        ),
+        compiler_params=params(),
+        name="cross_backward",
+    )(queries, memory_pairs, memory_pairs, query_docs, key_docs, prefix_keys, prefix_values, grad_out, crossed, inverse)
+
+
+def gelu_parts(pre):
+    upper = 0.5 * (1.0 + lax.erf(pre * (0.5 ** 0.5)))
+    return upper
+
+
+def gelu_slope(pre):
+    return gelu_parts(pre) + pre * jnp.exp(-0.5 * pre * pre) * (1.0 / math.sqrt(2.0 * math.pi))
+
+
+def norm_back_rows(resid, gain, upstream):
+    middle = jnp.mean(resid, axis=-1, keepdims=True)
+    centred = resid - middle
+    scale = lax.rsqrt(jnp.mean(centred * centred, axis=-1, keepdims=True) + 1e-05)
+    unit = centred * scale
+    pulled = upstream * gain
+    return scale * (
+        pulled - jnp.mean(pulled, axis=-1, keepdims=True) - unit * jnp.mean(pulled * unit, axis=-1, keepdims=True)
+    )
+
+
+def feed_kernel(
+    normed, cotangent, gain, inner, outer, mixed,
+    layer_out, second_grad, small_grads,
+    low, pre, adapter_pre, total, feed_low,
+):
+    step = pl.program_id(0)
+    down = mixed[:, :, :ADAPTER].reshape(D, ADAPTER)
+    up_left = mixed[:, :16, ADAPTER:].reshape(ADAPTER, ADAPTER)
+    up_right = mixed[:, 16:, ADAPTER:].reshape(ADAPTER, ADAPTER)
+    half = ADAPTER
+
+    @pl.when(step == 0)
+    def _():
+        low[...] = normed[...].astype(BF16)
+        adapter_pre[...] = dot_nn(low[...], down)
+        act = adapter_pre[...]
+        act = (act * gelu_parts(act)).astype(BF16)
+        total[:, :half] = normed[:, :half] + 4.0 * dot_nn(act, up_left)
+        total[:, half:] = normed[:, half:] + 4.0 * dot_nn(act, up_right)
+
+    @pl.when(step < 4)
+    def _():
+        hidden = dot_nn(low[...], inner[...].reshape(D, D))
+        pre[jnp.minimum(step, 3)] = hidden
+        act = (hidden * gelu_parts(hidden)).astype(BF16)
+        total[...] += dot_nn(act, outer[...].reshape(D, D))
+
+    @pl.when(step == 3)
+    def _():
+        resid = total[...]
+        layer_out[...] = norm_rows(resid, gain[...]).astype(BF16)
+        third_grad = norm_back_rows(resid, gain[...], cotangent[...].astype(F32))
+        feed_low[...] = third_grad.astype(BF16)
+        adapter_low = (4.0 * third_grad).astype(BF16)
+        act = adapter_pre[...]
+        upper = gelu_parts(act)
+        slope = gelu_slope(act)
+        act = (act * upper).astype(BF16)
+        grad = dot_right(adapter_low[:, :half], up_left) + dot_right(adapter_low[:, half:], up_right)
+        grad = (slope * grad).astype(BF16)
+        second_grad[...] = third_grad + dot_right(grad, down)
+        small_grads[:, :, :half] = dot_left(low[...], grad).astype(BF16).reshape(32, 32, half)
+        small_grads[:, :16, half:] = dot_left(act, adapter_low[:, :half]).astype(BF16).reshape(32, 16, half)
+        small_grads[:, 16:, half:] = dot_left(act, adapter_low[:, half:]).astype(BF16).reshape(32, 16, half)
+
+    @pl.when(step >= 4)
+    def _():
+        hidden = pre[jnp.clip(7 - step, 0, 3)]
+        grad = dot_right(feed_low[...], outer[...].reshape(D, D))
+        grad = (gelu_slope(hidden) * grad).astype(BF16)
+        second_grad[...] += dot_right(grad, inner[...].reshape(D, D))
+
+
+def feed_forward_backward(normed, cotangent, gain, weights):
+    tokens = normed.shape[0]
+    at = lambda step: jnp.minimum(step, 7 - step)
+    still = lambda step: (0, 0)
+    rows = pl.BlockSpec((tokens, D), still)
+    return pl.pallas_call(
+        feed_kernel,
+        grid=(8,),
+        out_shape=(
+            jax.ShapeDtypeStruct((tokens, D), BF16),
+            jax.ShapeDtypeStruct((tokens, D), F32),
+            jax.ShapeDtypeStruct((32, 32, D), BF16),
+        ),
+        in_specs=[
+            rows, rows, pl.BlockSpec((1, D), still),
+            pl.BlockSpec((32, 32, D), lambda step: (0, at(step), 0)),
+            pl.BlockSpec((8, 128, D), lambda step: (at(step), 1, 0)),
+            pl.BlockSpec((32, 32, D), lambda step: (0, 8, 0)),
+        ],
+        out_specs=(rows, rows, pl.BlockSpec((32, 32, D), lambda step: (0, 0, 0))),
+        scratch_shapes=[
+            pltpu.VMEM((tokens, D), BF16),
+            pltpu.VMEM((4, tokens, D), F32),
+            pltpu.VMEM((tokens, ADAPTER), F32),
+            pltpu.VMEM((tokens, D), F32),
+            pltpu.VMEM((tokens, D), BF16),
+        ],
+        compiler_params=params(),
+        name="feed",
+    )(normed, cotangent, gain, weights, weights, weights)
+
+
+def fast_device(
+    inputs, memory, out_grad, token_docs, memory_docs, self_project, self_output, cross_query,
+    cross_memory, cross_output, inner_weight, outer_weight, adapter_down, adapter_up, norm_gains, prefixes,
+):
+    seq, x = lax.axis_index("seq"), lax.axis_index("rows")
+    tokens = 2 * S_DEV
+    mixed = jnp.concatenate(
+        [adapter_down, jnp.concatenate([adapter_up[:, :ADAPTER], adapter_up[:, ADAPTER:]], axis=0)], axis=1
+    )
+    feed_flat = jnp.concatenate(
+        [inner_weight[:, part * D:(part + 1) * D] for part in range(4)] + [outer_weight, mixed], axis=0
+    )
+    feed_weights = lax.all_gather(feed_flat, ("seq", "rows"), axis=0, tiled=True).reshape(32, FEED_ROWS, D)
+
+    small = jnp.concatenate([
+        norm_gains.reshape(-1), prefixes.reshape(-1),
+        token_docs.astype(BF16).reshape(-1), memory_docs.astype(BF16).reshape(-1),
+    ])
+    small = jnp.pad(small, (0, SMALL_ROWS * D - small.shape[0])).reshape(SMALL_ROWS, D)
+    full, memory_all = gather_first(
+        self_project, self_output, cross_query, cross_memory, cross_output, small, memory
+    )
+
+    def weight(first):
+        return full[:, first:first + 32].reshape(D, D)
+
+    flat = full[:, SMALL_AT:SMALL_AT + 5].reshape(32, 5 * D)
+    gains = flat[:, :96].reshape(32, 3, 32).transpose(1, 0, 2).reshape(3, D).astype(F32)
+    prefix_parts = flat[:, 96:3936].reshape(32, 4, PREFIX, 32)
+    cross_prefixes = prefix_parts[:, 2:].transpose(1, 2, 0, 3).reshape(2, PREFIX, D)
+    cross_prefixes = jnp.pad(cross_prefixes, ((0, 0), (0, 2), (0, 0)))
+    pair_prefixes = lax.dynamic_slice_in_dim(prefix_parts[:, :2], 4 * (seq // 2), 4, 0)
+    pair_prefixes = pair_prefixes.transpose(1, 2, 0, 3).reshape(2, PREFIX, LANES)
+    pair_prefixes = jnp.pad(pair_prefixes, ((0, 0), (0, 2), (0, 0)))
+    row_docs = lax.dynamic_index_in_dim(flat[:, 3936:4256].reshape(16, 2, 320), x, 1, False).astype(F32)
+    own_docs = lax.dynamic_index_in_dim(row_docs[:, :256].reshape(16, 2, S_DEV), seq % 2, 1, False)
+    docs_row = own_docs.reshape(1, 16 * S_DEV)
+    docs_column = jnp.broadcast_to(docs_row.reshape(-1, 1), (16 * S_DEV, LANES))
+    memory_row = row_docs[:, 256:].reshape(16, 2, M_DEV).transpose(1, 0, 2).reshape(2, 1, 16 * M_DEV)
+    memory_column = jnp.broadcast_to(memory_row.reshape(2, -1, 1), (2, 16 * M_DEV, LANES))
+    query_row = token_docs.astype(F32).reshape(2, 1, S_DEV)
+    query_column = jnp.broadcast_to(query_row.reshape(2, S_DEV, 1), (2, S_DEV, 16 * M_DEV))
+
+    arrived = project_exchange(inputs, full)
+    attended, pair_attended, pair_inverse = self_forward(
+        arrived, docs_row, docs_column, pair_prefixes[0], pair_prefixes[1]
+    )
+    memory_pairs = jnp.concatenate(
+        [jnp.dot(memory_all.reshape(-1, D), weight(at), preferred_element_type=F32) for at in (MEM_K_AT, MEM_V_AT)],
+        axis=1,
+    ).astype(BF16).reshape(16, 2, M_DEV, 2 * D)
+
+    first_resid = inputs.reshape(tokens, D).astype(F32) + jnp.dot(
+        attended.reshape(tokens, D), weight(SELF_OUT_AT), preferred_element_type=F32
+    )
+    first_norm = norm_rows(first_resid, gains[0])
+    cross_queries = jnp.dot(
+        first_norm.astype(BF16), weight(CROSS_Q_AT), preferred_element_type=F32
+    ).astype(BF16).reshape(2, S_DEV, D)
+    crossed, cross_inverse = cross_forward(
+        cross_queries, memory_pairs, query_column, memory_row, cross_prefixes[0], cross_prefixes[1]
+    )
+    second_resid = first_norm + jnp.dot(
+        crossed.reshape(tokens, D).astype(BF16), weight(CROSS_OUT_AT), preferred_element_type=F32
+    )
+    second_norm = norm_rows(second_resid, gains[1])
+
+    layer_out, second_grad, small_grads = feed_forward_backward(
+        second_norm, out_grad.reshape(tokens, D), gains[2:3], feed_weights
+    )
+    small_sums = lax.psum_scatter(small_grads.reshape(1024, D), "seq", scatter_dimension=0, tiled=True)
+
+    second_resid_grad = norm_back_rows(second_resid, gains[1], second_grad)
+    cross_out_grad = dot_right(second_resid_grad.astype(BF16), weight(CROSS_OUT_AT))
+    cross_query_grad, key_terms, value_terms, cross_prefix_grads = cross_backward(
+        cross_queries, memory_pairs, query_row, memory_column, cross_prefixes[0], cross_prefixes[1],
+        cross_out_grad.reshape(2, S_DEV, D), crossed, cross_inverse,
+    )
+    memory_terms = dot_right(key_terms.reshape(-1, D), weight(MEM_K_AT)) + dot_right(
+        value_terms.reshape(-1, D), weight(MEM_V_AT)
+    )
+    prefix_flat = cross_prefix_grads[:, :PREFIX].reshape(2 * PREFIX, 16, 64).transpose(1, 0, 2).reshape(16, -1)
+    prefix_flat = jnp.pad(prefix_flat, ((0, 0), (0, 8 * D - prefix_flat.shape[1]))).reshape(16, 8, D)
+    memory_terms = jnp.concatenate(
+        [memory_terms.astype(BF16).reshape(16, 64, D), prefix_flat.astype(BF16)], axis=1
+    )
+    memory_sums = lax.psum_scatter(memory_terms, "seq", scatter_dimension=0, tiled=False)
+
+    first_grad = second_resid_grad + dot_right(cross_query_grad.reshape(tokens, D), weight(CROSS_Q_AT))
+    first_resid_grad = norm_back_rows(first_resid, gains[0], first_grad)
+    self_out_grad = dot_right(first_resid_grad.astype(BF16), weight(SELF_OUT_AT))
+    project_grads, self_prefix_grads = self_backward(
+        arrived, self_out_grad.astype(BF16).reshape(2, S_DEV, D), pair_attended, pair_inverse,
+        docs_row, docs_column, pair_prefixes[0], pair_prefixes[1],
+    )
+    project_grads = project_grads.transpose(2, 1, 3, 0, 4).reshape(3, tokens, D)
+    input_grad = first_resid_grad
+    for part in range(3):
+        input_grad = input_grad + dot_right(project_grads[part], weight(32 * part))
+
+    def swapped(values):
+        return lax.ppermute(values, "rows", [(0, 1), (1, 0)])
+
+    halves = small_sums.astype(F32).reshape(2, 32, D)
+    give = lax.dynamic_index_in_dim(halves, 1 - x, 0, False)
+    keep = lax.dynamic_index_in_dim(halves, x, 0, False)
+    prefix_half = memory_sums[64:].astype(F32).reshape(-1)[:60 * 64].reshape(60, 2, 32)
+    cross_give = lax.dynamic_index_in_dim(prefix_half, 1 - x, 1, False)
+    cross_keep = lax.dynamic_index_in_dim(prefix_half, x, 1, False)
+    pair_sum = self_prefix_grads + lax.ppermute(
+        self_prefix_grads, "seq", [(at, at ^ 1) for at in range(16)]
+    )
+    pair_sum = pair_sum[:, :PREFIX].reshape(60, 2, 2, 32)
+    pair_sum = lax.dynamic_index_in_dim(pair_sum, seq % 2, 1, False)
+    self_give = lax.dynamic_index_in_dim(pair_sum, 1 - x, 1, False)
+    self_keep = lax.dynamic_index_in_dim(pair_sum, x, 1, False)
+    keep = keep + swapped(give)
+    prefix_grad = jnp.concatenate([self_keep, cross_keep], axis=0) + swapped(
+        jnp.concatenate([self_give, cross_give], axis=0)
+    )
+    return (
+        layer_out.reshape(2, S_DEV, D),
+        input_grad.reshape(2, S_DEV, D),
+        memory_sums[:64].astype(F32).reshape(2, M_DEV, D),
+        prefix_grad.reshape(4, PREFIX, 32),
+        keep[:, :ADAPTER],
+        jnp.concatenate([keep[:16, ADAPTER:], keep[16:, ADAPTER:]], axis=1),
+    )
+
+
 def solution(mesh):
     placed = (
         P("rows", "seq", None),
@@ -602,8 +1422,9 @@
         P(None, ("seq", "rows")),
         P(None, None, ("seq", "rows")),
     )
+    small_slice = mesh.shape["seq"] == 16 and mesh.shape["rows"] == 2
     return jax.shard_map(
-        per_device,
+        fast_device if small_slice else per_device,
         mesh=mesh,
         in_specs=placed,
         out_specs=(

time: 1680 us -> 483 us (0.29)
  waiting for transfers between devices: 1010 us -> 3.74 us
  Pallas kernels: 0 us -> 373 us
  matrix products: 255 us -> 25.4 us
  blocking collectives: 175 us -> 0 us
  local copies, waits for them, and re-layouts: 183 us -> 46.9 us
    all_gather x13 -> x1, waiting for transfers between devices: 483 us -> 0.01 us  [fast_device(): lax.all_gather(feed_flat, ('seq', 'rows'), axis=0, tiled=True)]
    reduce_scatter x4 -> x2, waiting for transfers between devices: 473 us -> 0.02 us  [the longest x1 0.02 us: fast_device(): lax.psum_scatter(memory_terms, 'seq', scatter_dimension=0, tiled=False)]
    pallas_call x0 -> x7, Pallas kernels: none -> 373 us  [the longest x1 154 us: gather_first(): pl.pallas_call(gather_kernel, out_shape=(jax.ShapeDtypeStruct((4, 2, 2, 2...]
    dot_general x114 -> x5, matrix products: 195 us -> 9.51 us  [the longest x2 4.71 us: fast_device(): jnp.dot(memory_all.reshape(-1, D), weight(at), preferred_element_type=F32)]
    all_gather x4 -> x0, blocking collectives: 175 us -> none  [the longest x1 69.2 us: fetch_all(): lax.all_gather(prefixes, ('seq', 'rows'), axis=2, tiled=True)]
    unnamed x23 -> x3, waiting for transfers between devices: 52 us -> 0.05 us
    dot_general x16 -> x8, matrix products: 59.7 us -> 15.9 us  [dot_right(): lax.dot_general(left, right, (((1,), (1,)), ((), ())), preferred_element_...]
    unnamed x304 -> x53, local copies, waits for them, and re-layouts: 53.7 us -> 14.6 us
  transfers between devices with their start and end apart: 20 -> 6, of which waited for: 14 -> 1; matrix products, arithmetic and copies ran while one was open for 20% -> 14% of each run, Pallas kernels for 0% -> 73%
where the time goes in v1:
time: 483 us; the launch traced here: 480 us
  Pallas kernels  373 us (77%)
  local copies, waits for them, and re-layouts  46.9 us (10%)
  matrix products  25.4 us (5%)
  between operations  14.4 us (3%)
  other arithmetic  13.6 us (3%)
    pallas_call x1, Pallas kernels, gather_first(): pl.pallas_call(gather_kernel, out_shape=(jax.ShapeDtypeStruct((4, 2, 2, 2...  154 us
    pallas_call x1, Pallas kernels, self_backward(): pl.pallas_call(self_backward_kernel, out_shape=(jax.ShapeDtypeStruct((PAI...  80.8 us
    pallas_call x1, Pallas kernels, project_exchange(): pl.pallas_call(project_kernel, out_shape=jax.ShapeDtypeStruct((16, 3, S_D...  46 us
    pallas_call x1, Pallas kernels, self_forward(): pl.pallas_call(self_forward_kernel, out_shape=(jax.ShapeDtypeStruct((2, S...  35.1 us
    pallas_call x1, Pallas kernels, feed_forward_backward(): pl.pallas_call(feed_kernel, grid=(8,), out_shape=(jax.ShapeDtypeStruct((t...  22.8 us
    pallas_call x1, Pallas kernels, cross_backward(): pl.pallas_call(cross_backward_kernel, grid=(PAIRS, 2), out_shape=(jax.Sha...  21 us
    dot_general x8, matrix products, dot_right(): lax.dot_general(left, right, (((1,), (1,)), ((), ())), preferred_element_...  15.9 us
    unnamed x53, local copies, waits for them, and re-layouts  14.6 us
  transfers between devices with their start and end apart: 6, of which 1 were waited for; matrix products, arithmetic and copies ran while one was open for 14% of the time, Pallas kernels for 73%

profile of v1, /device:TPU:28, one launch (start us, length us, event | category | flops | bytes accessed | tf_op | source)
XLA Modules:
  0.0 480.2 jit_solution(11905305331372175297)
XLA Ops:
  8.0 0.8 slice_dynamic-update-slice_fusion.3
  8.8 0.8 slice_dynamic-update-slice_fusion.2
  9.6 0.8 slice_dynamic-update-slice_fusion.1
  10.5 0.8 slice_dynamic-update-slice_fusion
  11.3 1.0 constant_dynamic-update-slice_fusion
  13.1 0.8 copy-done.16
  17.9 153.9 %gather_first.1 = (bf16[4,2,2,2,272,1024]{5,4,3,2,1,0:T(8,128)(2,1)}, bf16[4,2,2,2,32,1024]{5,4,3,2,1,0:T(8,128)(2,1)}) custom-call(bf16[32,3072]{1,0:T(8,128)(2,1)} %project.1, bf16[32,1024]{1,0:T(8,128)(2,1)} %self_out.1, bf16[32,1024]{1,0:T(8,128)(2,1)} %cross_q.1, bf16[32,2048]{1,0:T(8,128)(2,1)} %cross_mem.1, bf16[32,1024]{1,0:T(8,128)(2,1)} %cross_out.1, ...), custom_call_target="tpu_custom_call" | custom-call | tf_op jit(solution)/shard_map/gather_first/pallas_call | solution.py:718
  171.8 1.1 slice.188
  173.4 1.2 reshape.252
  174.9 46.0 %project_exchange.1.arrived = bf16[16,3,128,128]{3,2,1,0:T(8,128)(2,1)} custom-call(bf16[2,128,1024]{2,1,0:T(8,128)(2,1)} %tokens.1, bf16[32,272,1024]{2,1,0:T(8,128)(2,1)} %bitcast.123), custom_call_target="tpu_custom_call" | custom-call | tf_op jit(solution)/shard_map/project_exchange/pallas_call | solution.py:767
  224.2 1.3 broadcast_in_dim.11.docs_column
  225.5 35.1 %self_forward.1 = (bf16[2,128,1024]{2,1,0:T(8,128)(2,1)}, f32[2048,128]{1,0:T(8,128)}, f32[2048,128]{1,0:T(8,128)}) custom-call(bf16[16,3,128,128]{3,2,1,0:T(8,128)(2,1)} %project_exchange.1.arrived, f32[1,2048]{1,0:T(1,128)} %fusion.51.docs_row, f32[2048,128]{1,0:T(8,128)} %broadcast_in_dim.11.docs_column, bf16[32,128]{1,0:T(8,128)(2,1)} %get-tuple-element.83.prefix_keys, ...), custom_call_target="tpu_custom_call" | custom-call | tf_op jit(solution)/shard_map/self_forward/pallas_call | solution.py:879
  261.2 10.3 %fusion.21 = (bf16[32,32,1024]{2,1,0:T(8,128)(2,1)}, bf16[32,32,1024]{2,1,0:T(8,128)(2,1)}, bf16[32,32,1024]{2,1,0:T(8,128)(2,1)}, bf16[32,32,1024]{2,1,0:T(8,12...) fusion(bf16[32,272,1024]{2,1,0:T(8,128)(2,1)} %bitcast.124), kind=kLoop, calls=%fused_computation.84 | loop fusion | bytes 33554432 | tf_op jit(solution)/shard_map/slice | solution.py:1300
  273.5 1.6 convolution_convert_fusion.3
  275.1 1.0 copy-done.20
  276.1 2.4 convolution_convert_fusion.1
  278.4 2.4 convolution_convert_fusion
  280.8 2.5 pad_maximum_fusion.keys.values
  283.3 0.9 broadcast_in_dim.12.query_docs
  284.2 13.1 %cross_forward.1 = (f32[2,128,1024]{2,1,0:T(8,128)}, f32[2,128,1024]{2,1,0:T(8,128)}) custom-call(bf16[2,128,1024]{2,1,0:T(8,128)(2,1)} %bitcast.139, bf16[16,2,32,2048]{3,2,1,0:T(8,128)(2,1)} %pad_maximum_fusion.keys.values, bf16[16,2,32,2048]{3,2,1,0:T(8,128)(2,1)} %pad_maximum_fusion.keys.values, f32[2,128,512]{2,1,0:T(8,128)} %broadcast_in_dim.12.query_docs, ...), custom_call_target="tpu_custom_call" | custom-call | tf_op jit(solution)/shard_map/cross_forward/pallas_call | solution.py:1080
  297.3 1.3 convert_element_type.95
  299.4 2.4 fusion.27
  302.1 1.2 fusion.1.normed
  303.3 22.8 %feed.1 = (bf16[256,1024]{1,0:T(8,128)(2,1)}, f32[256,1024]{1,0:T(8,128)}, bf16[32,32,1024]{2,1,0:T(8,128)(2,1)}) custom-call(f32[256,1024]{1,0:T(8,128)} %fusion.1.normed, bf16[256,1024]{1,0:T(8,128)(2,1)} %bitcast.157, f32[1,1024]{1,0:T(1,128)} %slice.166.gain, bf16[32,288,1024]{2,1,0:T(8,128)(2,1)} %bitcast.119, bf16[32,288,1024]{2,1,0:T(8,128)(2,1)} %bitcast.120, ...), custom_call_target="tpu_custom_call" | custom-call | tf_op jit(solution)/shard_map/feed/pallas_call | solution.py:1249
  326.3 1.1 copy-done.8
  327.7 1.3 fusion.20
  329.6 1.8 fusion.28.grad_out
  331.4 1.0 broadcast_in_dim.14.key_docs
  332.4 21.0 %cross_backward.1 = (bf16[2,128,1024]{2,1,0:T(8,128)(2,1)}, bf16[16,2,32,1024]{3,2,1,0:T(8,128)(2,1)}, bf16[16,2,32,1024]{3,2,1,0:T(8,128)(2,1)}, f32[2,32,1024]{2,1,0:T(8,128)}) custom-call(bf16[2,128,1024]{2,1,0:T(8,128)(2,1)} %bitcast.140, bf16[16,2,32,2048]{3,2,1,0:T(8,128)(2,1)} %pad_maximum_fusion.keys.values, ...), custom_call_target="tpu_custom_call" | custom-call | tf_op jit(solution)/shard_map/cross_backward/pallas_call | solution.py:1150
  353.4 1.1 slice.245
  354.5 0.9 reshape.277
  355.4 1.0 copy.49
  356.9 4.1 fusion.29
  361.1 2.4 add_convert_fusion
  363.5 1.7 pad_maximum_fusion.1
  365.2 1.6 copy-done.7
  366.8 2.5 fusion.19
  369.3 1.7 convolution_convert_fusion.2
  371.0 80.8 %self_backward.1 = (bf16[8,2,3,128,128]{4,3,2,1,0:T(8,128)(2,1)}, f32[2,32,128]{2,1,0:T(8,128)}) custom-call(bf16[16,3,128,128]{3,2,1,0:T(8,128)(2,1)} %project_exchange.1.arrived, bf16[2,128,1024]{2,1,0:T(8,128)(2,1)} %bitcast.159, f32[2048,128]{1,0:T(8,128)} %get-tuple-element.30.attended, f32[2048,128]{1,0:T(8,128)} %get-tuple-element.31.inverse, ...), custom_call_target="tpu_custom_call" | custom-call | tf_op jit(solution)/shard_map/self_backward/pallas_call | solution.py:1030
  452.3 1.5 fusion.22
  455.8 0.9 convolution_add_fusion.2
  458.1 0.8 copy-done.3
  459.0 1.7 convolution_add_fusion
  460.7 0.9 convert.26
  461.6 1.5 collective-permute-start.2
  463.5 3.7 collective-permute-done.2
  468.3 1.5 collective-permute-start.1
  471.2 0.9 slice.211
  (130 shorter events, 22.9 us)
Async XLA Ops:
  7.2 296.1 %all-gather.2.cloned.1.call-start = ((), (), s32[]{:S(2)}) async-start(), calls=%async_computation.2 | async-start | bytes 19464192 | tf_op jit(solution)/shard_map/all_gather | solution.py:1288
  13.1 0.8 copy-start.16
  13.9 446.7 %reduce-scatter.5.cloned.1.call-start = ((), (), s32[]{:S(2)}) async-start(), calls=%async_computation.4 | async-start | bytes 2228224 | tf_op jit(solution)/shard_map/reduce_scatter | solution.py:1346
  17.2 266.1 %copy-start.19 = (f32[2,128]{1,0:T(2,128)}, f32[2,128]{1,0:T(2,128)S(1)}, u32[]{:S(2)}) copy-start(f32[2,128]{1,0:T(2,128)S(1)} %get-tuple-element.84) | copy-start | bytes 3076
  261.2 10.3 %copy-start.15 = (bf16[2,128,1024]{2,1,0:T(8,128)(2,1)S(1)}, bf16[2,128,1024]{2,1,0:T(8,128)(2,1)}, u32[]{:S(2)}) copy-start(bf16[2,128,1024]{2,1,0:T(8,128)(2,1)} %tokens.1) | copy-start | bytes 1572868
  261.2 10.3 %copy-start.17 = (bf16[2,128,1024]{2,1,0:T(8,128)(2,1)S(1)}, bf16[2,128,1024]{2,1,0:T(8,128)(2,1)}, u32[]{:S(2)}) copy-start(bf16[2,128,1024]{2,1,0:T(8,128)(2,1)} %get-tuple-element.23) | copy-start | bytes 1572868
  271.5 1.4 copy-start.1
  271.5 2.0 copy-start.6
  271.5 3.5 copy-start.13
  271.6 6.9 %copy-start.11 = (bf16[32,32,1024]{2,1,0:T(8,128)(2,1)}, bf16[32,32,1024]{2,1,0:T(8,128)(2,1)S(1)}, u32[]{:S(2)}) copy-start(bf16[32,32,1024]{2,1,0:T(8,128)(2,1)S(1)} %get-tuple-element.63) | copy-start | bytes 6291460
  273.2 2.9 copy-start.20
  326.1 1.2 copy-start.8
  326.1 141.1 %reduce-scatter.3.cloned.1.call-start = ((), (), s32[]{:S(2)}) async-start(), calls=%async_computation.3 | async-start | bytes 2506752 | tf_op jit(solution)/shard_map/reduce_scatter | solution.py:1362
  327.7 2.0 copy-start
  353.4 3.5 copy-start.14
  356.9 4.1 copy-start.12
  356.9 4.1 copy-start.21
  365.1 1.6 copy-start.7
  366.8 2.5 copy-start.2
  369.3 1.8 copy-start.9
  451.8 11.3 %collective-permute-start = (f32[2,32,128]{2,1,0:T(8,128)}, f32[2,32,128]{2,1,0:T(8,128)S(1)}, u32[]{:S(2)}, u32[]{:S(2)}) collective-permute-start(f32[2,32,128]{2,1,0:T(8,128)} %get-tuple-element.36), channel_id=1, source_target_pairs={{0,2},{2,0},{4,6},{6,4},{8,10},{10,8},{12,14},{14,12},{16,18},{18,... | collective-permute-start | bytes 98312 | tf_op jit(solution)/shard_map/ppermute | solution.py:1385
  453.9 1.6 copy-start.5
  453.9 1.9 copy-start.10
  455.7 1.6 copy-start.4
  457.4 1.6 copy-start.3
  459.0 4.1 copy-start.18
  461.6 5.5 %collective-permute-start.2 = (f32[32,1024]{1,0:T(8,128)S(1)}, f32[32,1024]{1,0:T(8,128)S(1)}, u32[]{:S(2)}, u32[]{:S(2)}) collective-permute-start(f32[32,1024]{1,0:T(8,128)S(1)} %dynamic-slice_bitcast_fusion), channel_id=1, source_target_pairs={{0,1},{1,0},{2,3},{3,2},{4,5},{5,4},{6,7},{7,6},{8,9},{9,8},{10,11... | collective-permute-start | bytes 393224 | tf_op jit(solution)/shard_map/ppermute | solution.py:1377
  468.3 4.5 collective-permute-start.1
Sparse Core Ops, SparseCore 0:
  14.1 195.8 all-gather.1
  326.3 65.8 reduce-scatter.4
  396.4 68.0 reduce-scatter.2

commit v2 on v1

--- a/solution.py
+++ b/solution.py
@@ -595,10 +595,17 @@
 VMEM_BYTES = 60 * 1024 * 1024
 PAIRS = HEADS // 2
 LANES = 2 * HEAD_DIM
-Q_AT, K_AT, V_AT, SELF_OUT_AT, CROSS_Q_AT, MEM_K_AT, MEM_V_AT, CROSS_OUT_AT, SMALL_AT = range(0, 288, 32)
-SMALL_ROWS = 16
-FIRST_ROWS = SMALL_AT + SMALL_ROWS
-FEED_ROWS = 288
+Q_AT, K_AT, V_AT, SELF_OUT_AT, CROSS_Q_AT, MEM_K_AT, MEM_V_AT, CROSS_OUT_AT = range(0, 256, 32)
+INNER_AT, OUTER_AT, MIXED_AT = 256, 384, 512
+ALL_ROWS = 544
+SMALL_ROWS = 144
+PIECE_ROWS = 16
+GAP = 2
+LEAD = 4
+SENDS = 2
+Z_LAST = ()
+WAIT_TICKS = 4
+STEP_TICKS = 2
 
 
 def whole(space=pltpu.VMEM):
@@ -631,155 +638,133 @@
     return lax.dot_general(left, right, (((1,), (0,)), ((), ())), preferred_element_type=F32)
 
 
-def gather_kernel(
-    project, self_out, cross_q, cross_mem, cross_out, small, memory,
-    full, memory_full, local_sem, *sems,
-):
-    seq, x = lax.axis_index("seq"), lax.axis_index("rows")
-    z, y, core = seq // 4, (seq // 2) % 2, seq % 2
-
-    def device(z, y, core, x):
+class Place:
+    def __init__(self):
+        self.seq, self.x = lax.axis_index("seq"), lax.axis_index("rows")
+        self.z, self.y, self.core = self.seq // 4, (self.seq // 2) % 2, self.seq % 2
+        self.pair, self.row = self.seq // 2, self.seq % 2
+
+    def device(self, z, y, core, x):
         return ((z * 2 + y) * 2 + core, x)
 
-    along_z = [device((z + step) % 4, y, core, x) for step in (1, 2, 3)]
-    along_x, along_y = device(z, y, core, 1 - x), device(z, 1 - y, core, x)
-    other_core = device(z, y, 1 - core, x)
-    greet(along_z + [along_x, along_y, other_core])
-    send0, recv0, send1, recv1, send2, recv2, send3, recv3 = sems
-
-    pieces = [
-        (project.at[:, pl.ds(0, 1024)], Q_AT, 32),
-        (project.at[:, pl.ds(1024, 1024)], K_AT, 32),
-        (project.at[:, pl.ds(2048, 1024)], V_AT, 32),
-        (small, SMALL_AT, SMALL_ROWS),
-        (self_out, SELF_OUT_AT, 32),
-        (cross_q, CROSS_Q_AT, 32),
-        (cross_mem.at[:, pl.ds(0, 1024)], MEM_K_AT, 32),
-        (cross_mem.at[:, pl.ds(1024, 1024)], MEM_V_AT, 32),
-        (cross_out, CROSS_OUT_AT, 32),
-    ]
-    stages = []
-    for k, (source, first, count) in enumerate(pieces):
+    def along_z(self, step):
+        return self.device((self.z + step) % 4, self.y, self.core, self.x)
+
+    def along_y(self):
+        return self.device(self.z, 1 - self.y, self.core, self.x)
+
+    def along_x(self):
+        return self.device(self.z, self.y, self.core, 1 - self.x)
+
+    def other_core(self):
+        return self.device(self.z, self.y, 1 - self.core, self.x)
+
+    def diagonal(self):
+        return self.device(self.z, self.y, 1 - self.core, 1 - self.x)
+
+    def others(self):
+        return [((self.seq + step) % 16, self.x) for step in range(1, 16)]
+
+
+class Gather:
+    def __init__(self, place, full, local_sem, sems, gap):
+        self.place, self.full, self.local_sem, self.sems, self.gap = place, full, local_sem, sems, gap
+        self.stages = []
+        self.waiting = []
+        self.tick_at = 0
+
+    def copies(self, level, source, target, device, slot):
+        k = len(self.stages)
+        return remote(source, target, self.sems[2 * level].at[k, slot], self.sems[2 * level + 1].at[k, slot], device)
+
+    def add(self, source, first, count, piece=PIECE_ROWS):
+        for from_row in range(0, count, piece):
+            self.add_piece(source.at[pl.ds(from_row, piece)], first + from_row, piece)
+        return len(self.stages) - 1
+
+    def add_piece(self, source, first, count):
+        at, full = self.place, self.full
+        z, y, core, x = at.z, at.y, at.core, at.x
         rows = pl.ds(first, count)
         mine = full.at[z, y, core, x, rows]
-        near, far = pl.ds(0, 2), pl.ds(2, 2)
+        k = len(self.stages)
+        if k in Z_LAST:
+            plane = full.at[z, :, core, :, rows]
+            first_way, then_way = (at.along_x(), at.along_y()) if k % 2 else (at.along_y(), at.along_x())
+            line = full.at[z, y, core, :, rows] if k % 2 else full.at[z, :, core, x, rows]
+            self.stages.append((
+                pltpu.make_async_copy(source, mine, self.local_sem.at[k]),
+                [self.copies(0, source, mine, first_way, 0)],
+                [self.copies(1, line, line, then_way, 0)],
+                [self.copies(2, plane, plane, at.along_z(d + 1), d) for d in range(3)],
+                [self.copies(3, full.at[:, :, core, :, rows], full.at[:, :, core, :, rows], at.other_core(), 0)],
+            ))
+            return
+        cut = 2 if k % 3 == 0 else 1
+        near, far = pl.ds(0, cut), pl.ds(cut, 4 - cut)
         near1, far1 = full.at[near, y, core, x, rows], full.at[far, y, core, x, rows]
         near2, far2 = full.at[near, y, core, :, rows], full.at[far, :, core, x, rows]
         half = full.at[:, :, core, :, rows]
-        stages.append((
-            pltpu.make_async_copy(source, mine, local_sem.at[k]),
-            [remote(source, mine, send0.at[k, d], recv0.at[k, d], along_z[d]) for d in range(3)],
-            [remote(near1, near1, send1.at[k, 0], recv1.at[k, 0], along_x),
-             remote(far1, far1, send1.at[k, 1], recv1.at[k, 1], along_y)],
-            [remote(near2, near2, send2.at[k, 0], recv2.at[k, 0], along_y),
-             remote(far2, far2, send2.at[k, 1], recv2.at[k, 1], along_x)],
-            [remote(half, half, send3.at[k, 0], recv3.at[k, 0], other_core)],
+        self.stages.append((
+            pltpu.make_async_copy(source, mine, self.local_sem.at[len(self.stages)]),
+            [self.copies(0, source, mine, at.along_z(d + 1), d) for d in range(3)],
+            [self.copies(1, near1, near1, at.along_x(), 0), self.copies(1, far1, far1, at.along_y(), 1)],
+            [self.copies(2, near2, near2, at.along_y(), 0), self.copies(2, far2, far2, at.along_x(), 1)],
+            [self.copies(3, half, half, at.other_core(), 0)],
         ))
-    k = len(pieces)
-    mine = memory_full.at[z, y, core]
-    column = memory_full.at[:, y, core]
-    half = memory_full.at[:, :, core]
-    stages.append((
-        pltpu.make_async_copy(memory, mine, local_sem.at[k]),
-        [remote(memory, mine, send0.at[k, d], recv0.at[k, d], along_z[d]) for d in range(3)],
-        [remote(column, column, send1.at[k, 1], recv1.at[k, 1], along_y)],
-        [],
-        [remote(half, half, send3.at[k, 0], recv3.at[k, 0], other_core)],
-    ))
-    order = list(range(4)) + [k] + list(range(4, k))
-    stages = [stages[at] for at in order]
-    for local, *_ in stages:
-        local.start()
-    total = len(stages)
-    for tick in range(total + 4):
-        for level in range(5):
-            k = tick - level
-            if not 0 <= k < total:
-                continue
-            if level == 1:
-                stages[k][0].wait()
-            if level > 0:
-                for copy in stages[k][level]:
-                    copy.wait_recv()
-            if level < 4:
-                for copy in stages[k][level + 1]:
-                    copy.start()
-    for _, *levels in stages:
-        for level in levels:
-            for copy in level:
-                copy.wait_send()
-
-
-def gather_first(project, self_out, cross_q, cross_mem, cross_out, small, memory):
-    count = 10
-    sems = []
-    for width in (3, 2, 2, 1):
-        sems += [pltpu.SemaphoreType.DMA((count, width))] * 2
-    full, memory_full = pl.pallas_call(
-        gather_kernel,
-        out_shape=(
-            jax.ShapeDtypeStruct((4, 2, 2, 2, FIRST_ROWS, D), BF16),
-            jax.ShapeDtypeStruct((4, 2, 2) + memory.shape, BF16),
-        ),
-        in_specs=[whole(pl.ANY)] * 7,
-        out_specs=(whole(pl.ANY), whole(pl.ANY)),
-        scratch_shapes=[pltpu.SemaphoreType.DMA((count,))] + sems,
-        compiler_params=params(0),
-        name="gather_first",
-    )(project, self_out, cross_q, cross_mem, cross_out, small, memory)
-    return full.reshape(32, FIRST_ROWS, D), memory_full.reshape((16,) + memory.shape)
-
-
-def project_kernel(tokens, full, arrived, weights, staged, weight_sem, local_sem, send_sem, recv_sem):
-    seq, x = lax.axis_index("seq"), lax.axis_index("rows")
-    fetches = [
-        pltpu.make_async_copy(full.at[:, pl.ds(32 * part, 32)], weights.at[part], weight_sem.at[part])
-        for part in range(3)
-    ]
-    for fetch in fetches:
-        fetch.start()
-    greet([((seq + step) % 16, x) for step in range(1, 16)])
-    rows = tokens[...].reshape(2 * S_DEV, D)
-    for part in range(3):
-        fetches[part].wait()
-        result = dot_nn(rows, weights[part].reshape(D, D)).astype(BF16)
+
+    def add_memory(self, source, full):
         for row in range(2):
-            for pair in range(PAIRS):
-                staged[pair, row, part] = result[
-                    row * S_DEV:(row + 1) * S_DEV, pair * LANES:(pair + 1) * LANES
-                ]
-    copies = []
-    for step in range(1, 16):
-        to = (seq + step) % 16
-        copies.append(remote(
-            staged.at[to // 2, to % 2], arrived.at[seq], send_sem.at[step], recv_sem.at[step], (to, x)
+            self.add_memory_row(source.at[row], full.at[:, :, :, row])
+        return len(self.stages) - 1
+
+    def add_memory_row(self, source, full):
+        at = self.place
+        mine, column, half = full.at[at.z, at.y, at.core], full.at[:, at.y, at.core], full.at[:, :, at.core]
+        self.stages.append((
+            pltpu.make_async_copy(source, mine, self.local_sem.at[len(self.stages)]),
+            [self.copies(0, source, mine, at.along_z(d + 1), d) for d in range(3)],
+            [self.copies(1, column, column, at.along_y(), 1)],
+            [],
+            [self.copies(3, half, half, at.other_core(), 0)],
         ))
-    own = pltpu.make_async_copy(staged.at[seq // 2, seq % 2], arrived.at[seq], local_sem)
-    own.start()
-    for copy in copies:
-        copy.start()
-    own.wait()
-    for copy in copies:
-        copy.wait()
-
-
-def project_exchange(tokens, full):
-    return pl.pallas_call(
-        project_kernel,
-        out_shape=jax.ShapeDtypeStruct((16, 3, S_DEV, LANES), BF16),
-        in_specs=[whole(), whole(pl.ANY)],
-        out_specs=whole(pl.ANY),
-        scratch_shapes=[
-            pltpu.VMEM((3, 32, 32, D), BF16),
-            pltpu.VMEM((PAIRS, 2, 3, S_DEV, LANES), BF16),
-            pltpu.SemaphoreType.DMA((3,)),
-            pltpu.SemaphoreType.DMA,
-            pltpu.SemaphoreType.DMA((16,)),
-            pltpu.SemaphoreType.DMA((16,)),
-        ],
-        compiler_params=params(1),
-        name="project_exchange",
-    )(tokens, full)
+
+    def start(self):
+        for stage in self.stages:
+            stage[0].start()
+
+    def tick(self, count=1):
+        for _ in range(count):
+            for level in range(5):
+                k = self.tick_at - self.after(level)
+                if not 0 <= k < len(self.stages):
+                    continue
+                if level == 1:
+                    self.stages[k][0].wait()
+                if level > 0:
+                    for copy in self.stages[k][level]:
+                        copy.wait_recv()
+                if level < 4:
+                    for copy in self.stages[k][level + 1]:
+                        copy.start()
+            self.tick_at += 1
+            for _ in range(SENDS):
+                if self.waiting:
+                    self.waiting.pop(0).start()
+
+    def after(self, level):
+        return 0 if level == 0 else LEAD + (level - 1) * self.gap
+
+    def until(self, k):
+        while self.tick_at <= k + self.after(4):
+            self.tick()
+
+    def finish(self):
+        self.until(len(self.stages) - 1)
+        for _, *levels in self.stages:
+            for level in levels:
+                for copy in level:
+                    copy.wait_send()
 
 
 def head_masks():
@@ -809,42 +794,155 @@
     )
 
 
-def self_forward_kernel(
-    arrived, docs_row, docs_column, prefix_keys, prefix_values,
-    gathered, attended, inverse, staged, sums, parts, local_sem, send_sem, recv_sem,
+def first_kernel(
+    tokens, memory, small, docs,
+    project, self_out, cross_q, cross_mem, cross_out, inner, outer, mixed,
+    full, memory_full, memory_pairs, small_full, docs_all, docs_row, docs_column, arrived, attended, inverse,
+    first_resid, cross_queries, crossed, cross_inverse, second_resid, second_norm,
+    gathered, first_norm, weights, staged, quad, memory_held, result_staged, sums, parts,
+    local_sem, send0, recv0, send1, recv1, send2, recv2, send3, recv3,
+    fetch_sem, own_sem, quad_send, quad_recv, small_send, small_recv, docs_send, docs_recv,
+    head_send, head_recv, out_send, out_recv,
 ):
-    seq, x = lax.axis_index("seq"), lax.axis_index("rows")
+    place = Place()
+    seq, x, pair, row = place.seq, place.x, place.pair, place.row
+    others = place.others()
+    quad_peers = [place.other_core(), place.along_x(), place.diagonal()]
+    greet(others + quad_peers[1:])
+
+    engine = Gather(place, full, local_sem, (send0, recv0, send1, recv1, send2, recv2, send3, recv3), GAP)
+    project_done = [
+        engine.add(project.at[:, pl.ds(part * D, D)], at, 32) for part, at in enumerate((Q_AT, K_AT, V_AT))
+    ]
+    engine.add_memory(memory, memory_full)
+    for part, at in enumerate((MEM_K_AT, MEM_V_AT)):
+        memory_done = engine.add(cross_mem.at[:, pl.ds(part * D, D)], at, 32)
+    out_done = engine.add(self_out, SELF_OUT_AT, 32)
+    query_done = engine.add(cross_q, CROSS_Q_AT, 32)
+    cross_done = engine.add(cross_out, CROSS_OUT_AT, 32)
+    for part in range(4):
+        engine.add(inner.at[:, pl.ds(part * D, D)], INNER_AT + 32 * part, 32)
+    for part in range(4):
+        engine.add(outer.at[pl.ds(32 * part, 32)], OUTER_AT + 32 * part, 32)
+    engine.add(mixed, MIXED_AT, 32)
+    engine.start()
+    engine.tick()
+
+    mine = place.core * 2 + x
+    quad_copies = [
+        remote(small, quad.at[mine], quad_send.at[k], quad_recv.at[k], quad_peers[k]) for k in range(3)
+    ]
+    own_small = pltpu.make_async_copy(small, quad.at[mine], own_sem.at[0])
+    docs_copies = [
+        remote(docs, docs_all.at[seq], docs_send.at[k], docs_recv.at[k], others[k]) for k in range(15)
+    ]
+    own_docs = pltpu.make_async_copy(docs, docs_all.at[seq], own_sem.at[1])
+    own_small.start()
+    own_docs.start()
+    for copy in quad_copies + docs_copies:
+        copy.start()
+    engine.tick()
+    own_small.wait()
+    for copy in quad_copies:
+        copy.wait()
+    small_full[pair] = (quad[0] + quad[1]) + (quad[2] + quad[3])
+    small_copies = []
+    for k in range(1, 8):
+        to = (((pair + k) % 8) * 2 + place.core, x)
+        small_copies.append(
+            remote(small_full.at[pair], small_full.at[pair], small_send.at[k], small_recv.at[k], to)
+        )
+        small_copies[-1].start()
+    own_docs.wait()
+    for copy in docs_copies:
+        copy.wait()
+
+    def spread_docs(at, carry):
+        tile = docs_all[at]
+        line = jnp.where(row == 0, tile[0:1], tile[1:2])
+        docs_row[:, pl.ds(pl.multiple_of(at * S_DEV, S_DEV), S_DEV)] = jnp.broadcast_to(line, (8, S_DEV))
+        docs_column[pl.ds(at * S_DEV, S_DEV)] = jnp.transpose(jnp.broadcast_to(line, (S_DEV, LANES)))
+        return carry
+
+    lax.fori_loop(0, 16, spread_docs, 0)
+
+    rows = tokens[...].reshape(2 * S_DEV, D)
+    for part in range(3):
+        engine.until(project_done[part])
+        fetch = pltpu.make_async_copy(full_rows(full, 32 * part), weights.at[part], fetch_sem.at[part])
+        fetch.start()
+        fetch.wait()
+        result = dot_nn(rows, weights[part].reshape(D, D)).astype(BF16)
+        for at_row in range(2):
+            for at_pair in range(PAIRS):
+                staged[at_pair, at_row, part] = result[
+                    at_row * S_DEV:(at_row + 1) * S_DEV, at_pair * LANES:(at_pair + 1) * LANES
+                ]
+    head_copies = []
+    for k in range(15):
+        to = (seq + k + 1) % 16
+        head_copies.append(
+            remote(staged.at[to // 2, to % 2], arrived.at[seq], head_send.at[k], head_recv.at[k], others[k])
+        )
+    own_heads = pltpu.make_async_copy(staged.at[pair, row], arrived.at[seq], own_sem.at[2])
+    own_heads.start()
+    engine.waiting = list(head_copies)
+
+    engine.until(memory_done)
+    fetch_memory = pltpu.make_async_copy(memory_full, memory_held, own_sem.at[3])
+    fetch_memory.start()
+    fetches = [
+        pltpu.make_async_copy(full_rows(full, at), weights.at[part], fetch_sem.at[part])
+        for part, at in enumerate((MEM_K_AT, MEM_V_AT))
+    ]
+    for fetch in fetches:
+        fetch.start()
+    fetch_memory.wait()
+    for part in range(2):
+        fetches[part].wait()
+
+        def project_memory(at, carry):
+            held = memory_held[at].reshape(4 * 2 * M_DEV, D)
+            result = dot_nn(held, weights[part].reshape(D, D)).astype(BF16)
+            memory_pairs[pl.ds(4 * at, 4), :, :, pl.ds(part * D, D)] = result.reshape(4, 2, M_DEV, D)
+            return carry
+
+        lax.fori_loop(0, 4, project_memory, 0)
+    engine.tick(max(WAIT_TICKS, -(-len(engine.waiting) // SENDS)))
+    own_heads.wait()
+    for copy in head_copies:
+        copy.wait()
+
     block = 2 * S_DEV
-    greet([((seq + step) % 16, x) for step in range(1, 16)])
-    pair, row = seq // 2, seq % 2
     columns = pl.ds(pl.multiple_of(pair * LANES, LANES), LANES)
-    mine = gathered.at[row, :, columns]
+    target = gathered.at[row, :, columns]
     away = (
         lax.broadcasted_iota(jnp.int32, (block, block), 1)
         - lax.broadcasted_iota(jnp.int32, (block, block), 0)
     )
     prefix_lane = lax.broadcasted_iota(jnp.int32, (2 * block, 32), 1)
-
-    def one_block(step, carry):
-        at = (step + seq // 2) % 8
+    prefix_keys, prefix_values = small_full[pair, 0:32], small_full[pair, 32:64]
+
+    for step in range(8):
+        at = (step + pair) % 8
         queries = stack_heads(arrived[pl.ds(2 * at, 2), 0].reshape(block, LANES))
         query_docs = docs_column[pl.ds(at * block, block)]
-        scores = dot_right(queries, prefix_keys[...]) * score_scale
-        weights = jnp.where(prefix_lane < PREFIX, jnp.exp(scores), 0.0)
-        sums[...] = jnp.concatenate([weights, jnp.zeros((2 * block, LANES - 32), F32)], axis=1)
-        parts[...] = dot_nn(weights.astype(BF16), prefix_values[...])
+        scores = dot_right(queries, prefix_keys) * score_scale
+        e = jnp.where(prefix_lane < PREFIX, jnp.exp(scores), 0.0)
+        sums[...] = jnp.concatenate([e, jnp.zeros((2 * block, LANES - 32), F32)], axis=1)
+        parts[...] = dot_nn(e.astype(BF16), prefix_values)
 
         def one_tile(key_at, carry):
             keys = arrived[pl.ds(2 * key_at, 2), 1].reshape(block, LANES)
             values = arrived[pl.ds(2 * key_at, 2), 2].reshape(block, LANES)
-            key_docs = docs_row[:, pl.ds(pl.multiple_of(key_at * block, block), block)]
+            key_docs = docs_row[0:1, pl.ds(pl.multiple_of(key_at * block, block), block)]
             same = jnp.concatenate([query_docs, query_docs], axis=1) == key_docs
             allowed = same & (away <= (at - key_at) * block)
             scores = dot_right(queries, keys) * score_scale
-            weights = jnp.where(allowed[None], jnp.exp(scores).reshape(2, block, block), 0.0)
-            weights = weights.reshape(2 * block, block)
-            sums[...] += weights[:, :LANES] + weights[:, LANES:]
-            parts[...] += dot_nn(weights.astype(BF16), values)
+            e = jnp.where(allowed[None], jnp.exp(scores).reshape(2, block, block), 0.0)
+            e = e.reshape(2 * block, block)
+            sums[...] += e[:, :LANES] + e[:, LANES:]
+            parts[...] += dot_nn(e.astype(BF16), values)
             return carry
 
         lax.fori_loop(0, at + 1, one_tile, 0)
@@ -853,49 +951,141 @@
         here = pl.ds(at * block, block)
         attended[here] = result
         inverse[here] = merge_heads(jnp.broadcast_to(totals, (2 * block, LANES)))
-        staged[pl.ds(2 * at, 2)] = result.astype(BF16).reshape(2, S_DEV, LANES)
+        result_staged[pl.ds(2 * at, 2)] = result.astype(BF16).reshape(2, S_DEV, LANES)
         for half in range(2):
             to = 2 * at + half
 
             @pl.when(to != seq)
             def _():
-                remote(staged.at[to], mine, send_sem.at[to], recv_sem.at[seq], (to, x)).start()
+                remote(result_staged.at[to], target, out_send.at[to], out_recv.at[seq], (to, x)).start()
 
             @pl.when(to == seq)
             def _():
-                pltpu.make_async_copy(staged.at[to], mine, local_sem).start()
-
-        return carry
-
-    lax.fori_loop(0, 8, one_block, 0)
-    pltpu.make_async_copy(staged.at[seq], mine, local_sem).wait()
-    for step in range(1, 16):
-        other = (seq + step) % 16
-        remote(staged.at[other], mine, send_sem.at[other], recv_sem.at[other], (other, x)).wait()
-
-
-def self_forward(arrived, docs_row, docs_column, prefix_keys, prefix_values):
+                pltpu.make_async_copy(result_staged.at[to], target, own_sem.at[4]).start()
+
+        engine.tick(STEP_TICKS)
+
+    for copy in small_copies:
+        copy.wait()
+    engine.until(cross_done)
+    fetches = [
+        pltpu.make_async_copy(full_rows(full, at), weights.at[part], fetch_sem.at[part])
+        for part, at in enumerate((SELF_OUT_AT, CROSS_Q_AT, CROSS_OUT_AT))
+    ]
+    for fetch in fetches:
+        fetch.start()
+    gains = [
+        jnp.concatenate(
+            [small_full[at_pair, 128:144].astype(F32)[part:part + 1] for at_pair in range(PAIRS)], axis=1
+        )
+        for part in range(2)
+    ]
+    pltpu.make_async_copy(result_staged.at[seq], target, own_sem.at[4]).wait()
+    for other, _ in others:
+        remote(result_staged.at[other], target, out_send.at[other], out_recv.at[other], (other, x)).wait()
+    fetches[0].wait()
+    resid = tokens[...].reshape(2 * S_DEV, D).astype(F32) + dot_nn(
+        gathered[...].reshape(2 * S_DEV, D), weights[0].reshape(D, D)
+    )
+    first_resid[...] = resid
+    normed = norm_rows(resid, gains[0])
+    first_norm[...] = normed
+    engine.tick(STEP_TICKS)
+    fetches[1].wait()
+    cross_queries[...] = dot_nn(normed.astype(BF16), weights[1].reshape(D, D)).astype(BF16).reshape(2, S_DEV, D)
+    engine.tick(STEP_TICKS)
+    memory_len = 16 * M_DEV
+    cross_prefix_lane = lax.broadcasted_iota(jnp.int32, (2 * S_DEV, 32), 1)
+    for at_row in range(2):
+        own = jnp.transpose(jnp.broadcast_to(docs[at_row:at_row + 1], (LANES, S_DEV)))
+        own = jnp.concatenate([own] * (memory_len // LANES), axis=1)
+        lines = [
+            sum(docs_all[4 * at + k, 2 + at_row:3 + at_row] for k in range(4)) for at in range(4)
+        ]
+        allowed = own == jnp.concatenate(lines, axis=1)
+
+        def one_pair(at_pair, carry):
+            first = pl.multiple_of(at_pair * LANES, LANES)
+            columns, value_columns = pl.ds(first, LANES), pl.ds(pl.multiple_of(first + D, LANES), LANES)
+            stacked = stack_heads(cross_queries[at_row, :, columns])
+            keys = memory_pairs[:, at_row, :, columns].reshape(memory_len, LANES)
+            values = memory_pairs[:, at_row, :, value_columns].reshape(memory_len, LANES)
+            scores = dot_right(stacked, small_full[at_pair, 64:96]) * score_scale
+            prefix_e = jnp.where(cross_prefix_lane < PREFIX, jnp.exp(scores), 0.0)
+            scores = dot_right(stacked, keys) * score_scale
+            e = jnp.where(allowed[None], jnp.exp(scores).reshape(2, S_DEV, memory_len), 0.0)
+            e = e.reshape(2 * S_DEV, memory_len)
+            totals = jnp.sum(e, axis=1, keepdims=True) + jnp.sum(prefix_e, axis=1, keepdims=True)
+            totals = 1.0 / totals
+            summed = dot_nn(e.astype(BF16), values) + dot_nn(prefix_e.astype(BF16), small_full[at_pair, 96:128])
+            crossed[at_row, :, columns] = merge_heads(summed * totals)
+            cross_inverse[at_row, :, columns] = merge_heads(jnp.broadcast_to(totals, (2 * S_DEV, LANES)))
+            return carry
+
+        lax.fori_loop(0, PAIRS // 2, one_pair, 0)
+        engine.tick(STEP_TICKS)
+        lax.fori_loop(PAIRS // 2, PAIRS, one_pair, 0)
+        engine.tick(STEP_TICKS)
+    fetches[2].wait()
+    resid = first_norm[...] + dot_nn(
+        crossed[...].reshape(2 * S_DEV, D).astype(BF16), weights[2].reshape(D, D)
+    )
+    second_resid[...] = resid
+    second_norm[...] = norm_rows(resid, gains[1])
+    engine.finish()
+
+
+def full_rows(full, first):
+    return full.at[:, :, :, :, pl.ds(first, 32)]
+
+
+def first_call(tokens, memory, small, docs, *weights):
     length = 16 * S_DEV
-    return pl.pallas_call(
-        self_forward_kernel,
+    chunks = 16 * 32 // PIECE_ROWS + 32 // PIECE_ROWS + 2
+    dma = pltpu.SemaphoreType.DMA
+    shape = jax.ShapeDtypeStruct
+    outs = pl.pallas_call(
+        first_kernel,
         out_shape=(
-            jax.ShapeDtypeStruct((2, S_DEV, D), BF16),
-            jax.ShapeDtypeStruct((length, LANES), F32),
-            jax.ShapeDtypeStruct((length, LANES), F32),
+            shape((4, 2, 2, 2, ALL_ROWS, D), BF16),
+            shape((4, 2, 2, 2, M_DEV, D), BF16),
+            shape((16, 2, M_DEV, 2 * D), BF16),
+            shape((8, SMALL_ROWS, LANES), BF16),
+            shape((16, 8, LANES), F32),
+            shape((8, length), F32),
+            shape((length, LANES), F32),
+            shape((16, 3, S_DEV, LANES), BF16),
+            shape((length, LANES), F32),
+            shape((length, LANES), F32),
+            shape((2 * S_DEV, D), F32),
+            shape((2, S_DEV, D), BF16),
+            shape((2, S_DEV, D), F32),
+            shape((2, S_DEV, D), F32),
+            shape((2 * S_DEV, D), F32),
+            shape((2 * S_DEV, D), F32),
         ),
-        in_specs=[whole()] * 5,
-        out_specs=(whole(), whole(), whole()),
+        in_specs=[whole(), whole(pl.ANY), whole(), whole()] + [whole(pl.ANY)] * 8,
+        out_specs=(whole(pl.ANY), whole(pl.ANY)) + (whole(),) * 14,
         scratch_shapes=[
+            pltpu.VMEM((2, S_DEV, D), BF16),
+            pltpu.VMEM((2 * S_DEV, D), F32),
+            pltpu.VMEM((3, 4, 2, 2, 2, 32, D), BF16),
+            pltpu.VMEM((PAIRS, 2, 3, S_DEV, LANES), BF16),
+            pltpu.VMEM((4, SMALL_ROWS, LANES), BF16),
+            pltpu.VMEM((4, 2, 2, 2, M_DEV, D), BF16),
             pltpu.VMEM((16, S_DEV, LANES), BF16),
             pltpu.VMEM((4 * S_DEV, LANES), F32),
             pltpu.VMEM((4 * S_DEV, LANES), F32),
-            pltpu.SemaphoreType.DMA,
-            pltpu.SemaphoreType.DMA((16,)),
-            pltpu.SemaphoreType.DMA((16,)),
+            dma((chunks,)),
+            dma((chunks, 3)), dma((chunks, 3)), dma((chunks, 2)), dma((chunks, 2)),
+            dma((chunks, 3)), dma((chunks, 3)), dma((chunks, 1)), dma((chunks, 1)),
+            dma((3,)), dma((5,)), dma((3,)), dma((3,)), dma((8,)), dma((8,)), dma((15,)), dma((15,)),
+            dma((15,)), dma((15,)), dma((16,)), dma((16,)),
         ],
-        compiler_params=params(2),
-        name="self_forward",
-    )(arrived, docs_row, docs_column, prefix_keys, prefix_values)
+        compiler_params=params(0),
+        name="first",
+    )(tokens, memory, small, docs, *weights)
+    return (outs[0].reshape(32, ALL_ROWS, D),) + tuple(outs[2:])
 
 
 def self_backward_kernel(
@@ -984,7 +1174,7 @@
             here = pl.ds(at * block, block)
             queries = arrived[pl.ds(2 * at, 2), 0].reshape(block, LANES)
             low = grad_low[here]
-            query_docs = docs_row[:, pl.ds(pl.multiple_of(at * block, block), block)]
+            query_docs = docs_row[0:1, pl.ds(pl.multiple_of(at * block, block), block)]
             allowed = (key_docs == query_docs) & (away <= (at - key_at) * block)
             weights = jnp.exp(dot_right(keys, queries) * score_scale).reshape(2, block, block)
             weights = jnp.where(allowed[None], weights, 0.0).reshape(2 * block, block)
@@ -1048,49 +1238,6 @@
         compiler_params=params(3),
         name="self_backward",
     )(arrived, grad_out, attended, inverse, docs_row, docs_column, prefix_keys, prefix_values)
-
-
-def cross_forward_kernel(
-    queries, keys, values, query_docs, key_docs, prefix_keys, prefix_values, crossed, inverse
-):
-    stacked = stack_heads(queries[0])
-    count = 2 * S_DEV
-    prefix_lane = lax.broadcasted_iota(jnp.int32, (count, 32), 1)
-    scores = dot_right(stacked, prefix_keys[...]) * score_scale
-    prefix_weights = jnp.where(prefix_lane < PREFIX, jnp.exp(scores), 0.0)
-    memory_len = keys.shape[0] * keys.shape[2]
-    scores = dot_right(stacked, keys[...].reshape(memory_len, LANES)) * score_scale
-    allowed = query_docs[0] == key_docs[0]
-    weights = jnp.where(allowed[None], jnp.exp(scores).reshape(2, S_DEV, memory_len), 0.0)
-    weights = weights.reshape(count, memory_len)
-    totals = jnp.sum(weights, axis=1, keepdims=True) + jnp.sum(prefix_weights, axis=1, keepdims=True)
-    totals = 1.0 / totals
-    summed = dot_nn(weights.astype(BF16), values[...].reshape(memory_len, LANES))
-    summed += dot_nn(prefix_weights.astype(BF16), prefix_values[...])
-    crossed[0] = merge_heads(summed * totals)
-    inverse[0] = merge_heads(jnp.broadcast_to(totals, (count, LANES)))
-
-
-def cross_forward(queries, memory_pairs, query_docs, key_docs, prefix_keys, prefix_values):
-    memory_len = 16 * M_DEV
-    head_block = pl.BlockSpec((1, S_DEV, LANES), lambda row, pair: (row, 0, pair))
-    keys = pl.BlockSpec((16, 1, M_DEV, LANES), lambda row, pair: (0, row, 0, pair))
-    values = pl.BlockSpec((16, 1, M_DEV, LANES), lambda row, pair: (0, row, 0, PAIRS + pair))
-    prefix = pl.BlockSpec((32, LANES), lambda row, pair: (0, pair))
-    return pl.pallas_call(
-        cross_forward_kernel,
-        grid=(2, PAIRS),
-        out_shape=(jax.ShapeDtypeStruct((2, S_DEV, D), F32),) * 2,
-        in_specs=[
-            head_block, keys, values,
-            pl.BlockSpec((1, S_DEV, memory_len), lambda row, pair: (row, 0, 0)),
-            pl.BlockSpec((1, 1, memory_len), lambda row, pair: (row, 0, 0)),
-            prefix, prefix,
-        ],
-        out_specs=(head_block, head_block),
-        compiler_params=params(),
-        name="cross_forward",
-    )(queries, memory_pairs, memory_pairs, query_docs, key_docs, prefix_keys, prefix_values)
 
 
 def cross_backward_kernel(
@@ -1256,9 +1403,9 @@
         ),
         in_specs=[
             rows, rows, pl.BlockSpec((1, D), still),
-            pl.BlockSpec((32, 32, D), lambda step: (0, at(step), 0)),
-            pl.BlockSpec((8, 128, D), lambda step: (at(step), 1, 0)),
-            pl.BlockSpec((32, 32, D), lambda step: (0, 8, 0)),
+            pl.BlockSpec((32, 32, D), lambda step: (0, INNER_AT // 32 + at(step), 0)),
+            pl.BlockSpec((8, 128, D), lambda step: (at(step), OUTER_AT // 128, 0)),
+            pl.BlockSpec((32, 32, D), lambda step: (0, MIXED_AT // 32, 0)),
         ],
         out_specs=(rows, rows, pl.BlockSpec((32, 32, D), lambda step: (0, 0, 0))),
         scratch_shapes=[
@@ -1282,66 +1429,33 @@
     mixed = jnp.concatenate(
         [adapter_down, jnp.concatenate([adapter_up[:, :ADAPTER], adapter_up[:, ADAPTER:]], axis=0)], axis=1
     )
-    feed_flat = jnp.concatenate(
-        [inner_weight[:, part * D:(part + 1) * D] for part in range(4)] + [outer_weight, mixed], axis=0
-    )
-    feed_weights = lax.all_gather(feed_flat, ("seq", "rows"), axis=0, tiled=True).reshape(32, FEED_ROWS, D)
-
+    lane_group = lax.broadcasted_iota(jnp.int32, (1, LANES), 1) // 32
     small = jnp.concatenate([
-        norm_gains.reshape(-1), prefixes.reshape(-1),
-        token_docs.astype(BF16).reshape(-1), memory_docs.astype(BF16).reshape(-1),
+        jnp.pad(prefixes, ((0, 0), (0, 2), (0, 0))).reshape(128, 32), jnp.pad(norm_gains, ((0, 13), (0, 0)))
     ])
-    small = jnp.pad(small, (0, SMALL_ROWS * D - small.shape[0])).reshape(SMALL_ROWS, D)
-    full, memory_all = gather_first(
-        self_project, self_output, cross_query, cross_memory, cross_output, small, memory
+    small = jnp.where(lane_group == (seq % 2) * 2 + x, jnp.tile(small, (1, 4)), jnp.zeros((), BF16))
+    memory_line = jnp.where(lane_group == seq % 4, jnp.tile(memory_docs, (1, 4)), 0)
+    docs = jnp.concatenate([token_docs, memory_line, jnp.zeros((4, LANES), jnp.int32)]).astype(F32)
+    (
+        full, memory_pairs, small_full, docs_all, docs_row, docs_column, arrived, pair_attended, pair_inverse,
+        first_resid, cross_queries, crossed, cross_inverse, second_resid, second_norm,
+    ) = first_call(
+        inputs, memory.reshape(2, M_DEV, D), small, docs,
+        self_project, self_output, cross_query, cross_memory, cross_output, inner_weight, outer_weight, mixed,
     )
 
     def weight(first):
         return full[:, first:first + 32].reshape(D, D)
 
-    flat = full[:, SMALL_AT:SMALL_AT + 5].reshape(32, 5 * D)
-    gains = flat[:, :96].reshape(32, 3, 32).transpose(1, 0, 2).reshape(3, D).astype(F32)
-    prefix_parts = flat[:, 96:3936].reshape(32, 4, PREFIX, 32)
-    cross_prefixes = prefix_parts[:, 2:].transpose(1, 2, 0, 3).reshape(2, PREFIX, D)
-    cross_prefixes = jnp.pad(cross_prefixes, ((0, 0), (0, 2), (0, 0)))
-    pair_prefixes = lax.dynamic_slice_in_dim(prefix_parts[:, :2], 4 * (seq // 2), 4, 0)
-    pair_prefixes = pair_prefixes.transpose(1, 2, 0, 3).reshape(2, PREFIX, LANES)
-    pair_prefixes = jnp.pad(pair_prefixes, ((0, 0), (0, 2), (0, 0)))
-    row_docs = lax.dynamic_index_in_dim(flat[:, 3936:4256].reshape(16, 2, 320), x, 1, False).astype(F32)
-    own_docs = lax.dynamic_index_in_dim(row_docs[:, :256].reshape(16, 2, S_DEV), seq % 2, 1, False)
-    docs_row = own_docs.reshape(1, 16 * S_DEV)
-    docs_column = jnp.broadcast_to(docs_row.reshape(-1, 1), (16 * S_DEV, LANES))
-    memory_row = row_docs[:, 256:].reshape(16, 2, M_DEV).transpose(1, 0, 2).reshape(2, 1, 16 * M_DEV)
+    gains = small_full[:, 128:131].transpose(1, 0, 2).reshape(3, D).astype(F32)
+    cross_prefixes = small_full[:, 64:128].reshape(8, 2, 32, LANES).transpose(1, 2, 0, 3).reshape(2, 32, D)
+    pair_prefixes = lax.dynamic_index_in_dim(small_full, seq // 2, 0, False)[:64].reshape(2, 32, LANES)
+    memory_row = docs_all[:, 2:4].reshape(4, 4, 2, LANES).sum(axis=1).transpose(1, 0, 2).reshape(2, 1, 16 * M_DEV)
     memory_column = jnp.broadcast_to(memory_row.reshape(2, -1, 1), (2, 16 * M_DEV, LANES))
     query_row = token_docs.astype(F32).reshape(2, 1, S_DEV)
-    query_column = jnp.broadcast_to(query_row.reshape(2, S_DEV, 1), (2, S_DEV, 16 * M_DEV))
-
-    arrived = project_exchange(inputs, full)
-    attended, pair_attended, pair_inverse = self_forward(
-        arrived, docs_row, docs_column, pair_prefixes[0], pair_prefixes[1]
-    )
-    memory_pairs = jnp.concatenate(
-        [jnp.dot(memory_all.reshape(-1, D), weight(at), preferred_element_type=F32) for at in (MEM_K_AT, MEM_V_AT)],
-        axis=1,
-    ).astype(BF16).reshape(16, 2, M_DEV, 2 * D)
-
-    first_resid = inputs.reshape(tokens, D).astype(F32) + jnp.dot(
-        attended.reshape(tokens, D), weight(SELF_OUT_AT), preferred_element_type=F32
-    )
-    first_norm = norm_rows(first_resid, gains[0])
-    cross_queries = jnp.dot(
-        first_norm.astype(BF16), weight(CROSS_Q_AT), preferred_element_type=F32
-    ).astype(BF16).reshape(2, S_DEV, D)
-    crossed, cross_inverse = cross_forward(
-        cross_queries, memory_pairs, query_column, memory_row, cross_prefixes[0], cross_prefixes[1]
-    )
-    second_resid = first_norm + jnp.dot(
-        crossed.reshape(tokens, D).astype(BF16), weight(CROSS_OUT_AT), preferred_element_type=F32
-    )
-    second_norm = norm_rows(second_resid, gains[1])
 
     layer_out, second_grad, small_grads = feed_forward_backward(
-        second_norm, out_grad.reshape(tokens, D), gains[2:3], feed_weights
+        second_norm, out_grad.reshape(tokens, D), gains[2:3], full
     )
     small_sums = lax.psum_scatter(small_grads.reshape(1024, D), "seq", scatter_dimension=0, tiled=True)
 

time: 483 us -> 447 us (0.925); the launches traced: 480 us -> 438 us
  local copies, waits for them, and re-layouts: 46.9 us -> 30.2 us
  Pallas kernels: 373 us -> 357 us
  matrix products: 25.4 us -> 17 us
    pallas_call x4 -> x1, Pallas kernels: 248 us -> 235 us  [first_call(): pl.pallas_call(first_kernel, out_shape=(shape((4, 2, 2, 2, ALL_ROWS, D),...]
    dot_general x5 -> x0, matrix products: 9.51 us -> none  [the longest x2 4.71 us: fast_device(): jnp.dot(memory_all.reshape(-1, D), weight(at), preferred_element_type=F32)]
    unnamed x53 -> x32, local copies, waits for them, and re-layouts: 14.6 us -> 7.23 us
    reshape x14 -> x2, local copies, waits for them, and re-layouts: 5.22 us -> 0.18 us  [the longest x1 0.09 us: fast_device(): jnp.pad(prefixes, ((0, 0), (0, 2), (0, 0))).reshape(128, 32)]
  transfers between devices with their start and end apart: 6 -> 5, of which waited for: 1 -> 2; matrix products, arithmetic and copies ran while one was open for 14% -> 10% of each run, Pallas kernels for 73% -> 23%
where the time goes in v2:
time: 447 us; the launch traced here: 438 us
  Pallas kernels  357 us (80%)
  local copies, waits for them, and re-layouts  30.2 us (7%)
  matrix products  17 us (4%)
  between operations  14.9 us (3%)
  other arithmetic  12.1 us (3%)
  waiting for transfers between devices  5.81 us (1%)
    pallas_call x1, Pallas kernels, first_call(): pl.pallas_call(first_kernel, out_shape=(shape((4, 2, 2, 2, ALL_ROWS, D),...  235 us
    pallas_call x1, Pallas kernels, self_backward(): pl.pallas_call(self_backward_kernel, out_shape=(jax.ShapeDtypeStruct((PAI...  78.5 us
    pallas_call x1, Pallas kernels, feed_forward_backward(): pl.pallas_call(feed_kernel, grid=(8,), out_shape=(jax.ShapeDtypeStruct((t...  22.8 us
    pallas_call x1, Pallas kernels, cross_backward(): pl.pallas_call(cross_backward_kernel, grid=(PAIRS, 2), out_shape=(jax.Sha...  20.9 us
    dot_general x8, matrix products, dot_right(): lax.dot_general(left, right, (((1,), (1,)), ((), ())), preferred_element_...  17 us
    slice x1, local copies, waits for them, and re-layouts, weight(): return full[:, first:first + 32].reshape(D, D)  11.8 us
  transfers between devices with their start and end apart: 5, of which 2 were waited for; matrix products, arithmetic and copies ran while one was open for 10% of the time, Pallas kernels for 23%

profile of v2, /device:TPU:28, one launch (start us, length us, event | category | flops | bytes accessed | tf_op | source)
XLA Modules:
  0.0 438.1 jit_solution(1655383206193893243)
XLA Ops:
  7.2 0.9 copy.49
  8.2 0.8 copy.37
  9.1 0.7 tile.20
  10.0 0.7 fusion.16
  10.7 0.6 broadcast_select_fusion.small
  11.4 1.3 add_convert_fusion.1.docs
  12.7 1.4 maximum_maximum_fusion.mixed
  14.1 234.8 %first.1 = (bf16[4,2,2,2,544,1024]{5,4,3,2,1,0:T(8,128)(2,1)}, bf16[4,2,2,2,32,1024]{5,4,3,2,1,0:T(8,128)(2,1)}, bf16[16,2,32,2048]{3,2,1,0:T(8,128)(2,1)}, bf16...) custom-call(bf16[2,128,1024]{2,1,0:T(8,128)(2,1)} %tokens.1, ...), custom_call_target="tpu_custom_call" | custom-call | tf_op jit(solution)/shard_map/first/pallas_call | solution.py:1047
  249.0 0.7 convert_bitcast_fusion
  249.7 0.6 fusion.17
  250.3 22.8 %feed.1 = (bf16[256,1024]{1,0:T(8,128)(2,1)}, f32[256,1024]{1,0:T(8,128)}, bf16[32,32,1024]{2,1,0:T(8,128)(2,1)}) custom-call(f32[256,1024]{1,0:T(8,128)} %get-tuple-element.30.normed, bf16[256,1024]{1,0:T(8,128)(2,1)} %bitcast.122, f32[1,1024]{1,0:T(1,128)} %get-tuple-element.97.gain, bf16[32,544,1024]{2,1,0:T(8,128)(2,1)} %bitcast.99, ...), custom_call_target="tpu_custom_call" | custom-call | tf_op jit(solution)/shard_map/feed/pallas_call | solution.py:1396
  273.4 0.6 copy-done.9
  274.1 0.6 convert_element_type.52
  275.5 0.6 copy.72
  276.1 0.6 copy.73
  276.8 0.9 bitcast_reduce_fusion
  277.6 1.3 fusion.11
  279.0 11.8 %fusion.12 = (bf16[32,32,1024]{2,1,0:T(8,128)(2,1)}, bf16[32,32,1024]{2,1,0:T(8,128)(2,1)}, bf16[32,32,1024]{2,1,0:T(8,128)(2,1)S(1)}, bf16[32,32,1024]{2,1,0:T(...) fusion(bf16[32,544,1024]{2,1,0:T(8,128)(2,1)} %bitcast.102), kind=kLoop, calls=%fused_computation.65 | loop fusion | bytes 33554432 | tf_op jit(solution)/shard_map/slice | solution.py:1448
  290.7 1.7 fusion.18.grad_out
  292.5 1.0 broadcast_in_dim.48.key_docs
  293.5 20.9 %cross_backward.1 = (bf16[2,128,1024]{2,1,0:T(8,128)(2,1)}, bf16[16,2,32,1024]{3,2,1,0:T(8,128)(2,1)}, bf16[16,2,32,1024]{3,2,1,0:T(8,128)(2,1)}, f32[2,32,1024]{2,1,0:T(8,128)}) custom-call(bf16[2,128,1024]{2,1,0:T(8,128)(2,1)} %get-tuple-element.37.queries, bf16[16,2,32,2048]{3,2,1,0:T(8,128)(2,1)} %get-tuple-element.38.keys.values, ...), custom_call_target="tpu_custom_call" | custom-call | tf_op jit(solution)/shard_map/cross_backward/pallas_call | solution.py:1297
  314.4 1.0 slice.182
  316.1 4.7 %fusion.19 = f32[1024,1024]{1,0:T(8,128)S(1)} fusion(bf16[1024,1024]{1,0:T(8,128)(2,1)} %bitcast.144, bf16[1024,1024]{1,0:T(8,128)(2,1)} %bitcast.110), kind=kOutput, calls=%fused_computation.72 | convolution fusion | flops 2147483648 | bytes 8388608 | tf_op jit(solution)/shard_map/dot_general | solution.py:28
  320.8 2.4 add_convert_fusion
  323.2 1.7 pad_maximum_fusion
  324.9 1.2 copy-done.1
  326.6 0.6 dynamic-slice_bitcast_fusion.1
  327.2 3.1 fusion.10
  330.3 1.7 convolution_convert_fusion
  332.0 78.5 %self_backward.1 = (bf16[8,2,3,128,128]{4,3,2,1,0:T(8,128)(2,1)}, f32[2,32,128]{2,1,0:T(8,128)}) custom-call(bf16[16,3,128,128]{3,2,1,0:T(8,128)(2,1)} %get-tuple-element.43.arrived, bf16[2,128,1024]{2,1,0:T(8,128)(2,1)} %bitcast.127, f32[2048,128]{1,0:T(8,128)} %get-tuple-element.44.attended, f32[2048,128]{1,0:T(8,128)} %get-tuple-element.45.inverse, ...), custom_call_target="tpu_custom_call" | custom-call | tf_op jit(solution)/shard_map/self_backward/pallas_call | solution.py:1220
  410.8 1.5 fusion.13
  412.3 0.3 copy.40
  412.6 0.3 copy.41
  413.0 0.3 copy.42
  413.3 0.5 copy-done.3
  414.2 0.9 convolution_add_fusion.2
  415.1 0.7 copy-done.2
  415.8 0.7 convolution_add_fusion.1
  416.5 1.7 convolution_add_fusion
  418.3 0.9 convert.14
  419.7 5.3 %collective-permute-done.2 = f32[32,1024]{1,0:T(8,128)S(1)} collective-permute-done((f32[32,1024]{1,0:T(8,128)S(1)}, f32[32,1024]{1,0:T(8,128)S(1)}, u32[]{:S(2)}, u32[]{:S(2)}) %collective-permute-start.2) | collective-permute-done | bytes 131104 | tf_op jit(solution)/shard_map/ppermute | solution.py:1491
  425.1 0.7 slice.169
  426.4 0.6 pad_maximum_fusion.1
  427.1 0.6 slice.171
  427.8 0.9 slice.166
  428.7 0.7 convert.15
  429.4 0.5 collective-permute-done.1
  430.1 0.7 copy.48
  (79 shorter events, 4.6 us)
Async XLA Ops:
  7.2 411.1 %reduce-scatter.5.cloned.1.call-start = ((), (), s32[]{:S(2)}) async-start(), calls=%async_computation.3 | async-start | bytes 2228224 | tf_op jit(solution)/shard_map/reduce_scatter | solution.py:1460
  273.1 1.0 copy-start.9
  273.1 1.0 copy-start.11
  273.1 1.5 copy-start
  273.1 1.9 copy-start.4
  273.1 151.9 %reduce-scatter.3.cloned.1.call-start = ((), (), s32[]{:S(2)}) async-start(), calls=%async_computation.2 | async-start | bytes 2506752 | tf_op jit(solution)/shard_map/reduce_scatter | solution.py:1476
  316.1 4.8 %copy-start.8 = (bf16[32,32,1024]{2,1,0:T(8,128)(2,1)S(1)}, bf16[32,32,1024]{2,1,0:T(8,128)(2,1)}, u32[]{:S(2)}) copy-start(bf16[32,32,1024]{2,1,0:T(8,128)(2,1)} %get-tuple-element.72) | copy-start | bytes 6291460
  316.1 4.8 %copy-start.12 = (bf16[16,2,32,1024]{3,2,1,0:T(8,128)(2,1)S(1)}, bf16[16,2,32,1024]{3,2,1,0:T(8,128)(2,1)}, u32[]{:S(2)}) copy-start(bf16[16,2,32,1024]{3,2,1,0:T(8,128)(2,1)} %get-tuple-element.50) | copy-start | bytes 6291460
  324.9 1.2 copy-start.1
  327.2 3.1 copy-start.7
  330.3 1.8 copy-start.5
  410.6 8.7 %collective-permute-start = (f32[2,32,128]{2,1,0:T(8,128)}, f32[2,32,128]{2,1,0:T(8,128)S(1)}, u32[]{:S(2)}, u32[]{:S(2)}) collective-permute-start(f32[2,32,128]{2,1,0:T(8,128)} %get-tuple-element.52), channel_id=1, source_target_pairs={{0,2},{2,0},{4,6},{6,4},{8,10},{10,8},{12,14},{14,12},{16,18},{18,... | collective-permute-start | bytes 98312 | tf_op jit(solution)/shard_map/ppermute | solution.py:1499
  412.3 1.6 copy-start.3
  412.3 1.9 copy-start.6
  414.2 1.6 copy-start.2
  416.5 2.8 copy-start.10
  419.2 5.8 %collective-permute-start.2 = (f32[32,1024]{1,0:T(8,128)S(1)}, f32[32,1024]{1,0:T(8,128)S(1)}, u32[]{:S(2)}, u32[]{:S(2)}) collective-permute-start(f32[32,1024]{1,0:T(8,128)S(1)} %dynamic-slice_bitcast_fusion), channel_id=1, source_target_pairs={{0,1},{1,0},{2,3},{3,2},{4,5},{5,4},{6,7},{7,6},{8,9},{9,8},{10,11... | collective-permute-start | bytes 393224 | tf_op jit(solution)/shard_map/ppermute | solution.py:1491
  426.1 3.7 collective-permute-start.1
Sparse Core Ops, SparseCore 0:
  273.2 59.6 reduce-scatter.4
  337.2 78.6 reduce-scatter.2

commit v3 on v2

--- a/solution.py
+++ b/solution.py
@@ -1088,34 +1088,211 @@
     return (outs[0].reshape(32, ALL_ROWS, D),) + tuple(outs[2:])
 
 
-def self_backward_kernel(
-    arrived, grad_out, attended, inverse, docs_row, docs_column, prefix_keys, prefix_values,
-    gathered, prefix_grads,
-    grads, grad_low, delta, query_grads, key_grads, value_grads, staged,
-    local_sem, in_send, in_recv, out_send, out_recv, query_send, query_recv,
+def second_kernel(
+    second_grad, second_resid, small_full, docs, docs_all, docs_row, crossed, cross_inverse, cross_queries,
+    full, memory_pairs_far, first_resid_far, arrived_far, attended_far, inverse_far, docs_column_far, small_grads,
+    input_grad, memory_grad, down_grad, up_grad, prefix_sum,
+    weights, memory_pairs, first_resid, arrived, attended, inverse, docs_column,
+    pull, cross_grad, cross_query_grad, key_terms, value_terms, cross_prefix,
+    small_core, small_mine, small_x, small_pair, small_all,
+    memory_part, memory_core, memory_mine, memory_all, prefix_all, prefix_mine, prefix_quad,
+    heads_out, grads, grad_low, delta, query_grads, key_grads, value_grads, staged, gathered,
+    fetch_sem, own_sem, near_send, near_recv, small_send, small_recv, memory_send, memory_recv,
+    prefix_send, prefix_recv, quad_send, quad_recv,
+    in_send, in_recv, out_send, out_recv, query_send, query_recv,
 ):
-    seq, x = lax.axis_index("seq"), lax.axis_index("rows")
+    place = Place()
+    seq, x, pair, row, core = place.seq, place.x, place.pair, place.row, place.core
+    z, y = place.z, place.y
+    others = place.others()
+    tokens = 2 * S_DEV
+    memory_len = 16 * M_DEV
     block = 2 * S_DEV
-    pair, row = seq // 2, seq % 2
-    greet([((seq + step) % 16, x) for step in range(1, 16)])
-
-    def heads_for(to):
-        return grad_out.at[to % 2, :, pl.ds(pl.multiple_of((to // 2) * LANES, LANES), LANES)]
-
-    own = pltpu.make_async_copy(heads_for(seq), grads.at[seq], local_sem.at[0])
-    own.start()
+
+    fetches = {}
+
+    def fetch(name, source, target):
+        fetches[name] = pltpu.make_async_copy(source, target, fetch_sem.at[len(fetches)])
+        fetches[name].start()
+
+    firsts = (CROSS_OUT_AT, CROSS_Q_AT, SELF_OUT_AT, MEM_K_AT, MEM_V_AT, Q_AT, K_AT, V_AT)
+
+    def fetch_weight(at):
+        fetch(at, full.at[:, pl.ds(at, 32)], weights.at[firsts.index(at)])
+
+    def weight(at):
+        return weights[firsts.index(at)].reshape(D, D)
+
+    fetch_weight(CROSS_OUT_AT)
+    fetch("pairs", memory_pairs_far, memory_pairs)
+    fetch_weight(CROSS_Q_AT)
+    fetch("resid", first_resid_far, first_resid)
+    fetch_weight(SELF_OUT_AT)
+    fetch_weight(MEM_K_AT)
+    fetch_weight(MEM_V_AT)
+    fetch("arrived", arrived_far, arrived)
+    fetch("attended", attended_far, attended)
+    fetch("inverse", inverse_far, inverse)
+    fetch("docs", docs_column_far, docs_column)
+    for at in (K_AT, V_AT, Q_AT):
+        fetch_weight(at)
+    greet(others + [place.along_x(), place.diagonal()])
+
+    small_first = remote(
+        small_grads.at[:, :, 1 - core], small_core, near_send.at[0], near_recv.at[0], place.other_core()
+    )
+    small_own = pltpu.make_async_copy(small_grads.at[:, :, core], small_mine, own_sem.at[0])
+    small_second = remote(small_mine.at[:, :, 1 - x], small_x, near_send.at[1], near_recv.at[1], place.along_x())
+    plane = z * 2 + y
+
+    def chips(source, target, sends, recvs):
+        copies = []
+        for k in range(1, 8):
+            to = (plane + k) % 8
+            copies.append(
+                remote(source.at[to // 2, to % 2], target.at[plane], sends.at[k], recvs.at[k], (to * 2 + core, x))
+            )
+        return copies
+
+    small_third = chips(small_pair, small_all, small_send, small_recv)
+    memory_first = remote(
+        memory_part.at[:, :, 1 - core], memory_core, near_send.at[2], near_recv.at[2], place.other_core()
+    )
+    memory_second = chips(memory_mine, memory_all, memory_send, memory_recv)
+    small_first.start()
+    small_own.start()
+
+    gains = [
+        jnp.concatenate(
+            [small_full[at_pair, 128:144].astype(F32)[part:part + 1] for at_pair in range(PAIRS)], axis=1
+        )
+        for part in range(2)
+    ]
+    pulled = norm_back_rows(second_resid[...], gains[1], second_grad[...])
+    pull[...] = pulled
+    fetches[CROSS_OUT_AT].wait()
+    cross_grad[...] = dot_right(pulled.astype(BF16), weight(CROSS_OUT_AT)).reshape(2, S_DEV, D)
+    fetches["pairs"].wait()
+
+    cross_pad = lax.broadcasted_iota(jnp.int32, (64, S_DEV), 0) % 32
+    for at_row in range(2):
+        lines = [sum(docs_all[4 * at + k, 2 + at_row:3 + at_row] for k in range(4)) for at in range(4)]
+        key_docs = jnp.concatenate(
+            [jnp.transpose(jnp.broadcast_to(line, (S_DEV, LANES))) for line in lines], axis=0
+        )
+        allowed = key_docs == docs[at_row:at_row + 1]
+
+        def one_pair(at_pair, carry):
+            first = pl.multiple_of(at_pair * LANES, LANES)
+            columns, value_columns = pl.ds(first, LANES), pl.ds(pl.multiple_of(first + D, LANES), LANES)
+            heads = cross_queries[at_row, :, columns]
+            grad = cross_grad[at_row, :, columns] * cross_inverse[at_row, :, columns]
+            low = grad.astype(BF16)
+            lines = rows_in_lanes(grad * crossed[at_row, :, columns])
+
+            def head_rows(count):
+                return jnp.concatenate(
+                    [jnp.broadcast_to(lines[0:1], (count, S_DEV)), jnp.broadcast_to(lines[1:2], (count, S_DEV))],
+                    axis=0,
+                )
+
+            prefix_key_stack = stack_heads(small_full[at_pair, 64:96])
+            prefix_value_stack = stack_heads(small_full[at_pair, 96:128])
+            e = jnp.exp(dot_right(prefix_key_stack, heads) * score_scale)
+            e = jnp.where(cross_pad < PREFIX, e, 0.0)
+            slopes = (e * (dot_right(prefix_value_stack, low) - head_rows(32))).astype(BF16)
+            from_prefix = dot_left(slopes, prefix_key_stack)
+            key_grad = merge_heads(dot_nn(slopes, heads)) * score_scale
+            value_grad = merge_heads(dot_nn(e.astype(BF16), low))
+            if at_row == 0:
+                cross_prefix[at_pair, 0] = key_grad
+                cross_prefix[at_pair, 1] = value_grad
+            else:
+                cross_prefix[at_pair, 0] += key_grad
+                cross_prefix[at_pair, 1] += value_grad
+            key_stack = stack_heads(memory_pairs[:, at_row, :, columns].reshape(memory_len, LANES))
+            value_stack = stack_heads(memory_pairs[:, at_row, :, value_columns].reshape(memory_len, LANES))
+            e = jnp.exp(dot_right(key_stack, heads) * score_scale).reshape(2, memory_len, S_DEV)
+            e = jnp.where(allowed[None], e, 0.0).reshape(2 * memory_len, S_DEV)
+            slopes = (e * (dot_right(value_stack, low) - head_rows(memory_len))).astype(BF16)
+            terms = merge_heads(dot_nn(slopes, heads)) * score_scale
+            key_terms[:, at_row, :, columns] = terms.astype(BF16).reshape(16, M_DEV, LANES)
+            terms = merge_heads(dot_nn(e.astype(BF16), low))
+            value_terms[:, at_row, :, columns] = terms.astype(BF16).reshape(16, M_DEV, LANES)
+            query_grad = (from_prefix + dot_left(slopes, key_stack)) * score_scale
+            cross_query_grad[at_row, :, columns] = query_grad.astype(BF16)
+            return carry
+
+        lax.fori_loop(0, PAIRS, one_pair, 0)
+        if at_row == 0:
+            small_own.wait()
+            small_first.wait_recv()
+            small_mine[...] = small_mine[...] + small_core[...]
+            small_second.start()
+    small_second.wait()
+    small_pair[...] = small_mine[:, :, x] + small_x[...]
+    for copy in small_third:
+        copy.start()
+    small_all[plane] = small_pair[z, y]
+
+    prefix_copies = []
+    for k in range(1, 8):
+        to = (pair + k) % 8
+        prefix_copies.append(
+            remote(cross_prefix.at[to], prefix_all.at[pair], prefix_send.at[k], prefix_recv.at[k], (to * 2 + core, x))
+        )
+        prefix_copies[-1].start()
+    prefix_all[pair] = cross_prefix[pair]
+
+    fetches[CROSS_Q_AT].wait()
+    fetches["resid"].wait()
+    first_grad = pull[...] + dot_right(cross_query_grad[...].reshape(tokens, D), weight(CROSS_Q_AT))
+    resid_grad = norm_back_rows(first_resid[...], gains[0], first_grad)
+    pull[...] = resid_grad
+    fetches[SELF_OUT_AT].wait()
+    out_grad = dot_right(resid_grad.astype(BF16), weight(SELF_OUT_AT)).astype(BF16)
+    for at_pair in range(PAIRS):
+        for at_row in range(2):
+            heads_out[at_pair, at_row] = out_grad[
+                at_row * S_DEV:(at_row + 1) * S_DEV, at_pair * LANES:(at_pair + 1) * LANES
+            ]
     arrivals = []
-    for step in range(1, 16):
-        to = (seq + step) % 16
-        arrivals.append(remote(heads_for(to), grads.at[seq], in_send.at[step], in_recv.at[step], (to, x)))
+    for k in range(15):
+        to = (seq + k + 1) % 16
+        arrivals.append(remote(heads_out.at[to // 2, to % 2], grads.at[seq], in_send.at[k], in_recv.at[k], others[k]))
         arrivals[-1].start()
-    own.wait()
+    own_heads = pltpu.make_async_copy(heads_out.at[pair, row], grads.at[seq], own_sem.at[1])
+    own_heads.start()
+
+    fetches[MEM_K_AT].wait()
+    fetches[MEM_V_AT].wait()
+
+    def memory_block(at, carry):
+        there = pl.ds(4 * at, 4)
+        terms = dot_right(key_terms[there].reshape(8 * M_DEV, D), weight(MEM_K_AT))
+        terms += dot_right(value_terms[there].reshape(8 * M_DEV, D), weight(MEM_V_AT))
+        memory_part[at] = terms.astype(BF16).reshape(2, 2, 2 * M_DEV, D)
+        return carry
+
+    lax.fori_loop(0, 4, memory_block, 0)
+    memory_first.start()
+    for copy in small_third:
+        copy.wait()
+    total = small_all[0].astype(F32)
+    for k in range(1, 8):
+        total += small_all[k].astype(F32)
+    down_grad[...] = total[:, :ADAPTER]
+    up_grad[:, :ADAPTER] = total[:16, ADAPTER:]
+    up_grad[:, ADAPTER:] = total[16:, ADAPTER:]
+    for name in ("arrived", "attended", "inverse", "docs"):
+        fetches[name].wait()
+    own_heads.wait()
     for copy in arrivals:
         copy.wait()
 
     pad_row = lax.broadcasted_iota(jnp.int32, (64, block), 0) % 32
-    prefix_key_stack = stack_heads(prefix_keys[...])
-    prefix_value_stack = stack_heads(prefix_values[...])
+    prefix_key_stack = stack_heads(small_full[pair, 0:32])
+    prefix_value_stack = stack_heads(small_full[pair, 32:64])
 
     def head_rows(at, count):
         there = delta[:, pl.ds(pl.multiple_of(at * block, block), block)]
@@ -1124,7 +1301,7 @@
             axis=0,
         )
 
-    prefix_grads[...] = jnp.zeros(prefix_grads.shape, F32)
+    prefix_mine[...] = jnp.zeros(prefix_mine.shape, F32)
 
     def prepare(at, carry):
         here = pl.ds(at * block, block)
@@ -1133,15 +1310,32 @@
         grad_low[here] = low
         delta[:, pl.ds(pl.multiple_of(at * block, block), block)] = rows_in_lanes(grad * attended[here])
         queries = arrived[pl.ds(2 * at, 2), 0].reshape(block, LANES)
-        weights = jnp.exp(dot_right(prefix_key_stack, queries) * score_scale)
-        weights = jnp.where(pad_row < PREFIX, weights, 0.0)
-        slopes = (weights * (dot_right(prefix_value_stack, low) - head_rows(at, 32))).astype(BF16)
-        prefix_grads[0] += merge_heads(dot_nn(slopes, queries)) * score_scale
-        prefix_grads[1] += merge_heads(dot_nn(weights.astype(BF16), low))
+        e = jnp.exp(dot_right(prefix_key_stack, queries) * score_scale)
+        e = jnp.where(pad_row < PREFIX, e, 0.0)
+        slopes = (e * (dot_right(prefix_value_stack, low) - head_rows(at, 32))).astype(BF16)
+        prefix_mine[0] += merge_heads(dot_nn(slopes, queries)) * score_scale
+        prefix_mine[1] += merge_heads(dot_nn(e.astype(BF16), low))
         query_grads[here] = dot_left(slopes, prefix_key_stack)
         return carry
 
     lax.fori_loop(0, 8, prepare, 0)
+    memory_first.wait()
+    memory_mine[...] = memory_part[:, :, core] + memory_core[...]
+    for copy in memory_second:
+        copy.start()
+    memory_all[plane] = memory_mine[z, y]
+    for copy in prefix_copies:
+        copy.wait()
+    for part in range(2):
+        prefix_mine[2 + part] = sum(prefix_all[k, part] for k in range(8))
+    prefix_quad[core * 2 + x] = prefix_mine[...]
+    quad_copies = [
+        remote(prefix_mine, prefix_quad.at[core * 2 + x], quad_send.at[k], quad_recv.at[k], peer)
+        for k, peer in enumerate((place.other_core(), place.along_x(), place.diagonal()))
+    ]
+    for copy in quad_copies:
+        copy.start()
+
     away = (
         lax.broadcasted_iota(jnp.int32, (block, block), 0)
         - lax.broadcasted_iota(jnp.int32, (block, block), 1)
@@ -1159,10 +1353,10 @@
 
             @pl.when(to == seq)
             def _():
-                pltpu.make_async_copy(source, mine, local_sem.at[1 + part]).start()
+                pltpu.make_async_copy(source, mine, own_sem.at[2 + part]).start()
 
     def one_block(step, carry):
-        key_at = (step + seq // 2) % 8
+        key_at = (step + pair) % 8
         keys = stack_heads(arrived[pl.ds(2 * key_at, 2), 1].reshape(block, LANES))
         values = stack_heads(arrived[pl.ds(2 * key_at, 2), 2].reshape(block, LANES))
         key_docs = docs_column[pl.ds(key_at * block, block)]
@@ -1176,11 +1370,11 @@
             low = grad_low[here]
             query_docs = docs_row[0:1, pl.ds(pl.multiple_of(at * block, block), block)]
             allowed = (key_docs == query_docs) & (away <= (at - key_at) * block)
-            weights = jnp.exp(dot_right(keys, queries) * score_scale).reshape(2, block, block)
-            weights = jnp.where(allowed[None], weights, 0.0).reshape(2 * block, block)
-            slopes = (weights * (dot_right(values, low) - head_rows(at, block))).astype(BF16)
+            e = jnp.exp(dot_right(keys, queries) * score_scale).reshape(2, block, block)
+            e = jnp.where(allowed[None], e, 0.0).reshape(2 * block, block)
+            slopes = (e * (dot_right(values, low) - head_rows(at, block))).astype(BF16)
             key_grads[...] += dot_nn(slopes, queries)
-            value_grads[...] += dot_nn(weights.astype(BF16), low)
+            value_grads[...] += dot_nn(e.astype(BF16), low)
             query_grads[here] += dot_left(slopes, keys)
             return carry
 
@@ -1194,38 +1388,89 @@
     lax.fori_loop(0, 8, one_block, 0)
 
     def last_block(step, carry):
-        at = (step + seq // 2) % 8
+        at = (step + pair) % 8
         result = (query_grads[pl.ds(at * block, block)] * score_scale).astype(BF16)
         staged[pl.ds(2 * at, 2), 0] = result.reshape(2, S_DEV, LANES)
         send_block(0, 1, at, query_send, query_recv)
         return carry
 
     lax.fori_loop(0, 8, last_block, 0)
-    pltpu.make_async_copy(staged.at[seq, pl.ds(1, 2)], gathered.at[pair, row, pl.ds(1, 2)], local_sem.at[2]).wait()
-    pltpu.make_async_copy(staged.at[seq, pl.ds(0, 1)], gathered.at[pair, row, pl.ds(0, 1)], local_sem.at[1]).wait()
-    for step in range(1, 16):
-        other = (seq + step) % 16
-        mine = gathered.at[other // 2, other % 2]
+    small_first.wait_send()
+    for copy in memory_second:
+        copy.wait()
+    total = memory_all[0].astype(F32)
+    for k in range(1, 8):
+        total += memory_all[k].astype(F32)
+    memory_grad[...] = total
+    for copy in quad_copies:
+        copy.wait()
+    prefix_sum[...] = (prefix_quad[0] + prefix_quad[1]) + (prefix_quad[2] + prefix_quad[3])
+
+    pltpu.make_async_copy(staged.at[seq, pl.ds(1, 2)], gathered.at[pair, row, pl.ds(1, 2)], own_sem.at[3]).wait()
+    for other, _ in others:
         remote(
-            staged.at[other, pl.ds(1, 2)], mine.at[pl.ds(1, 2)], out_send.at[other], out_recv.at[other], (other, x)
+            staged.at[other, pl.ds(1, 2)], gathered.at[other // 2, other % 2, pl.ds(1, 2)],
+            out_send.at[other], out_recv.at[other], (other, x),
         ).wait()
+
+    def part_grad(part, at):
+        fetches[at].wait()
+        joined = jnp.concatenate([gathered[k, :, part].reshape(tokens, LANES) for k in range(PAIRS)], axis=1)
+        return dot_right(joined, weight(at))
+
+    input_grad[...] = pull[...] + part_grad(1, K_AT) + part_grad(2, V_AT)
+    pltpu.make_async_copy(staged.at[seq, pl.ds(0, 1)], gathered.at[pair, row, pl.ds(0, 1)], own_sem.at[2]).wait()
+    for other, _ in others:
         remote(
-            staged.at[other, pl.ds(0, 1)], mine.at[pl.ds(0, 1)], query_send.at[other], query_recv.at[other], (other, x)
+            staged.at[other, pl.ds(0, 1)], gathered.at[other // 2, other % 2, pl.ds(0, 1)],
+            query_send.at[other], query_recv.at[other], (other, x),
         ).wait()
-
-
-def self_backward(arrived, grad_out, attended, inverse, docs_row, docs_column, prefix_keys, prefix_values):
+    input_grad[...] += part_grad(0, Q_AT)
+
+
+def second_call(*operands):
     length = 16 * S_DEV
+    tokens = 2 * S_DEV
     dma = pltpu.SemaphoreType.DMA
+    shape = jax.ShapeDtypeStruct
     return pl.pallas_call(
-        self_backward_kernel,
+        second_kernel,
         out_shape=(
-            jax.ShapeDtypeStruct((PAIRS, 2, 3, S_DEV, LANES), BF16),
-            jax.ShapeDtypeStruct((2, 32, LANES), F32),
+            shape((tokens, D), F32),
+            shape((2 * M_DEV, D), F32),
+            shape((32, ADAPTER), F32),
+            shape((16, D), F32),
+            shape((4, 32, LANES), F32),
         ),
-        in_specs=[whole()] * 8,
-        out_specs=(whole(), whole()),
+        in_specs=[whole()] * 9 + [whole(pl.ANY)] * 8,
+        out_specs=(whole(),) * 5,
         scratch_shapes=[
+            pltpu.VMEM((8, 32, 32, D), BF16),
+            pltpu.VMEM((16, 2, M_DEV, 2 * D), BF16),
+            pltpu.VMEM((tokens, D), F32),
+            pltpu.VMEM((16, 3, S_DEV, LANES), BF16),
+            pltpu.VMEM((length, LANES), F32),
+            pltpu.VMEM((length, LANES), F32),
+            pltpu.VMEM((length, LANES), F32),
+            pltpu.VMEM((tokens, D), F32),
+            pltpu.VMEM((2, S_DEV, D), F32),
+            pltpu.VMEM((2, S_DEV, D), BF16),
+            pltpu.VMEM((16, 2, M_DEV, D), BF16),
+            pltpu.VMEM((16, 2, M_DEV, D), BF16),
+            pltpu.VMEM((PAIRS, 2, 32, LANES), F32),
+            pltpu.VMEM((4, 2, 2, 32, D), BF16),
+            pltpu.VMEM((4, 2, 2, 32, D), BF16),
+            pltpu.VMEM((4, 2, 32, D), BF16),
+            pltpu.VMEM((4, 2, 32, D), BF16),
+            pltpu.VMEM((8, 32, D), BF16),
+            pltpu.VMEM((4, 2, 2, 2 * M_DEV, D), BF16),
+            pltpu.VMEM((4, 2, 2 * M_DEV, D), BF16),
+            pltpu.VMEM((4, 2, 2 * M_DEV, D), BF16),
+            pltpu.VMEM((8, 2 * M_DEV, D), BF16),
+            pltpu.VMEM((8, 2, 32, LANES), F32),
+            pltpu.VMEM((4, 32, LANES), F32),
+            pltpu.VMEM((4, 4, 32, LANES), F32),
+            pltpu.VMEM((PAIRS, 2, S_DEV, LANES), BF16),
             pltpu.VMEM((16, S_DEV, LANES), BF16),
             pltpu.VMEM((length, LANES), BF16),
             pltpu.VMEM((8, length), F32),
@@ -1233,86 +1478,14 @@
             pltpu.VMEM((4 * S_DEV, LANES), F32),
             pltpu.VMEM((4 * S_DEV, LANES), F32),
             pltpu.VMEM((16, 3, S_DEV, LANES), BF16),
-            dma((3,)), dma((16,)), dma((16,)), dma((16,)), dma((16,)), dma((16,)), dma((16,)),
+            pltpu.VMEM((PAIRS, 2, 3, S_DEV, LANES), BF16),
+            dma((14,)), dma((4,)), dma((3,)), dma((3,)), dma((8,)), dma((8,)), dma((8,)), dma((8,)),
+            dma((8,)), dma((8,)), dma((3,)), dma((3,)),
+            dma((15,)), dma((15,)), dma((16,)), dma((16,)), dma((16,)), dma((16,)),
         ],
-        compiler_params=params(3),
-        name="self_backward",
-    )(arrived, grad_out, attended, inverse, docs_row, docs_column, prefix_keys, prefix_values)
-
-
-def cross_backward_kernel(
-    queries, keys, values, query_docs, key_docs, prefix_keys, prefix_values, grad_out, crossed, inverse,
-    query_grad, key_grad, value_grad, prefix_grads,
-):
-    row = pl.program_id(1)
-    memory_len = keys.shape[0] * keys.shape[2]
-    heads = queries[0]
-    grad = grad_out[0] * inverse[0]
-    low = grad.astype(BF16)
-    delta = rows_in_lanes(grad * crossed[0])
-
-    def head_rows(count):
-        return jnp.concatenate(
-            [jnp.broadcast_to(delta[0:1], (count, S_DEV)), jnp.broadcast_to(delta[1:2], (count, S_DEV))],
-            axis=0,
-        )
-
-    pad_row = lax.broadcasted_iota(jnp.int32, (64, S_DEV), 0) % 32
-    prefix_key_stack = stack_heads(prefix_keys[...])
-    weights = jnp.exp(dot_right(prefix_key_stack, heads) * score_scale)
-    weights = jnp.where(pad_row < PREFIX, weights, 0.0)
-    slopes = (weights * (dot_right(stack_heads(prefix_values[...]), low) - head_rows(32))).astype(BF16)
-    from_prefix = dot_left(slopes, prefix_key_stack)
-    prefix_key_grad = merge_heads(dot_nn(slopes, heads)) * score_scale
-    prefix_value_grad = merge_heads(dot_nn(weights.astype(BF16), low))
-
-    @pl.when(row == 0)
-    def _():
-        prefix_grads[0] = prefix_key_grad
-        prefix_grads[1] = prefix_value_grad
-
-    @pl.when(row > 0)
-    def _():
-        prefix_grads[0] += prefix_key_grad
-        prefix_grads[1] += prefix_value_grad
-
-    key_stack = stack_heads(keys[...].reshape(memory_len, LANES))
-    value_stack = stack_heads(values[...].reshape(memory_len, LANES))
-    allowed = key_docs[0] == query_docs[0]
-    weights = jnp.exp(dot_right(key_stack, heads) * score_scale).reshape(2, memory_len, S_DEV)
-    weights = jnp.where(allowed[None], weights, 0.0).reshape(2 * memory_len, S_DEV)
-    slopes = (weights * (dot_right(value_stack, low) - head_rows(memory_len))).astype(BF16)
-    key_grad[...] = (merge_heads(dot_nn(slopes, heads)) * score_scale).astype(BF16).reshape(key_grad.shape)
-    value_grad[...] = merge_heads(dot_nn(weights.astype(BF16), low)).astype(BF16).reshape(value_grad.shape)
-    query_grad[0] = ((from_prefix + dot_left(slopes, key_stack)) * score_scale).astype(BF16)
-
-
-def cross_backward(queries, memory_pairs, query_docs, key_docs, prefix_keys, prefix_values, grad_out, crossed, inverse):
-    memory_len = 16 * M_DEV
-    head_block = pl.BlockSpec((1, S_DEV, LANES), lambda pair, row: (row, 0, pair))
-    keys = pl.BlockSpec((16, 1, M_DEV, LANES), lambda pair, row: (0, row, 0, pair))
-    values = pl.BlockSpec((16, 1, M_DEV, LANES), lambda pair, row: (0, row, 0, PAIRS + pair))
-    prefix = pl.BlockSpec((32, LANES), lambda pair, row: (0, pair))
-    terms = jax.ShapeDtypeStruct((16, 2, M_DEV, D), BF16)
-    return pl.pallas_call(
-        cross_backward_kernel,
-        grid=(PAIRS, 2),
-        out_shape=(
-            jax.ShapeDtypeStruct((2, S_DEV, D), BF16), terms, terms,
-            jax.ShapeDtypeStruct((2, 32, D), F32),
-        ),
-        in_specs=[
-            head_block, keys, values,
-            pl.BlockSpec((1, 1, S_DEV), lambda pair, row: (row, 0, 0)),
-            pl.BlockSpec((1, memory_len, LANES), lambda pair, row: (row, 0, 0)),
-            prefix, prefix, head_block, head_block, head_block,
-        ],
-        out_specs=(
-            head_block, keys, keys, pl.BlockSpec((2, 32, LANES), lambda pair, row: (0, 0, pair)),
-        ),
-        compiler_params=params(),
-        name="cross_backward",
-    )(queries, memory_pairs, memory_pairs, query_docs, key_docs, prefix_keys, prefix_values, grad_out, crossed, inverse)
+        compiler_params=params(1),
+        name="second",
+    )(*operands)
 
 
 def gelu_parts(pre):
@@ -1444,76 +1617,23 @@
         self_project, self_output, cross_query, cross_memory, cross_output, inner_weight, outer_weight, mixed,
     )
 
-    def weight(first):
-        return full[:, first:first + 32].reshape(D, D)
-
-    gains = small_full[:, 128:131].transpose(1, 0, 2).reshape(3, D).astype(F32)
-    cross_prefixes = small_full[:, 64:128].reshape(8, 2, 32, LANES).transpose(1, 2, 0, 3).reshape(2, 32, D)
-    pair_prefixes = lax.dynamic_index_in_dim(small_full, seq // 2, 0, False)[:64].reshape(2, 32, LANES)
-    memory_row = docs_all[:, 2:4].reshape(4, 4, 2, LANES).sum(axis=1).transpose(1, 0, 2).reshape(2, 1, 16 * M_DEV)
-    memory_column = jnp.broadcast_to(memory_row.reshape(2, -1, 1), (2, 16 * M_DEV, LANES))
-    query_row = token_docs.astype(F32).reshape(2, 1, S_DEV)
-
+    third_gain = small_full[:, 130].reshape(1, D).astype(F32)
     layer_out, second_grad, small_grads = feed_forward_backward(
-        second_norm, out_grad.reshape(tokens, D), gains[2:3], full
-    )
-    small_sums = lax.psum_scatter(small_grads.reshape(1024, D), "seq", scatter_dimension=0, tiled=True)
-
-    second_resid_grad = norm_back_rows(second_resid, gains[1], second_grad)
-    cross_out_grad = dot_right(second_resid_grad.astype(BF16), weight(CROSS_OUT_AT))
-    cross_query_grad, key_terms, value_terms, cross_prefix_grads = cross_backward(
-        cross_queries, memory_pairs, query_row, memory_column, cross_prefixes[0], cross_prefixes[1],
-        cross_out_grad.reshape(2, S_DEV, D), crossed, cross_inverse,
-    )
-    memory_terms = dot_right(key_terms.reshape(-1, D), weight(MEM_K_AT)) + dot_right(
-        value_terms.reshape(-1, D), weight(MEM_V_AT)
-    )
-    prefix_flat = cross_prefix_grads[:, :PREFIX].reshape(2 * PREFIX, 16, 64).transpose(1, 0, 2).reshape(16, -1)
-    prefix_flat = jnp.pad(prefix_flat, ((0, 0), (0, 8 * D - prefix_flat.shape[1]))).reshape(16, 8, D)
-    memory_terms = jnp.concatenate(
-        [memory_terms.astype(BF16).reshape(16, 64, D), prefix_flat.astype(BF16)], axis=1
-    )
-    memory_sums = lax.psum_scatter(memory_terms, "seq", scatter_dimension=0, tiled=False)
-
-    first_grad = second_resid_grad + dot_right(cross_query_grad.reshape(tokens, D), weight(CROSS_Q_AT))
-    first_resid_grad = norm_back_rows(first_resid, gains[0], first_grad)
-    self_out_grad = dot_right(first_resid_grad.astype(BF16), weight(SELF_OUT_AT))
-    project_grads, self_prefix_grads = self_backward(
-        arrived, self_out_grad.astype(BF16).reshape(2, S_DEV, D), pair_attended, pair_inverse,
-        docs_row, docs_column, pair_prefixes[0], pair_prefixes[1],
-    )
-    project_grads = project_grads.transpose(2, 1, 3, 0, 4).reshape(3, tokens, D)
-    input_grad = first_resid_grad
-    for part in range(3):
-        input_grad = input_grad + dot_right(project_grads[part], weight(32 * part))
-
-    def swapped(values):
-        return lax.ppermute(values, "rows", [(0, 1), (1, 0)])
-
-    halves = small_sums.astype(F32).reshape(2, 32, D)
-    give = lax.dynamic_index_in_dim(halves, 1 - x, 0, False)
-    keep = lax.dynamic_index_in_dim(halves, x, 0, False)
-    prefix_half = memory_sums[64:].astype(F32).reshape(-1)[:60 * 64].reshape(60, 2, 32)
-    cross_give = lax.dynamic_index_in_dim(prefix_half, 1 - x, 1, False)
-    cross_keep = lax.dynamic_index_in_dim(prefix_half, x, 1, False)
-    pair_sum = self_prefix_grads + lax.ppermute(
-        self_prefix_grads, "seq", [(at, at ^ 1) for at in range(16)]
-    )
-    pair_sum = pair_sum[:, :PREFIX].reshape(60, 2, 2, 32)
-    pair_sum = lax.dynamic_index_in_dim(pair_sum, seq % 2, 1, False)
-    self_give = lax.dynamic_index_in_dim(pair_sum, 1 - x, 1, False)
-    self_keep = lax.dynamic_index_in_dim(pair_sum, x, 1, False)
-    keep = keep + swapped(give)
-    prefix_grad = jnp.concatenate([self_keep, cross_keep], axis=0) + swapped(
-        jnp.concatenate([self_give, cross_give], axis=0)
-    )
+        second_norm, out_grad.reshape(tokens, D), third_gain, full
+    )
+    input_grad, memory_grad, down_grad, up_grad, prefix_sum = second_call(
+        second_grad, second_resid, small_full, docs, docs_all, docs_row, crossed, cross_inverse, cross_queries,
+        full, memory_pairs, first_resid, arrived, pair_attended, pair_inverse, docs_column,
+        small_grads.reshape(4, 2, 2, 2, 32, D),
+    )
+    prefix_grad = lax.dynamic_slice_in_dim(prefix_sum[:, :PREFIX], 32 * ((seq % 2) * 2 + x), 32, 2)
     return (
         layer_out.reshape(2, S_DEV, D),
         input_grad.reshape(2, S_DEV, D),
-        memory_sums[:64].astype(F32).reshape(2, M_DEV, D),
-        prefix_grad.reshape(4, PREFIX, 32),
-        keep[:, :ADAPTER],
-        jnp.concatenate([keep[:16, ADAPTER:], keep[16:, ADAPTER:]], axis=1),
+        memory_grad.reshape(2, M_DEV, D),
+        prefix_grad,
+        down_grad,
+        up_grad,
     )
 
 

time: 447 us -> 395 us (0.88); the launches traced: 438 us -> 393 us
  Pallas kernels: 357 us -> 379 us
  local copies, waits for them, and re-layouts: 30.2 us -> 9.37 us
  matrix products: 17 us -> 0 us
  between operations: 14.9 us -> 0.73 us
  other arithmetic: 12.1 us -> 4.7 us
  waiting for transfers between devices: 5.81 us -> 0 us
    pallas_call x2 -> x1, Pallas kernels: 99.4 us -> 121 us  [second_call(): pl.pallas_call(second_kernel, out_shape=(shape((tokens, D), F32), shape((...]
    slice x13 -> x0, local copies, waits for them, and re-layouts: 18.1 us -> none  [the longest x1 11.8 us: weight(): return full[:, first:first + 32].reshape(D, D)]
    dot_general x8 -> x0, matrix products: 17 us -> none  [dot_right(): lax.dot_general(left, right, (((1,), (1,)), ((), ())), preferred_element_...]
    ppermute x3 -> x0, waiting for transfers between devices: 5.75 us -> none  [the longest x2 5.75 us: swapped(): return lax.ppermute(values, 'rows', [(0, 1), (1, 0)])]
  transfers between devices with their start and end apart: 5 -> 0, of which waited for: 2 -> 0; matrix products, arithmetic and copies ran while one was open for 10% -> 0% of each run, Pallas kernels for 23% -> 0%
where the time goes in v3:
time: 395 us; the launch traced here: 393 us
  Pallas kernels  379 us (96%)
  local copies, waits for them, and re-layouts  9.37 us (2%)
  other arithmetic  4.7 us (1%)
    pallas_call x1, Pallas kernels, first_call(): pl.pallas_call(first_kernel, out_shape=(shape((4, 2, 2, 2, ALL_ROWS, D),...  235 us
    pallas_call x1, Pallas kernels, second_call(): pl.pallas_call(second_kernel, out_shape=(shape((tokens, D), F32), shape((...  121 us
    pallas_call x1, Pallas kernels, feed_forward_backward(): pl.pallas_call(feed_kernel, grid=(8,), out_shape=(jax.ShapeDtypeStruct((t...  22.8 us

profile of v3, /device:TPU:28, one launch (start us, length us, event | category | flops | bytes accessed | tf_op | source)
XLA Modules:
  0.0 393.5 jit_solution(11535283982199491412)
XLA Ops:
  0.6 0.8 copy.24
  1.4 0.9 copy.27
  2.3 0.1 reshape.97
  2.4 0.1 copy.25
  2.6 0.6 broadcast_select_fusion.small
  3.2 0.7 tile.20
  3.9 0.1 tile.21
  4.0 0.1 pad.15.clone
  4.0 1.3 add_convert_fusion.docs
  5.4 0.7 fusion.2
  6.1 1.4 maximum_maximum_fusion.mixed
  7.5 234.8 %first.1 = (bf16[4,2,2,2,544,1024]{5,4,3,2,1,0:T(8,128)(2,1)}, bf16[4,2,2,2,32,1024]{5,4,3,2,1,0:T(8,128)(2,1)}, bf16[16,2,32,2048]{3,2,1,0:T(8,128)(2,1)}, bf16...) custom-call(bf16[2,128,1024]{2,1,0:T(8,128)(2,1)} %tokens.1, ...), custom_call_target="tpu_custom_call" | custom-call | tf_op jit(solution)/shard_map/first/pallas_call | solution.py:1047
  242.4 1.3 bitcast_convert_fusion.gain
  243.7 22.8 %feed.1 = (bf16[256,1024]{1,0:T(8,128)(2,1)}, f32[256,1024]{1,0:T(8,128)}, bf16[32,32,1024]{2,1,0:T(8,128)(2,1)}) custom-call(f32[256,1024]{1,0:T(8,128)} %get-tuple-element.29.normed, bf16[256,1024]{1,0:T(8,128)(2,1)} %bitcast.19, f32[1,1024]{1,0:T(1,128)} %bitcast_convert_fusion.gain, bf16[32,544,1024]{2,1,0:T(8,128)(2,1)} %bitcast.13, ...), custom_call_target="tpu_custom_call" | custom-call | tf_op jit(solution)/shard_map/feed/pallas_call | solution.py:1569
  266.5 121.0 %second.1 = (f32[256,1024]{1,0:T(8,128)}, f32[64,1024]{1,0:T(8,128)}, f32[32,512]{1,0:T(8,128)}, f32[16,1024]{1,0:T(8,128)}, f32[4,32,128]{2,1,0:T(8,128)}) custom-call(f32[256,1024]{1,0:T(8,128)} %get-tuple-element.33.second_grad, f32[256,1024]{1,0:T(8,128)} %get-tuple-element.34.second_resid, bf16[8,144,128]{2,1,0:T(8,128)(2,1)} %get-tuple-element.30.small_full, ...), custom_call_target="tpu_custom_call" | custom-call | tf_op jit(solution)/shard_map/second/pallas_call | solution.py:1436
  387.5 0.0 copy-start
  387.5 0.0 copy-start.2
  387.5 0.0 copy-start.1
  387.5 1.0 constant_dynamic-slice_fusion
  388.5 0.7 copy.26
  389.2 2.3 copy.32
  391.5 0.0 copy-done
  391.5 0.7 copy.33
  392.2 0.0 copy-done.2
  392.2 0.6 copy.34
  392.8 0.0 copy-done.1
  392.8 0.6 copy.35
  (7 shorter events, 0.1 us)
Async XLA Ops:
  387.5 4.0 %copy-start = (f32[64,1024]{1,0:T(8,128)S(1)}, f32[64,1024]{1,0:T(8,128)}, u32[]{:S(2)}) copy-start(f32[64,1024]{1,0:T(8,128)} %get-tuple-element.48) | copy-start | bytes 786436
  387.5 4.7 %copy-start.2 = (f32[32,512]{1,0:T(8,128)S(1)}, f32[32,512]{1,0:T(8,128)}, u32[]{:S(2)}) copy-start(f32[32,512]{1,0:T(8,128)} %get-tuple-element.76) | copy-start | bytes 196612
  387.5 5.3 %copy-start.1 = (f32[16,1024]{1,0:T(8,128)S(1)}, f32[16,1024]{1,0:T(8,128)}, u32[]{:S(2)}) copy-start(f32[16,1024]{1,0:T(8,128)} %get-tuple-element.77) | copy-start | bytes 196612

commit v4 on v3

--- a/solution.py
+++ b/solution.py
@@ -600,7 +600,7 @@
 ALL_ROWS = 544
 SMALL_ROWS = 144
 PIECE_ROWS = 16
-GAP = 2
+GAP = 3
 LEAD = 4
 SENDS = 2
 Z_LAST = ()
@@ -671,6 +671,7 @@
         self.place, self.full, self.local_sem, self.sems, self.gap = place, full, local_sem, sems, gap
         self.stages = []
         self.waiting = []
+        self.cut = 1
         self.tick_at = 0
 
     def copies(self, level, source, target, device, slot):
@@ -700,7 +701,7 @@
                 [self.copies(3, full.at[:, :, core, :, rows], full.at[:, :, core, :, rows], at.other_core(), 0)],
             ))
             return
-        cut = 2 if k % 3 == 0 else 1
+        cut = self.cut
         near, far = pl.ds(0, cut), pl.ds(cut, 4 - cut)
         near1, far1 = full.at[near, y, core, x, rows], full.at[far, y, core, x, rows]
         near2, far2 = full.at[near, y, core, :, rows], full.at[far, :, core, x, rows]
@@ -712,11 +713,6 @@
             [self.copies(2, near2, near2, at.along_y(), 0), self.copies(2, far2, far2, at.along_x(), 1)],
             [self.copies(3, half, half, at.other_core(), 0)],
         ))
-
-    def add_memory(self, source, full):
-        for row in range(2):
-            self.add_memory_row(source.at[row], full.at[:, :, :, row])
-        return len(self.stages) - 1
 
     def add_memory_row(self, source, full):
         at = self.place
@@ -797,13 +793,22 @@
 def first_kernel(
     tokens, memory, small, docs,
     project, self_out, cross_q, cross_mem, cross_out, inner, outer, mixed,
-    full, memory_full, memory_pairs, small_full, docs_all, docs_row, docs_column, arrived, attended, inverse,
-    first_resid, cross_queries, crossed, cross_inverse, second_resid, second_norm,
+    full, memory_full, memory_pairs_far, docs_column_far, arrived_far, attended_far, inverse_far,
+    first_resid_far, cross_queries_far, crossed_far, cross_inverse_far,
+    small_full, docs_all, docs_row, second_resid, second_norm,
+    memory_pairs, docs_column, arrived, attended, inverse, first_resid, cross_queries, crossed, cross_inverse,
     gathered, first_norm, weights, staged, quad, memory_held, result_staged, sums, parts,
     local_sem, send0, recv0, send1, recv1, send2, recv2, send3, recv3,
     fetch_sem, own_sem, quad_send, quad_recv, small_send, small_recv, docs_send, docs_recv,
-    head_send, head_recv, out_send, out_recv,
+    head_send, head_recv, out_send, out_recv, leave_sem,
 ):
+    leaving = []
+
+    def leave(*arrays):
+        for held, target in arrays:
+            leaving.append(pltpu.make_async_copy(held, target, leave_sem.at[len(leaving)]))
+            leaving[-1].start()
+
     place = Place()
     seq, x, pair, row = place.seq, place.x, place.pair, place.row
     others = place.others()
@@ -814,12 +819,15 @@
     project_done = [
         engine.add(project.at[:, pl.ds(part * D, D)], at, 32) for part, at in enumerate((Q_AT, K_AT, V_AT))
     ]
-    engine.add_memory(memory, memory_full)
     for part, at in enumerate((MEM_K_AT, MEM_V_AT)):
-        memory_done = engine.add(cross_mem.at[:, pl.ds(part * D, D)], at, 32)
+        for half in range(2):
+            held = pl.ds(16 * half, 16)
+            engine.add_memory_row(memory.at[part, held], memory_full.at[:, :, :, part, held])
+            memory_done = engine.add(cross_mem.at[held, pl.ds(part * D, D)], at + 16 * half, 16)
     out_done = engine.add(self_out, SELF_OUT_AT, 32)
     query_done = engine.add(cross_q, CROSS_Q_AT, 32)
     cross_done = engine.add(cross_out, CROSS_OUT_AT, 32)
+    engine.cut = 2
     for part in range(4):
         engine.add(inner.at[:, pl.ds(part * D, D)], INNER_AT + 32 * part, 32)
     for part in range(4):
@@ -841,7 +849,31 @@
     own_docs.start()
     for copy in quad_copies + docs_copies:
         copy.start()
-    engine.tick()
+    rows = tokens[...].reshape(2 * S_DEV, D)
+    fetches = []
+    for part in range(3):
+        engine.until(project_done[part])
+        fetches.append(pltpu.make_async_copy(full_rows(full, 32 * part), weights.at[part], fetch_sem.at[part]))
+        fetches[part].start()
+    for part in range(3):
+        fetches[part].wait()
+        result = dot_nn(rows, weights[part].reshape(D, D)).astype(BF16)
+        for at_row in range(2):
+            for at_pair in range(PAIRS):
+                staged[at_pair, at_row, part] = result[
+                    at_row * S_DEV:(at_row + 1) * S_DEV, at_pair * LANES:(at_pair + 1) * LANES
+                ]
+        engine.tick()
+    head_copies = []
+    for k in range(15):
+        to = (seq + k + 1) % 16
+        head_copies.append(
+            remote(staged.at[to // 2, to % 2], arrived.at[seq], head_send.at[k], head_recv.at[k], others[k])
+        )
+    own_heads = pltpu.make_async_copy(staged.at[pair, row], arrived.at[seq], own_sem.at[2])
+    own_heads.start()
+    engine.waiting = list(head_copies)
+    engine.tick(2)
     own_small.wait()
     for copy in quad_copies:
         copy.wait()
@@ -866,28 +898,6 @@
 
     lax.fori_loop(0, 16, spread_docs, 0)
 
-    rows = tokens[...].reshape(2 * S_DEV, D)
-    for part in range(3):
-        engine.until(project_done[part])
-        fetch = pltpu.make_async_copy(full_rows(full, 32 * part), weights.at[part], fetch_sem.at[part])
-        fetch.start()
-        fetch.wait()
-        result = dot_nn(rows, weights[part].reshape(D, D)).astype(BF16)
-        for at_row in range(2):
-            for at_pair in range(PAIRS):
-                staged[at_pair, at_row, part] = result[
-                    at_row * S_DEV:(at_row + 1) * S_DEV, at_pair * LANES:(at_pair + 1) * LANES
-                ]
-    head_copies = []
-    for k in range(15):
-        to = (seq + k + 1) % 16
-        head_copies.append(
-            remote(staged.at[to // 2, to % 2], arrived.at[seq], head_send.at[k], head_recv.at[k], others[k])
-        )
-    own_heads = pltpu.make_async_copy(staged.at[pair, row], arrived.at[seq], own_sem.at[2])
-    own_heads.start()
-    engine.waiting = list(head_copies)
-
     engine.until(memory_done)
     fetch_memory = pltpu.make_async_copy(memory_full, memory_held, own_sem.at[3])
     fetch_memory.start()
@@ -913,6 +923,8 @@
     for copy in head_copies:
         copy.wait()
 
+    leave((memory_pairs, memory_pairs_far), (docs_column, docs_column_far), (arrived, arrived_far))
+
     block = 2 * S_DEV
     columns = pl.ds(pl.multiple_of(pair * LANES, LANES), LANES)
     target = gathered.at[row, :, columns]
@@ -964,6 +976,8 @@
                 pltpu.make_async_copy(result_staged.at[to], target, own_sem.at[4]).start()
 
         engine.tick(STEP_TICKS)
+
+    leave((attended, attended_far), (inverse, inverse_far))
 
     for copy in small_copies:
         copy.wait()
@@ -1026,12 +1040,18 @@
         engine.tick(STEP_TICKS)
         lax.fori_loop(PAIRS // 2, PAIRS, one_pair, 0)
         engine.tick(STEP_TICKS)
+    leave(
+        (first_resid, first_resid_far), (cross_queries, cross_queries_far),
+        (crossed, crossed_far), (cross_inverse, cross_inverse_far),
+    )
     fetches[2].wait()
     resid = first_norm[...] + dot_nn(
         crossed[...].reshape(2 * S_DEV, D).astype(BF16), weights[2].reshape(D, D)
     )
     second_resid[...] = resid
     second_norm[...] = norm_rows(resid, gains[1])
+    for copy in leaving:
+        copy.wait()
     engine.finish()
 
 
@@ -1041,7 +1061,7 @@
 
 def first_call(tokens, memory, small, docs, *weights):
     length = 16 * S_DEV
-    chunks = 16 * 32 // PIECE_ROWS + 32 // PIECE_ROWS + 2
+    chunks = 16 * 32 // PIECE_ROWS + 32 // PIECE_ROWS + 4
     dma = pltpu.SemaphoreType.DMA
     shape = jax.ShapeDtypeStruct
     outs = pl.pallas_call(
@@ -1050,9 +1070,6 @@
             shape((4, 2, 2, 2, ALL_ROWS, D), BF16),
             shape((4, 2, 2, 2, M_DEV, D), BF16),
             shape((16, 2, M_DEV, 2 * D), BF16),
-            shape((8, SMALL_ROWS, LANES), BF16),
-            shape((16, 8, LANES), F32),
-            shape((8, length), F32),
             shape((length, LANES), F32),
             shape((16, 3, S_DEV, LANES), BF16),
             shape((length, LANES), F32),
@@ -1061,12 +1078,24 @@
             shape((2, S_DEV, D), BF16),
             shape((2, S_DEV, D), F32),
             shape((2, S_DEV, D), F32),
+            shape((8, SMALL_ROWS, LANES), BF16),
+            shape((16, 8, LANES), F32),
+            shape((8, length), F32),
             shape((2 * S_DEV, D), F32),
             shape((2 * S_DEV, D), F32),
         ),
         in_specs=[whole(), whole(pl.ANY), whole(), whole()] + [whole(pl.ANY)] * 8,
-        out_specs=(whole(pl.ANY), whole(pl.ANY)) + (whole(),) * 14,
+        out_specs=(whole(pl.ANY),) * 11 + (whole(),) * 5,
         scratch_shapes=[
+            pltpu.VMEM((16, 2, M_DEV, 2 * D), BF16),
+            pltpu.VMEM((length, LANES), F32),
+            pltpu.VMEM((16, 3, S_DEV, LANES), BF16),
+            pltpu.VMEM((length, LANES), F32),
+            pltpu.VMEM((length, LANES), F32),
+            pltpu.VMEM((2 * S_DEV, D), F32),
+            pltpu.VMEM((2, S_DEV, D), BF16),
+            pltpu.VMEM((2, S_DEV, D), F32),
+            pltpu.VMEM((2, S_DEV, D), F32),
             pltpu.VMEM((2, S_DEV, D), BF16),
             pltpu.VMEM((2 * S_DEV, D), F32),
             pltpu.VMEM((3, 4, 2, 2, 2, 32, D), BF16),
@@ -1080,7 +1109,7 @@
             dma((chunks, 3)), dma((chunks, 3)), dma((chunks, 2)), dma((chunks, 2)),
             dma((chunks, 3)), dma((chunks, 3)), dma((chunks, 1)), dma((chunks, 1)),
             dma((3,)), dma((5,)), dma((3,)), dma((3,)), dma((8,)), dma((8,)), dma((15,)), dma((15,)),
-            dma((15,)), dma((15,)), dma((16,)), dma((16,)),
+            dma((15,)), dma((15,)), dma((16,)), dma((16,)), dma((9,)),
         ],
         compiler_params=params(0),
         name="first",
@@ -1094,10 +1123,11 @@
     input_grad, memory_grad, down_grad, up_grad, prefix_sum,
     weights, memory_pairs, first_resid, arrived, attended, inverse, docs_column,
     pull, cross_grad, cross_query_grad, key_terms, value_terms, cross_prefix,
-    small_core, small_mine, small_x, small_pair, small_all,
-    memory_part, memory_core, memory_mine, memory_all, prefix_all, prefix_mine, prefix_quad,
+    small_core, small_mine, small_x, small_pair, small_y, small_line, small_all,
+    memory_part, memory_core, memory_mine, memory_y, memory_line, memory_all,
+    prefix_y, prefix_line, prefix_all, prefix_mine, prefix_quad,
     heads_out, grads, grad_low, delta, query_grads, key_grads, value_grads, staged, gathered,
-    fetch_sem, own_sem, near_send, near_recv, small_send, small_recv, memory_send, memory_recv,
+    fetch_sem, own_sem, near_send, near_recv, line_send, line_recv, small_send, small_recv, memory_send, memory_recv,
     prefix_send, prefix_recv, quad_send, quad_recv,
     in_send, in_recv, out_send, out_recv, query_send, query_recv,
 ):
@@ -1143,22 +1173,25 @@
     )
     small_own = pltpu.make_async_copy(small_grads.at[:, :, core], small_mine, own_sem.at[0])
     small_second = remote(small_mine.at[:, :, 1 - x], small_x, near_send.at[1], near_recv.at[1], place.along_x())
-    plane = z * 2 + y
-
-    def chips(source, target, sends, recvs):
-        copies = []
-        for k in range(1, 8):
-            to = (plane + k) % 8
-            copies.append(
-                remote(source.at[to // 2, to % 2], target.at[plane], sends.at[k], recvs.at[k], (to * 2 + core, x))
-            )
-        return copies
-
-    small_third = chips(small_pair, small_all, small_send, small_recv)
+
+    def along_y(k, source, target):
+        return remote(source.at[:, 1 - y], target, line_send.at[k], line_recv.at[k], place.along_y())
+
+    def along_z(source, target, sends, recvs):
+        return [
+            remote(source.at[(z + k) % 4], target.at[z], sends.at[k], recvs.at[k], place.along_z(k))
+            for k in range(1, 4)
+        ]
+
+    small_third = along_y(0, small_pair, small_y)
+    small_fourth = along_z(small_line, small_all, small_send, small_recv)
     memory_first = remote(
         memory_part.at[:, :, 1 - core], memory_core, near_send.at[2], near_recv.at[2], place.other_core()
     )
-    memory_second = chips(memory_mine, memory_all, memory_send, memory_recv)
+    memory_second = along_y(1, memory_mine, memory_y)
+    memory_third = along_z(memory_line, memory_all, memory_send, memory_recv)
+    prefix_first = along_y(2, cross_prefix, prefix_y)
+    prefix_second = along_z(prefix_line, prefix_all, prefix_send, prefix_recv)
     small_first.start()
     small_own.start()
 
@@ -1204,12 +1237,13 @@
             from_prefix = dot_left(slopes, prefix_key_stack)
             key_grad = merge_heads(dot_nn(slopes, heads)) * score_scale
             value_grad = merge_heads(dot_nn(e.astype(BF16), low))
+            held = cross_prefix.at[at_pair // 2, at_pair % 2]
             if at_row == 0:
-                cross_prefix[at_pair, 0] = key_grad
-                cross_prefix[at_pair, 1] = value_grad
+                held[0] = key_grad
+                held[1] = value_grad
             else:
-                cross_prefix[at_pair, 0] += key_grad
-                cross_prefix[at_pair, 1] += value_grad
+                held[0] += key_grad
+                held[1] += value_grad
             key_stack = stack_heads(memory_pairs[:, at_row, :, columns].reshape(memory_len, LANES))
             value_stack = stack_heads(memory_pairs[:, at_row, :, value_columns].reshape(memory_len, LANES))
             e = jnp.exp(dot_right(key_stack, heads) * score_scale).reshape(2, memory_len, S_DEV)
@@ -1229,20 +1263,7 @@
             small_first.wait_recv()
             small_mine[...] = small_mine[...] + small_core[...]
             small_second.start()
-    small_second.wait()
-    small_pair[...] = small_mine[:, :, x] + small_x[...]
-    for copy in small_third:
-        copy.start()
-    small_all[plane] = small_pair[z, y]
-
-    prefix_copies = []
-    for k in range(1, 8):
-        to = (pair + k) % 8
-        prefix_copies.append(
-            remote(cross_prefix.at[to], prefix_all.at[pair], prefix_send.at[k], prefix_recv.at[k], (to * 2 + core, x))
-        )
-        prefix_copies[-1].start()
-    prefix_all[pair] = cross_prefix[pair]
+    prefix_first.start()
 
     fetches[CROSS_Q_AT].wait()
     fetches["resid"].wait()
@@ -1276,14 +1297,12 @@
 
     lax.fori_loop(0, 4, memory_block, 0)
     memory_first.start()
-    for copy in small_third:
-        copy.wait()
-    total = small_all[0].astype(F32)
-    for k in range(1, 8):
-        total += small_all[k].astype(F32)
-    down_grad[...] = total[:, :ADAPTER]
-    up_grad[:, :ADAPTER] = total[:16, ADAPTER:]
-    up_grad[:, ADAPTER:] = total[16:, ADAPTER:]
+    small_second.wait()
+    small_pair[...] = small_mine[:, :, x] + small_x[...]
+    small_third.start()
+    memory_first.wait()
+    memory_mine[...] = memory_part[:, :, core] + memory_core[...]
+    memory_second.start()
     for name in ("arrived", "attended", "inverse", "docs"):
         fetches[name].wait()
     own_heads.wait()
@@ -1319,22 +1338,16 @@
         return carry
 
     lax.fori_loop(0, 8, prepare, 0)
-    memory_first.wait()
-    memory_mine[...] = memory_part[:, :, core] + memory_core[...]
-    for copy in memory_second:
+    prefix_first.wait()
+    prefix_line[...] = cross_prefix[:, y] + prefix_y[...]
+    for copy in prefix_second:
         copy.start()
-    memory_all[plane] = memory_mine[z, y]
-    for copy in prefix_copies:
-        copy.wait()
-    for part in range(2):
-        prefix_mine[2 + part] = sum(prefix_all[k, part] for k in range(8))
-    prefix_quad[core * 2 + x] = prefix_mine[...]
-    quad_copies = [
-        remote(prefix_mine, prefix_quad.at[core * 2 + x], quad_send.at[k], quad_recv.at[k], peer)
-        for k, peer in enumerate((place.other_core(), place.along_x(), place.diagonal()))
-    ]
-    for copy in quad_copies:
+    prefix_all[z] = prefix_line[z]
+    small_third.wait()
+    small_line[...] = small_pair[:, y] + small_y[...]
+    for copy in small_fourth:
         copy.start()
+    small_all[z] = small_line[z]
 
     away = (
         lax.broadcasted_iota(jnp.int32, (block, block), 0)
@@ -1385,7 +1398,13 @@
         send_block(1, 2, key_at, out_send, out_recv)
         return carry
 
-    lax.fori_loop(0, 8, one_block, 0)
+    lax.fori_loop(0, 2, one_block, 0)
+    memory_second.wait()
+    memory_line[...] = memory_mine[:, y] + memory_y[...]
+    for copy in memory_third:
+        copy.start()
+    memory_all[z] = memory_line[z]
+    lax.fori_loop(2, 8, one_block, 0)
 
     def last_block(step, carry):
         at = (step + pair) % 8
@@ -1396,10 +1415,29 @@
 
     lax.fori_loop(0, 8, last_block, 0)
     small_first.wait_send()
-    for copy in memory_second:
+    for copy in prefix_second:
+        copy.wait()
+    for part in range(2):
+        prefix_mine[2 + part] = sum(prefix_all[k, part] for k in range(4))
+    prefix_quad[core * 2 + x] = prefix_mine[...]
+    quad_copies = [
+        remote(prefix_mine, prefix_quad.at[core * 2 + x], quad_send.at[k], quad_recv.at[k], peer)
+        for k, peer in enumerate((place.other_core(), place.along_x(), place.diagonal()))
+    ]
+    for copy in quad_copies:
+        copy.start()
+    for copy in small_fourth:
+        copy.wait()
+    total = small_all[0].astype(F32)
+    for k in range(1, 4):
+        total += small_all[k].astype(F32)
+    down_grad[...] = total[:, :ADAPTER]
+    up_grad[:, :ADAPTER] = total[:16, ADAPTER:]
+    up_grad[:, ADAPTER:] = total[16:, ADAPTER:]
+    for copy in memory_third:
         copy.wait()
     total = memory_all[0].astype(F32)
-    for k in range(1, 8):
+    for k in range(1, 4):
         total += memory_all[k].astype(F32)
     memory_grad[...] = total
     for copy in quad_copies:
@@ -1457,17 +1495,23 @@
             pltpu.VMEM((2, S_DEV, D), BF16),
             pltpu.VMEM((16, 2, M_DEV, D), BF16),
             pltpu.VMEM((16, 2, M_DEV, D), BF16),
-            pltpu.VMEM((PAIRS, 2, 32, LANES), F32),
+            pltpu.VMEM((4, 2, 2, 32, LANES), F32),
             pltpu.VMEM((4, 2, 2, 32, D), BF16),
             pltpu.VMEM((4, 2, 2, 32, D), BF16),
             pltpu.VMEM((4, 2, 32, D), BF16),
             pltpu.VMEM((4, 2, 32, D), BF16),
-            pltpu.VMEM((8, 32, D), BF16),
+            pltpu.VMEM((4, 32, D), BF16),
+            pltpu.VMEM((4, 32, D), BF16),
+            pltpu.VMEM((4, 32, D), BF16),
             pltpu.VMEM((4, 2, 2, 2 * M_DEV, D), BF16),
             pltpu.VMEM((4, 2, 2 * M_DEV, D), BF16),
             pltpu.VMEM((4, 2, 2 * M_DEV, D), BF16),
-            pltpu.VMEM((8, 2 * M_DEV, D), BF16),
-            pltpu.VMEM((8, 2, 32, LANES), F32),
+            pltpu.VMEM((4, 2 * M_DEV, D), BF16),
+            pltpu.VMEM((4, 2 * M_DEV, D), BF16),
+            pltpu.VMEM((4, 2 * M_DEV, D), BF16),
+            pltpu.VMEM((4, 2, 32, LANES), F32),
+            pltpu.VMEM((4, 2, 32, LANES), F32),
+            pltpu.VMEM((4, 2, 32, LANES), F32),
             pltpu.VMEM((4, 32, LANES), F32),
             pltpu.VMEM((4, 4, 32, LANES), F32),
             pltpu.VMEM((PAIRS, 2, S_DEV, LANES), BF16),
@@ -1479,8 +1523,8 @@
             pltpu.VMEM((4 * S_DEV, LANES), F32),
             pltpu.VMEM((16, 3, S_DEV, LANES), BF16),
             pltpu.VMEM((PAIRS, 2, 3, S_DEV, LANES), BF16),
-            dma((14,)), dma((4,)), dma((3,)), dma((3,)), dma((8,)), dma((8,)), dma((8,)), dma((8,)),
-            dma((8,)), dma((8,)), dma((3,)), dma((3,)),
+            dma((14,)), dma((4,)), dma((3,)), dma((3,)), dma((3,)), dma((3,)), dma((4,)), dma((4,)), dma((4,)), dma((4,)),
+            dma((4,)), dma((4,)), dma((3,)), dma((3,)),
             dma((15,)), dma((15,)), dma((16,)), dma((16,)), dma((16,)), dma((16,)),
         ],
         compiler_params=params(1),
@@ -1610,8 +1654,8 @@
     memory_line = jnp.where(lane_group == seq % 4, jnp.tile(memory_docs, (1, 4)), 0)
     docs = jnp.concatenate([token_docs, memory_line, jnp.zeros((4, LANES), jnp.int32)]).astype(F32)
     (
-        full, memory_pairs, small_full, docs_all, docs_row, docs_column, arrived, pair_attended, pair_inverse,
-        first_resid, cross_queries, crossed, cross_inverse, second_resid, second_norm,
+        full, memory_pairs, docs_column, arrived, pair_attended, pair_inverse,
+        first_resid, cross_queries, crossed, cross_inverse, small_full, docs_all, docs_row, second_resid, second_norm,
     ) = first_call(
         inputs, memory.reshape(2, M_DEV, D), small, docs,
         self_project, self_output, cross_query, cross_memory, cross_output, inner_weight, outer_weight, mixed,

time: 395 us -> 362 us (0.916)
  Pallas kernels: 379 us -> 344 us
    pallas_call x1, Pallas kernels: 121 us -> 100 us  [second_call(): pl.pallas_call(second_kernel, out_shape=(shape((tokens, D), F32), shape((...]
    pallas_call x1, Pallas kernels: 235 us -> 222 us  [first_call(): pl.pallas_call(first_kernel, out_shape=(shape((4, 2, 2, 2, ALL_ROWS, D),...]
where the time goes in v4:
time: 362 us; the launch traced here: 359 us
  Pallas kernels  344 us (95%)
  local copies, waits for them, and re-layouts  9.37 us (3%)
  other arithmetic  4.7 us (1%)
    pallas_call x1, Pallas kernels, first_call(): pl.pallas_call(first_kernel, out_shape=(shape((4, 2, 2, 2, ALL_ROWS, D),...  222 us
    pallas_call x1, Pallas kernels, second_call(): pl.pallas_call(second_kernel, out_shape=(shape((tokens, D), F32), shape((...  100 us
    pallas_call x1, Pallas kernels, feed_forward_backward(): pl.pallas_call(feed_kernel, grid=(8,), out_shape=(jax.ShapeDtypeStruct((t...  22.8 us

profile of v4, /device:TPU:28, one launch (start us, length us, event | category | flops | bytes accessed | tf_op | source)
XLA Modules:
  0.0 359.3 jit_solution(14838335398096047611)
XLA Ops:
  0.6 0.8 copy.24
  1.4 0.9 copy.27
  2.3 0.1 reshape.97
  2.4 0.1 copy.25
  2.6 0.6 broadcast_select_fusion.small
  3.2 0.7 tile.20
  3.9 0.1 tile.21
  4.0 0.1 pad.15.clone
  4.0 1.3 add_convert_fusion.docs
  5.4 0.7 fusion.2
  6.1 1.4 maximum_maximum_fusion.mixed
  7.5 221.5 %first.1 = (bf16[4,2,2,2,544,1024]{5,4,3,2,1,0:T(8,128)(2,1)}, bf16[4,2,2,2,32,1024]{5,4,3,2,1,0:T(8,128)(2,1)}, bf16[16,2,32,2048]{3,2,1,0:T(8,128)(2,1)}, f32[...) custom-call(bf16[2,128,1024]{2,1,0:T(8,128)(2,1)} %tokens.1, ...), custom_call_target="tpu_custom_call" | custom-call | tf_op jit(solution)/shard_map/first/pallas_call | solution.py:1067
  229.1 1.3 bitcast_convert_fusion.gain
  230.4 22.8 %feed.1 = (bf16[256,1024]{1,0:T(8,128)(2,1)}, f32[256,1024]{1,0:T(8,128)}, bf16[32,32,1024]{2,1,0:T(8,128)(2,1)}) custom-call(f32[256,1024]{1,0:T(8,128)} %get-tuple-element.29.normed, bf16[256,1024]{1,0:T(8,128)(2,1)} %bitcast.19, f32[1,1024]{1,0:T(1,128)} %bitcast_convert_fusion.gain, bf16[32,544,1024]{2,1,0:T(8,128)(2,1)} %bitcast.13, ...), custom_call_target="tpu_custom_call" | custom-call | tf_op jit(solution)/shard_map/feed/pallas_call | solution.py:1613
  253.2 100.1 %second.1 = (f32[256,1024]{1,0:T(8,128)}, f32[64,1024]{1,0:T(8,128)}, f32[32,512]{1,0:T(8,128)}, f32[16,1024]{1,0:T(8,128)}, f32[4,32,128]{2,1,0:T(8,128)}) custom-call(f32[256,1024]{1,0:T(8,128)} %get-tuple-element.33.second_grad, f32[256,1024]{1,0:T(8,128)} %get-tuple-element.34.second_resid, bf16[8,144,128]{2,1,0:T(8,128)(2,1)} %get-tuple-element.30.small_full, ...), custom_call_target="tpu_custom_call" | custom-call | tf_op jit(solution)/shard_map/second/pallas_call | solution.py:1474
  353.3 0.0 copy-start
  353.3 0.0 copy-start.2
  353.3 0.0 copy-start.1
  353.3 1.0 constant_dynamic-slice_fusion
  354.3 0.7 copy.26
  355.0 2.3 copy.32
  357.3 0.0 copy-done
  357.3 0.7 copy.33
  358.0 0.0 copy-done.2
  358.0 0.6 copy.34
  358.6 0.0 copy-done.1
  358.6 0.6 copy.35
  (7 shorter events, 0.1 us)
Async XLA Ops:
  353.3 4.0 %copy-start = (f32[64,1024]{1,0:T(8,128)S(1)}, f32[64,1024]{1,0:T(8,128)}, u32[]{:S(2)}) copy-start(f32[64,1024]{1,0:T(8,128)} %get-tuple-element.48) | copy-start | bytes 786436
  353.3 4.7 %copy-start.2 = (f32[32,512]{1,0:T(8,128)S(1)}, f32[32,512]{1,0:T(8,128)}, u32[]{:S(2)}) copy-start(f32[32,512]{1,0:T(8,128)} %get-tuple-element.76) | copy-start | bytes 196612
  353.3 5.3 %copy-start.1 = (f32[16,1024]{1,0:T(8,128)S(1)}, f32[16,1024]{1,0:T(8,128)}, u32[]{:S(2)}) copy-start(f32[16,1024]{1,0:T(8,128)} %get-tuple-element.77) | copy-start | bytes 196612

commit v5 on v4

--- a/solution.py
+++ b/solution.py
@@ -600,7 +600,7 @@
 ALL_ROWS = 544
 SMALL_ROWS = 144
 PIECE_ROWS = 16
-GAP = 3
+GAP = 6
 LEAD = 4
 SENDS = 2
 Z_LAST = ()

time: 362 us -> 355 us (0.981)
  Pallas kernels: 344 us -> 338 us
    pallas_call x1, Pallas kernels: 222 us -> 214 us  [first_call(): pl.pallas_call(first_kernel, out_shape=(shape((4, 2, 2, 2, ALL_ROWS, D),...]
where the time goes in v5:
time: 355 us; the launch traced here: 353 us
  Pallas kernels  338 us (95%)
  local copies, waits for them, and re-layouts  9.37 us (3%)
  other arithmetic  4.7 us (1%)
    pallas_call x1, Pallas kernels, first_call(): pl.pallas_call(first_kernel, out_shape=(shape((4, 2, 2, 2, ALL_ROWS, D),...  214 us
    pallas_call x1, Pallas kernels, second_call(): pl.pallas_call(second_kernel, out_shape=(shape((tokens, D), F32), shape((...  102 us
    pallas_call x1, Pallas kernels, feed_forward_backward(): pl.pallas_call(feed_kernel, grid=(8,), out_shape=(jax.ShapeDtypeStruct((t...  22.8 us

profile of v5, /device:TPU:28, one launch (start us, length us, event | category | flops | bytes accessed | tf_op | source)
XLA Modules:
  0.0 352.9 jit_solution(6193190834305450448)
XLA Ops:
  0.6 0.8 copy.24
  1.4 0.9 copy.27
  2.3 0.1 reshape.97
  2.4 0.1 copy.25
  2.6 0.6 broadcast_select_fusion.small
  3.2 0.7 tile.20
  3.9 0.1 tile.21
  4.0 0.1 pad.15.clone
  4.0 1.3 add_convert_fusion.docs
  5.4 0.7 fusion.2
  6.1 1.4 maximum_maximum_fusion.mixed
  7.5 213.6 %first.1 = (bf16[4,2,2,2,544,1024]{5,4,3,2,1,0:T(8,128)(2,1)}, bf16[4,2,2,2,32,1024]{5,4,3,2,1,0:T(8,128)(2,1)}, bf16[16,2,32,2048]{3,2,1,0:T(8,128)(2,1)}, f32[...) custom-call(bf16[2,128,1024]{2,1,0:T(8,128)(2,1)} %tokens.1, ...), custom_call_target="tpu_custom_call" | custom-call | tf_op jit(solution)/shard_map/first/pallas_call | solution.py:1067
  221.1 1.3 bitcast_convert_fusion.gain
  222.4 22.8 %feed.1 = (bf16[256,1024]{1,0:T(8,128)(2,1)}, f32[256,1024]{1,0:T(8,128)}, bf16[32,32,1024]{2,1,0:T(8,128)(2,1)}) custom-call(f32[256,1024]{1,0:T(8,128)} %get-tuple-element.29.normed, bf16[256,1024]{1,0:T(8,128)(2,1)} %bitcast.19, f32[1,1024]{1,0:T(1,128)} %bitcast_convert_fusion.gain, bf16[32,544,1024]{2,1,0:T(8,128)(2,1)} %bitcast.13, ...), custom_call_target="tpu_custom_call" | custom-call | tf_op jit(solution)/shard_map/feed/pallas_call | solution.py:1613
  245.2 101.8 %second.1 = (f32[256,1024]{1,0:T(8,128)}, f32[64,1024]{1,0:T(8,128)}, f32[32,512]{1,0:T(8,128)}, f32[16,1024]{1,0:T(8,128)}, f32[4,32,128]{2,1,0:T(8,128)}) custom-call(f32[256,1024]{1,0:T(8,128)} %get-tuple-element.33.second_grad, f32[256,1024]{1,0:T(8,128)} %get-tuple-element.34.second_resid, bf16[8,144,128]{2,1,0:T(8,128)(2,1)} %get-tuple-element.30.small_full, ...), custom_call_target="tpu_custom_call" | custom-call | tf_op jit(solution)/shard_map/second/pallas_call | solution.py:1474
  347.0 0.0 copy-start
  347.0 0.0 copy-start.2
  347.0 0.0 copy-start.1
  347.0 1.0 constant_dynamic-slice_fusion
  348.0 0.7 copy.26
  348.7 2.3 copy.32
  351.0 0.0 copy-done
  351.0 0.7 copy.33
  351.7 0.0 copy-done.2
  351.7 0.6 copy.34
  352.3 0.0 copy-done.1
  352.3 0.6 copy.35
  (7 shorter events, 0.1 us)
Async XLA Ops:
  347.0 4.0 %copy-start = (f32[64,1024]{1,0:T(8,128)S(1)}, f32[64,1024]{1,0:T(8,128)}, u32[]{:S(2)}) copy-start(f32[64,1024]{1,0:T(8,128)} %get-tuple-element.48) | copy-start | bytes 786436
  347.0 4.7 %copy-start.2 = (f32[32,512]{1,0:T(8,128)S(1)}, f32[32,512]{1,0:T(8,128)}, u32[]{:S(2)}) copy-start(f32[32,512]{1,0:T(8,128)} %get-tuple-element.76) | copy-start | bytes 196612
  347.0 5.3 %copy-start.1 = (f32[16,1024]{1,0:T(8,128)S(1)}, f32[16,1024]{1,0:T(8,128)}, u32[]{:S(2)}) copy-start(f32[16,1024]{1,0:T(8,128)} %get-tuple-element.77) | copy-start | bytes 196612

commit v6 on v5

--- a/solution.py
+++ b/solution.py
@@ -602,10 +602,10 @@
 PIECE_ROWS = 16
 GAP = 6
 LEAD = 4
-SENDS = 2
+SENDS = 3
 Z_LAST = ()
 WAIT_TICKS = 4
-STEP_TICKS = 2
+STEP_TICKS = 1
 
 
 def whole(space=pltpu.VMEM):
@@ -975,7 +975,7 @@
             def _():
                 pltpu.make_async_copy(result_staged.at[to], target, own_sem.at[4]).start()
 
-        engine.tick(STEP_TICKS)
+        engine.tick(step % 2)
 
     leave((attended, attended_far), (inverse, inverse_far))
 

time: 355 us -> 342 us (0.963)
  Pallas kernels: 338 us -> 325 us
    pallas_call x1, Pallas kernels: 214 us -> 203 us  [first_call(): pl.pallas_call(first_kernel, out_shape=(shape((4, 2, 2, 2, ALL_ROWS, D),...]
where the time goes in v6:
time: 342 us; the launch traced here: 340 us
  Pallas kernels  325 us (95%)
  local copies, waits for them, and re-layouts  9.37 us (3%)
  other arithmetic  4.7 us (1%)
    pallas_call x1, Pallas kernels, first_call(): pl.pallas_call(first_kernel, out_shape=(shape((4, 2, 2, 2, ALL_ROWS, D),...  203 us
    pallas_call x1, Pallas kernels, second_call(): pl.pallas_call(second_kernel, out_shape=(shape((tokens, D), F32), shape((...  99.7 us
    pallas_call x1, Pallas kernels, feed_forward_backward(): pl.pallas_call(feed_kernel, grid=(8,), out_shape=(jax.ShapeDtypeStruct((t...  22.8 us

profile of v6, /device:TPU:28, one launch (start us, length us, event | category | flops | bytes accessed | tf_op | source)
XLA Modules:
  0.0 339.9 jit_solution(5657743069297659826)
XLA Ops:
  0.6 0.8 copy.24
  1.4 0.9 copy.27
  2.3 0.1 reshape.97
  2.4 0.1 copy.25
  2.6 0.6 broadcast_select_fusion.small
  3.2 0.7 tile.20
  3.9 0.1 tile.21
  4.0 0.1 pad.15.clone
  4.0 1.3 add_convert_fusion.docs
  5.4 0.7 fusion.2
  6.1 1.4 maximum_maximum_fusion.mixed
  7.5 202.7 %first.1 = (bf16[4,2,2,2,544,1024]{5,4,3,2,1,0:T(8,128)(2,1)}, bf16[4,2,2,2,32,1024]{5,4,3,2,1,0:T(8,128)(2,1)}, bf16[16,2,32,2048]{3,2,1,0:T(8,128)(2,1)}, f32[...) custom-call(bf16[2,128,1024]{2,1,0:T(8,128)(2,1)} %tokens.1, ...), custom_call_target="tpu_custom_call" | custom-call | tf_op jit(solution)/shard_map/first/pallas_call | solution.py:1067
  210.2 1.3 bitcast_convert_fusion.gain
  211.5 22.8 %feed.1 = (bf16[256,1024]{1,0:T(8,128)(2,1)}, f32[256,1024]{1,0:T(8,128)}, bf16[32,32,1024]{2,1,0:T(8,128)(2,1)}) custom-call(f32[256,1024]{1,0:T(8,128)} %get-tuple-element.29.normed, bf16[256,1024]{1,0:T(8,128)(2,1)} %bitcast.19, f32[1,1024]{1,0:T(1,128)} %bitcast_convert_fusion.gain, bf16[32,544,1024]{2,1,0:T(8,128)(2,1)} %bitcast.13, ...), custom_call_target="tpu_custom_call" | custom-call | tf_op jit(solution)/shard_map/feed/pallas_call | solution.py:1613
  234.3 99.7 %second.1 = (f32[256,1024]{1,0:T(8,128)}, f32[64,1024]{1,0:T(8,128)}, f32[32,512]{1,0:T(8,128)}, f32[16,1024]{1,0:T(8,128)}, f32[4,32,128]{2,1,0:T(8,128)}) custom-call(f32[256,1024]{1,0:T(8,128)} %get-tuple-element.33.second_grad, f32[256,1024]{1,0:T(8,128)} %get-tuple-element.34.second_resid, bf16[8,144,128]{2,1,0:T(8,128)(2,1)} %get-tuple-element.30.small_full, ...), custom_call_target="tpu_custom_call" | custom-call | tf_op jit(solution)/shard_map/second/pallas_call | solution.py:1474
  334.0 0.0 copy-start
  334.0 0.0 copy-start.2
  334.0 0.0 copy-start.1
  334.0 1.0 constant_dynamic-slice_fusion
  335.0 0.7 copy.26
  335.7 2.3 copy.32
  338.0 0.0 copy-done
  338.0 0.7 copy.33
  338.7 0.0 copy-done.2
  338.7 0.6 copy.34
  339.3 0.0 copy-done.1
  339.3 0.6 copy.35
  (7 shorter events, 0.1 us)
Async XLA Ops:
  334.0 4.0 %copy-start = (f32[64,1024]{1,0:T(8,128)S(1)}, f32[64,1024]{1,0:T(8,128)}, u32[]{:S(2)}) copy-start(f32[64,1024]{1,0:T(8,128)} %get-tuple-element.48) | copy-start | bytes 786436
  334.0 4.7 %copy-start.2 = (f32[32,512]{1,0:T(8,128)S(1)}, f32[32,512]{1,0:T(8,128)}, u32[]{:S(2)}) copy-start(f32[32,512]{1,0:T(8,128)} %get-tuple-element.76) | copy-start | bytes 196612
  334.0 5.3 %copy-start.1 = (f32[16,1024]{1,0:T(8,128)S(1)}, f32[16,1024]{1,0:T(8,128)}, u32[]{:S(2)}) copy-start(f32[16,1024]{1,0:T(8,128)} %get-tuple-element.77) | copy-start | bytes 196612

commit v7 on v6

--- a/solution.py
+++ b/solution.py
@@ -975,7 +975,7 @@
             def _():
                 pltpu.make_async_copy(result_staged.at[to], target, own_sem.at[4]).start()
 
-        engine.tick(step % 2)
+        engine.tick(step % 4 // 3)
 
     leave((attended, attended_far), (inverse, inverse_far))
 

time: 342 us -> 347 us (1.015)
  Pallas kernels: 325 us -> 330 us
    pallas_call x1, Pallas kernels: 203 us -> 207 us  [first_call(): pl.pallas_call(first_kernel, out_shape=(shape((4, 2, 2, 2, ALL_ROWS, D),...]
where the time goes in v7:
time: 347 us; the launch traced here: 344 us
  Pallas kernels  330 us (95%)
  local copies, waits for them, and re-layouts  9.37 us (3%)
  other arithmetic  4.7 us (1%)
    pallas_call x1, Pallas kernels, first_call(): pl.pallas_call(first_kernel, out_shape=(shape((4, 2, 2, 2, ALL_ROWS, D),...  207 us
    pallas_call x1, Pallas kernels, second_call(): pl.pallas_call(second_kernel, out_shape=(shape((tokens, D), F32), shape((...  99.9 us
    pallas_call x1, Pallas kernels, feed_forward_backward(): pl.pallas_call(feed_kernel, grid=(8,), out_shape=(jax.ShapeDtypeStruct((t...  22.8 us

profile of v7, /device:TPU:28, one launch (start us, length us, event | category | flops | bytes accessed | tf_op | source)
XLA Modules:
  0.0 344.4 jit_solution(4962967739693136381)
XLA Ops:
  0.6 0.8 copy.24
  1.4 0.9 copy.27
  2.3 0.1 reshape.97
  2.4 0.1 copy.25
  2.6 0.6 broadcast_select_fusion.small
  3.2 0.7 tile.20
  3.9 0.1 tile.21
  4.0 0.1 pad.15.clone
  4.0 1.3 add_convert_fusion.docs
  5.4 0.7 fusion.2
  6.1 1.4 maximum_maximum_fusion.mixed
  7.5 206.9 %first.1 = (bf16[4,2,2,2,544,1024]{5,4,3,2,1,0:T(8,128)(2,1)}, bf16[4,2,2,2,32,1024]{5,4,3,2,1,0:T(8,128)(2,1)}, bf16[16,2,32,2048]{3,2,1,0:T(8,128)(2,1)}, f32[...) custom-call(bf16[2,128,1024]{2,1,0:T(8,128)(2,1)} %tokens.1, ...), custom_call_target="tpu_custom_call" | custom-call | tf_op jit(solution)/shard_map/first/pallas_call | solution.py:1067
  214.4 1.3 bitcast_convert_fusion.gain
  215.7 22.8 %feed.1 = (bf16[256,1024]{1,0:T(8,128)(2,1)}, f32[256,1024]{1,0:T(8,128)}, bf16[32,32,1024]{2,1,0:T(8,128)(2,1)}) custom-call(f32[256,1024]{1,0:T(8,128)} %get-tuple-element.29.normed, bf16[256,1024]{1,0:T(8,128)(2,1)} %bitcast.19, f32[1,1024]{1,0:T(1,128)} %bitcast_convert_fusion.gain, bf16[32,544,1024]{2,1,0:T(8,128)(2,1)} %bitcast.13, ...), custom_call_target="tpu_custom_call" | custom-call | tf_op jit(solution)/shard_map/feed/pallas_call | solution.py:1613
  238.5 99.9 %second.1 = (f32[256,1024]{1,0:T(8,128)}, f32[64,1024]{1,0:T(8,128)}, f32[32,512]{1,0:T(8,128)}, f32[16,1024]{1,0:T(8,128)}, f32[4,32,128]{2,1,0:T(8,128)}) custom-call(f32[256,1024]{1,0:T(8,128)} %get-tuple-element.33.second_grad, f32[256,1024]{1,0:T(8,128)} %get-tuple-element.34.second_resid, bf16[8,144,128]{2,1,0:T(8,128)(2,1)} %get-tuple-element.30.small_full, ...), custom_call_target="tpu_custom_call" | custom-call | tf_op jit(solution)/shard_map/second/pallas_call | solution.py:1474
  338.4 0.0 copy-start
  338.4 0.0 copy-start.2
  338.4 0.0 copy-start.1
  338.5 1.0 constant_dynamic-slice_fusion
  339.4 0.7 copy.26
  340.1 2.3 copy.32
  342.4 0.0 copy-done
  342.4 0.7 copy.33
  343.1 0.0 copy-done.2
  343.1 0.6 copy.34
  343.7 0.0 copy-done.1
  343.7 0.6 copy.35
  (7 shorter events, 0.1 us)
Async XLA Ops:
  338.4 4.0 %copy-start = (f32[64,1024]{1,0:T(8,128)S(1)}, f32[64,1024]{1,0:T(8,128)}, u32[]{:S(2)}) copy-start(f32[64,1024]{1,0:T(8,128)} %get-tuple-element.48) | copy-start | bytes 786436
  338.4 4.7 %copy-start.2 = (f32[32,512]{1,0:T(8,128)S(1)}, f32[32,512]{1,0:T(8,128)}, u32[]{:S(2)}) copy-start(f32[32,512]{1,0:T(8,128)} %get-tuple-element.76) | copy-start | bytes 196612
  338.4 5.3 %copy-start.1 = (f32[16,1024]{1,0:T(8,128)S(1)}, f32[16,1024]{1,0:T(8,128)}, u32[]{:S(2)}) copy-start(f32[16,1024]{1,0:T(8,128)} %get-tuple-element.77) | copy-start | bytes 196612
